TPU v7x, 32 devices: a whole 2x2x4 slice. The times are simulated.
32 devices in a mesh: req: 8 (over y, x, core), tp: 4 (over z).
Axes of the slice: x: 2, y: 2, z: 4, core: 2. Of those that a mesh axis runs over, the one named last changes fastest.
Arguments:
- hidden_in: bfloat16 [2048, 2304], P('req'), may hold values from -6 to 6
- cache_lengths: int32 [8], P('req'), may hold values from 128 to 2048, as said below
- key_cache: bfloat16 [8, 2048, 2304], P('req', None, 'tp'), may hold values from -104 to 104
- value_cache: bfloat16 [8, 2048, 2304], P('req', None, 'tp'), may hold values from -6 to 6
- attn_norm: float32 [2304], replicated, may hold values from 0.5 to 1.5
- w_qkv: bfloat16 [3, 2304, 2304], P(None, None, 'tp'), may hold values from -0.125 to 0.125
- w_out: bfloat16 [2304, 2304], P('tp'), may hold values from -0.125 to 0.125
- ffn_norm: float32 [2304], replicated, may hold values from 0.5 to 1.5
- router: bfloat16 [2304, 8], replicated, may hold values from -0.125 to 0.125
- routes: int32 [2048, 2], P('req'), may hold values from 0 to 7, all different within a row; in each aligned block of 256 rows (0 to 255, 256 to 511, ...) at most 96 rows name the same one
- expert_gate: bfloat16 [8, 2304, 5760], P('req', None, 'tp'), may hold values from -0.125 to 0.125
- expert_up: bfloat16 [8, 2304, 5760], P('req', None, 'tp'), may hold values from -0.125 to 0.125
- expert_down: bfloat16 [8, 5760, 2304], P('req', 'tp'), may hold values from -0.078125 to 0.078125
Outputs:
- block_out: bfloat16 [2048, 2304], P(('req', 'tp'))
Inputs may be any that keep to these rules, and one draw needn't show every extreme that they name: `cache_lengths`: some request has exactly 2048 cached tokens. `routes`: within the 256 rows of one request no expert is named by more than 96 rows, and in every draw, within some request, an expert is named by exactly 96 rows; a row's two experts differ.
All inputs are finite; a program needn't handle non-finite values.
Results may differ from a plain program's by a relative error of at most 0.013.
Values may be sent and summed in bfloat16 or wider, within the bound.
No kernel may reach another device: no remote copies, remote signals or barrier semaphores. Data moves between devices by JAX's collectives and lax.ppermute only.
A program may use at most 192 MiB of HBM per device.

v0:
```python
import math

import jax
import jax.numpy as jnp
from jax import lax
from jax.sharding import PartitionSpec as P

HEAD = 64
TOP = 2
CAP = 96


EPSILON = 1e-05


def normalize(inputs, scale_gain):
    mean_square = jnp.mean(inputs * inputs, axis=-1, keepdims=True)
    return inputs * lax.rsqrt(mean_square + EPSILON) * scale_gain


def rotate(inputs, positions):
    half_dim = inputs.shape[-1] // 2
    frequency = jnp.exp(
        jnp.arange(half_dim, dtype=jnp.float32) * (-2.0 * math.log(10000.0) / inputs.shape[-1])
    )
    angles = positions.astype(jnp.float32)[:, None] * frequency[None, :]
    cosine = jnp.cos(angles)[:, None, :]
    sine_part = jnp.sin(angles)[:, None, :]
    lower_half = inputs[..., :half_dim]
    upper_half = inputs[..., half_dim:]
    return jnp.concatenate(
        [
            lower_half * cosine - upper_half * sine_part,
            lower_half * sine_part + upper_half * cosine,
        ],
        axis=-1,
    )


def attention(queries, all_keys, all_values, length):
    query_count = queries.shape[0]
    cache_len = all_keys.shape[0] - query_count
    scores = jnp.einsum(
        "qhd,khd->hqk", queries, all_keys, preferred_element_type=jnp.float32
    ) * queries.shape[-1] ** (-0.5)
    slot_ids = jnp.arange(cache_len + query_count, dtype=jnp.int32)
    query_ids = jnp.arange(query_count, dtype=jnp.int32)
    is_live = jnp.where(
        slot_ids[None, :] < cache_len,
        slot_ids[None, :] < length,
        slot_ids[None, :] - cache_len <= query_ids[:, None],
    )
    scores = jnp.where(is_live[None], scores, -jnp.inf)
    row_max = jnp.max(scores, axis=-1, keepdims=True)
    weights = jnp.exp(scores - row_max)
    totals = jnp.sum(weights, axis=-1)
    mixture = jnp.einsum(
        "hqk,khd->qhd", weights.astype(jnp.bfloat16), all_values, preferred_element_type=jnp.float32
    )
    return (mixture / jnp.transpose(totals)[:, :, None]).astype(jnp.bfloat16)


def per_device(
    hidden_in,
    cache_lengths,
    key_cache,
    value_cache,
    attn_norm,
    w_qkv,
    w_out,
    ffn_norm,
    router,
    routes,
    expert_gate,
    expert_up,
    expert_down,
):
    token_count = hidden_in.shape[0]
    model_width = hidden_in.shape[1]
    local_lanes = w_qkv.shape[2]
    local_heads = local_lanes // HEAD
    cache_len = key_cache.shape[1]
    token_share = token_count // lax.axis_size("tp")
    offset = lax.axis_index("tp") * token_share
    expert_count = router.shape[1]
    copies = lax.axis_size("req") // expert_count
    residual = hidden_in.astype(jnp.float32)
    normed = normalize(residual, attn_norm).astype(jnp.bfloat16)
    projected = jnp.einsum("td,cdh->cth", normed, w_qkv, preferred_element_type=jnp.float32)
    length = cache_lengths[0]
    positions = length + jnp.arange(token_count, dtype=jnp.int32)
    queries = rotate(projected[0].reshape(token_count, local_heads, HEAD), positions).astype(
        jnp.bfloat16
    )
    fresh_keys = rotate(projected[1].reshape(token_count, local_heads, HEAD), positions).astype(
        jnp.bfloat16
    )
    fresh_values = projected[2].reshape(token_count, local_heads, HEAD).astype(jnp.bfloat16)
    all_keys = jnp.concatenate(
        [key_cache[0].reshape(cache_len, local_heads, HEAD), fresh_keys], axis=0
    )
    all_values = jnp.concatenate(
        [value_cache[0].reshape(cache_len, local_heads, HEAD), fresh_values], axis=0
    )
    attended = attention(queries, all_keys, all_values, length).reshape(token_count, local_lanes)
    summed_attn = lax.psum(
        jnp.dot(attended, w_out, preferred_element_type=jnp.float32).astype(jnp.bfloat16), "tp"
    ).astype(jnp.float32)
    updated = residual + summed_attn
    moe_input = normalize(updated, ffn_norm).astype(jnp.bfloat16)
    own_residual = lax.dynamic_slice_in_dim(updated, offset, token_share, 0)
    logits = jnp.dot(moe_input, router, preferred_element_type=jnp.float32)
    chosen = jnp.take_along_axis(logits, routes, axis=1)
    first_gate = 1.0 / (1.0 + jnp.exp(chosen[:, 1] - chosen[:, 0]))
    second_gate = 1.0 / (1.0 + jnp.exp(chosen[:, 0] - chosen[:, 1]))
    flat_routes = routes.reshape(-1)
    onehot = (flat_routes[:, None] == jnp.arange(expert_count, dtype=jnp.int32)[None, :]).astype(
        jnp.int32
    )
    slot_rank = jnp.sum((jnp.cumsum(onehot, axis=0) - onehot) * onehot, axis=1)
    slot_ids = flat_routes * CAP + slot_rank
    paired = slot_ids.reshape(token_count, TOP)
    placing = jnp.any(
        paired[None, :, :] == jnp.arange(expert_count * CAP, dtype=jnp.int32)[:, None, None], axis=2
    ).astype(jnp.bfloat16)
    packed = (
        jnp.dot(placing, moe_input, preferred_element_type=jnp.float32)
        .astype(jnp.bfloat16)
        .reshape(expert_count, CAP, model_width)
    )
    outgoing = jnp.broadcast_to(packed[:, None], (expert_count, copies, CAP, model_width)).reshape(
        expert_count * copies, CAP, model_width
    )
    received = lax.all_to_all(outgoing, "req", split_axis=0, concat_axis=0, tiled=True)
    token_rows = received.reshape(-1, model_width)
    gate_proj = jnp.dot(token_rows, expert_gate[0], preferred_element_type=jnp.float32)
    up_proj = jnp.dot(token_rows, expert_up[0], preferred_element_type=jnp.float32)
    activation = (jax.nn.silu(gate_proj) * up_proj).astype(jnp.bfloat16)
    partial_value = jnp.dot(activation, expert_down[0], preferred_element_type=jnp.float32).astype(
        jnp.bfloat16
    )
    returned = lax.all_to_all(
        partial_value.reshape(received.shape), "req", split_axis=0, concat_axis=0, tiled=True
    )
    back_rows = returned.reshape(-1, model_width)
    back_index = (
        flat_routes[None, :] * copies + jnp.arange(copies, dtype=jnp.int32)[:, None]
    ) * CAP + slot_rank[None, :]
    fetched = jnp.take(back_rows, back_index, axis=0)
    summed = jnp.sum(fetched.astype(jnp.float32), axis=0).reshape(token_count, TOP, model_width)
    local_sum = first_gate[:, None] * summed[:, 0] + second_gate[:, None] * summed[:, 1]
    moe_own = lax.psum_scatter(
        local_sum.astype(jnp.bfloat16), "tp", scatter_dimension=0, tiled=True
    ).astype(jnp.float32)
    return (own_residual + moe_own).astype(jnp.bfloat16)


def solution(mesh):
    return jax.shard_map(
        per_device,
        mesh=mesh,
        in_specs=(
            P("req", None),
            P("req"),
            P("req", None, "tp"),
            P("req", None, "tp"),
            P(),
            P(None, None, "tp"),
            P("tp", None),
            P(),
            P(),
            P("req", None),
            P("req", None, "tp"),
            P("req", None, "tp"),
            P("req", "tp", None),
        ),
        out_specs=P(("req", "tp"), None),
        check_vma=False,
    )
```

profile of v0, /device:TPU:0, one launch (start us, length us, event | category | flops | bytes accessed | tf_op | source)
XLA Modules:
  0.0 286.3 jit_solution(9189410265880102057)
XLA Ops:
  6.6 1.7 fusion.28
  8.3 6.1 %convolution_bitcast_fusion = f32[3,256,576]{1,2,0:T(8,128)S(1)} fusion(bf16[3,2304,576]{1,2,0:T(8,128)(2,1)} %param.18, bf16[256,2304]{1,0:T(8,128)(2,1)} %param.13, f32[2304]{0:T(1024)} %param.17, f32[256]{0:T(256)S(1)} %add_rsqrt_fusion.1), kind=kOutput, calls=%fused_computation.49 | convolution fusion | flops 2040791040 | bytes 10921984 | tf_op jit(solution)/shard_map/td,cdh->cth/dot_general | solution.py:89
  14.5 0.1 fusion.72
  15.4 0.2 multiply_cosine_fusion
  15.6 0.4 fusion.36
  16.0 0.2 subtract_convert_fusion.1
  16.2 9.9 %fusion = (f32[9,256]{1,0:T(8,128)S(1)}, f32[9,256,2304]{2,1,0:T(8,128)}) fusion(pred[256,2304]{1,0:T(8,128)(4,1)S(1)} %fusion.36, bf16[256,9,32]{0,2,1:T(8,128)(2,1)S(1)} %get-tuple-element.15, bf16[256,9,32]{0,2,1:T(8,128)(2,1)S(1)} %get-tuple-element.16, bf16[2048,9,64]{0,2,1:T(8,128)(2,1)S(1)} %bitcast.93, ...), kind=kOutput, calls=%fused_computation.4 | convolution fusion | flops 703952640 | bytes 24781824 | tf_op jit(solution)/shard_map/qhd,khd->hqk/dot_general | solution.py:43
  26.0 10.6 %fusion.1 = f32[9,256]{1,0:T(8,128)S(1)} fusion(f32[9,256,2304]{2,1,0:T(8,128)} %get-tuple-element.22, f32[9,256]{1,0:T(8,128)S(1)} %get-tuple-element.21, pred[256,2304]{1,0:T(8,128)(4,1)S(1)} %fusion.36), kind=kLoop, calls=%fused_computation.5 | loop fusion | flops 21231360 | bytes 21841920 | tf_op jit(solution)/shard_map/reduce_sum | solution.py:56
  36.7 10.0 %fusion.53 = bf16[256,9,64]{0,2,1:T(8,128)(2,1)S(1)} fusion(f32[9,256,2304]{2,1,0:T(8,128)} %get-tuple-element.22, f32[9,256]{1,0:T(8,128)S(1)} %get-tuple-element.21, pred[256,2304]{1,0:T(8,128)(4,1)S(1)} %fusion.36, bf16[256,9,64]{0,2,1:T(8,128)(2,1)S(1)} %bitcast.85, bf16[2048,9,64]{0,2,1:T(8,128)(2,1)S(1)} %bitcast.94, f32[256,9]{0,1:T(8,128)S(1)} %bitcast.87), kind=kOutput, calls=%fused_computation.55 | convolution fusion | flops 706314240 | bytes 24791040 | tf_op jit(solution)/shard_map/hqk,khd->qhd/dot_general | solution.py:57
  46.7 2.1 convolution_convert_fusion.1
  48.9 0.0 all-reduce.2.cloned.1.call-update
  48.9 0.1 copy.48
  49.0 0.1 eq.39
  49.2 0.1 broadcast_in_dim_reshape.2
  49.3 1.1 reduce-window.6
  50.5 0.2 slice_reduce_fusion
  50.7 0.1 fusion.62
  50.8 0.1 reduce_sum.48
  51.0 0.1 copy.50
  51.1 0.5 compare_and_fusion
  51.6 0.3 fusion.38
  51.9 55.7 %all-reduce.2.cloned.1.call-done = bf16[256,2304]{1,0:T(8,128)(2,1)} async-done(((bf16[256,2304]{1,0:T(8,128)(2,1)}), bf16[256,2304]{1,0:T(8,128)(2,1)}) %all-reduce.2.cloned.1.call-update) | async-done | bytes 1179664 | tf_op jit(solution)/shard_map/psum | solution.py:106
  107.6 3.3 %convert_add_fusion = (f32[256,2304]{1,0:T(8,128)}, f32[256]{0:T(256)S(1)}) fusion(bf16[256,2304]{1,0:T(8,128)(2,1)S(1)} %copy-done.2, bf16[256,2304]{1,0:T(8,128)(2,1)} %all-reduce.2.cloned.1.call-done), kind=kLoop, calls=%fused_computation.19 | loop fusion | flops 2948864 | bytes 4719616 | tf_op jit(solution)/shard_map/add | solution.py:109
  110.9 0.0 slice-start.1
  110.9 1.3 convolution_convert_fusion
  112.2 45.5 %all_to_all.10 = bf16[8,96,2304]{2,1,0:T(8,128)(2,1)S(1)} all-to-all(bf16[8,96,2304]{2,1,0:T(8,128)(2,1)S(1)} %bitcast.78), channel_id=1, replica_groups=mesh['req'=8,'tp'=4] {'req'}, dimensions={0} | all-to-all | bytes 7077888 | tf_op jit(solution)/shard_map/all_to_all | solution.py:134
  157.7 7.1 %fusion.10 = f32[768,1440]{0,1:T(8,128)} fusion(bf16[768,2304]{1,0:T(8,128)(2,1)S(1)} %bitcast.80, bf16[1,2304,1440]{1,2,0:T(8,128)(2,1)S(1)} %bitcast.92), kind=kOutput, calls=%fused_computation.13 | convolution fusion | flops 5096079360 | bytes 14598144 | tf_op jit(solution)/shard_map/dot_general | solution.py:136
  164.8 29.2 %fusion.12 = bf16[768,2304]{1,0:T(8,128)(2,1)} fusion(bf16[1,1440,2304]{2,1,0:T(8,128)(2,1)} %param.25, f32[768,1440]{0,1:T(8,128)} %fusion.10, bf16[768,2304]{1,0:T(8,128)(2,1)S(1)} %bitcast.81, bf16[1,2304,1440]{1,2,0:T(8,128)(2,1)} %param.24), kind=kOutput, calls=%fused_computation.16 | convolution fusion | flops 10200563712 | bytes 24772608 | tf_op jit(solution)/shard_map/dot_general | solution.py:139
  194.1 3.7 %all-to-all-start.1 = ((bf16[8,96,2304]{2,1,0:T(8,128)(2,1)}), bf16[8,96,2304]{2,1,0:T(8,128)(2,1)S(1)}, u32[]{:S(2)}, u32[]{:S(2)}) async-start(bf16[8,96,2304]{2,1,0:T(8,128)(2,1)} %bitcast.79), calls=%async_computation.1 | async-start | bytes 7077888 | tf_op jit(solution)/shard_map/all_to_all | solution.py:142
  197.7 0.0 reduce-scatter.2.cloned.1.call-start
  197.8 0.8 copy.51
  198.6 1.0 mul.229
  199.7 0.8 copy.46
  200.5 1.0 reshape.267
  201.5 0.6 pad_clamp_fusion
  202.1 2.2 fusion.70
  204.3 3.5 %gather_fusion.1 = f32[512]{0:T(512)S(1)} fusion(f32[256,8]{0,1:T(8,128)S(1)} %fusion.70, s32[512]{0:T(512)S(1)} %reshape.267), kind=kCustom, calls=%fused_computation.1 | custom fusion | bytes 8192 | tf_op jit(solution)/shard_map/jit(take_along_axis)/gather | solution.py:113
  207.8 0.8 reshape.270
  208.6 1.0 copy.47
  209.6 0.7 and_select_fusion
  210.3 29.4 %all-to-all-done.1 = bf16[8,96,2304]{2,1,0:T(8,128)(2,1)S(1)} async-done(((bf16[8,96,2304]{2,1,0:T(8,128)(2,1)}), bf16[8,96,2304]{2,1,0:T(8,128)(2,1)S(1)}, u32[]{:S(2)}, u32[]{:S(2)}) %all-to-all-start.1) | async-done | bytes 3538976 | tf_op jit(solution)/shard_map/all_to_all | solution.py:142
  239.8 3.6 %gather_fusion = bf16[512,2304]{1,0:T(8,128)(2,1)} fusion(bf16[768,2304]{1,0:T(8,128)(2,1)S(1)} %bitcast.77, s32[1024]{0:T(1024)} %pad_clamp_fusion), kind=kCustom, calls=%fused_computation | custom fusion | bytes 4720640 | tf_op jit(solution)/shard_map/jit(_take)/gather | solution.py:149
  243.3 4.8 %gather.12 = bf16[256,2,2304]{2,1,0:T(2,128)(2,1)S(1)} reshape(bf16[512,2304]{1,0:T(8,128)(2,1)} %gather_fusion) | data formatting | bytes 4718592 | tf_op jit(solution)/shard_map/jit(_take)/gather | solution.py:149
  248.1 0.5 fusion.35
  248.7 1.4 fusion.33
  250.0 0.0 reduce-scatter.2.cloned.1.call-update
  250.0 27.1 %reduce-scatter.2.cloned.1.call-done = bf16[64,2304]{1,0:T(8,128)(2,1)} async-done(((bf16[256,2304]{1,0:T(8,128)(2,1)}), bf16[64,2304]{1,0:T(8,128)(2,1)}) %reduce-scatter.2.cloned.1.call-update) | async-done | bytes 294928 | tf_op jit(solution)/shard_map/reduce_scatter | solution.py:152
  277.1 1.9 add_convert_fusion
  (39 shorter events, 0.2 us)
Async XLA Ops:
  6.5 40.2 %copy-start = (bf16[576,2304]{1,0:T(8,128)(2,1)S(1)}, bf16[576,2304]{1,0:T(8,128)(2,1)}, u32[]{:S(2)}) copy-start(bf16[576,2304]{1,0:T(8,128)(2,1)} %param.19) | copy-start | bytes 7962628
  6.5 101.1 %all-reduce.2.cloned.1.call-start = ((), (), s32[]{:S(2)}) async-start(), calls=%async_computation.3 | async-start | bytes 2359296 | tf_op jit(solution)/shard_map/psum | solution.py:106
  14.4 1.8 copy-start.8
  26.0 10.6 %copy-start.9 = (bf16[1,2048,576]{1,2,0:T(8,128)(2,1)S(1)}, bf16[1,2048,576]{1,2,0:T(8,128)(2,1)}, u32[]{:S(2)}) copy-start(bf16[1,2048,576]{1,2,0:T(8,128)(2,1)} %param.16) | copy-start | bytes 7077892
  46.7 2.2 copy-start.4
  48.8 58.8 %copy-start.2 = (bf16[256,2304]{1,0:T(8,128)(2,1)S(1)}, bf16[256,2304]{1,0:T(8,128)(2,1)}, u32[]{:S(2)}) copy-start(bf16[256,2304]{1,0:T(8,128)(2,1)} %param.13) | copy-start | bytes 3538948
  49.3 61.6 %copy-start.5 = (f32[2304]{0:T(1024)S(1)}, f32[2304]{0:T(1024)}, u32[]{:S(2)}) copy-start(f32[2304]{0:T(1024)} %param.20) | copy-start | bytes 27652
  107.6 3.3 %copy-start.3 = (bf16[256,2304]{1,0:T(8,128)(2,1)S(1)}, bf16[256,2304]{1,0:T(8,128)(2,1)}, u32[]{:S(2)}) copy-start(bf16[256,2304]{1,0:T(8,128)(2,1)} %all-reduce.2.cloned.1.call-done) | copy-start | bytes 3538948
  107.6 50.1 %slice-start = ((s8[6635520]{0:T(1024)(128)(4,1)}), s8[4194304]{0:T(1024)(128)(4,1)S(1)}, s32[]{:S(2)}) async-start(s8[6635520]{0:T(1024)(128)(4,1)} %bitcast.91), calls=%async_computation.5 | async-start | bytes 8388608
  110.9 1.3 copy-start.6
  110.9 46.8 %slice-start.1 = ((s8[6635520]{0:T(1024)(128)(4,1)}), s8[2441216]{0:T(1024)(128)(4,1)S(1)}, s32[]{:S(2)}) async-start(s8[6635520]{0:T(1024)(128)(4,1)} %bitcast.91), calls=%async_computation.6 | async-start | bytes 4882432
  194.1 45.7 %all-to-all-start.1 = ((bf16[8,96,2304]{2,1,0:T(8,128)(2,1)}), bf16[8,96,2304]{2,1,0:T(8,128)(2,1)S(1)}, u32[]{:S(2)}, u32[]{:S(2)}) async-start(bf16[8,96,2304]{2,1,0:T(8,128)(2,1)} %bitcast.79), calls=%async_computation.1 | async-start | bytes 7077888 | tf_op jit(solution)/shard_map/all_to_all | solution.py:142
  197.7 79.4 %reduce-scatter.2.cloned.1.call-start = ((), (), s32[]{:S(2)}) async-start(), calls=%async_computation.4 | async-start | bytes 1474560 | tf_op jit(solution)/shard_map/reduce_scatter | solution.py:152
  243.3 4.8 %copy-start.7 = (pred[256,2]{0,1:T(4,128)(4,1)S(1)}, pred[256,2]{0,1:T(4,128)(4,1)}, u32[]{:S(2)}) copy-start(pred[256,2]{0,1:T(4,128)(4,1)} %get-tuple-element.5) | copy-start | bytes 1540
  248.6 30.4 %copy-start.1 = (bf16[576,2304]{1,0:T(8,128)(2,1)S(1)}, bf16[576,2304]{1,0:T(8,128)(2,1)}, u32[]{:S(2)}) copy-start(bf16[576,2304]{1,0:T(8,128)(2,1)} %param.19) | copy-start | bytes 7962628
Sparse Core Ops, SparseCore 0:
  49.0 58.5 all-reduce.1
  250.2 26.9 reduce-scatter.1
where the time goes:
time: 290 us; the launch traced here: 286 us
  waiting for transfers between devices  112 us (39%)
  matrix products  67.9 us (23%)
  blocking collectives  45.5 us (16%)
  other arithmetic  23.7 us (8%)
  local copies, waits for them, and re-layouts  18.4 us (6%)
  between operations  14.9 us (5%)
  starting transfers between devices  3.71 us (1%)
    psum x1, waiting for transfers between devices, per_device(): lax.psum(jnp.dot(attended, w_out, preferred_element_type=jnp.float32).ast...  55.7 us
    all_to_all x1, blocking collectives, per_device(): lax.all_to_all(outgoing, 'req', split_axis=0, concat_axis=0, tiled=True)  45.5 us
    all_to_all x1, waiting for transfers between devices, per_device(): lax.all_to_all(partial_value.reshape(received.shape), 'req', split_axis=0...  29.4 us
    dot_general x1, matrix products, per_device(): jnp.dot(activation, expert_down[0], preferred_element_type=jnp.float32)  29.2 us
    reduce_scatter x1, waiting for transfers between devices, per_device(): lax.psum_scatter(local_sum.astype(jnp.bfloat16), 'tp', scatter_dimension=...  27.1 us
    reduce_sum x1, other arithmetic, attention(): totals = jnp.sum(weights, axis=-1)  10.6 us
    dot_general x1, matrix products, attention(): jnp.einsum('hqk,khd->qhd', weights.astype(jnp.bfloat16), all_values, pref...  10 us
    dot_general x1, matrix products, attention(): jnp.einsum('qhd,khd->hqk', queries, all_keys, preferred_element_type=jnp....  9.87 us
  transfers between devices with their start and end apart: 3, of which 3 were waited for; matrix products, arithmetic and copies ran while one was open for 5% of the time, Pallas kernels for 0%

commit v1 on v0

v1 whole, which is shorter than its diff:
```python
import functools
import math

import jax
import jax.numpy as jnp
from jax import lax
from jax.experimental import pallas as pl
from jax.experimental.pallas import tpu as pltpu
from jax.sharding import PartitionSpec as P

HEAD = 64
TOP = 2
CAP = 96
PACK = 16
SLICE = 256
MASKED = -1e30
EPSILON = 1e-05
NT = (((1,), (1,)), ((), ()))


def normalize(inputs, scale_gain):
    mean_square = jnp.mean(inputs * inputs, axis=-1, keepdims=True)
    return inputs * lax.rsqrt(mean_square + EPSILON) * scale_gain


def rotate_rows(inputs, cosine, sine_part):
    half_dim = inputs.shape[0] // 2
    lower_half = inputs[:half_dim]
    upper_half = inputs[half_dim:]
    return jnp.concatenate(
        [
            lower_half * cosine - upper_half * sine_part,
            lower_half * sine_part + upper_half * cosine,
        ],
        axis=0,
    )


def scores_of(first, count, length, shift, tokens, q, kc, kf):
    cache_len = kc.shape[1]
    slots = lax.broadcasted_iota(jnp.int32, (PACK, cache_len), 1)
    top_row = lax.broadcasted_iota(jnp.int32, (PACK, cache_len), 0) == 0
    bias = jnp.where(top_row & (slots >= length), MASKED, 0.0).astype(jnp.bfloat16)
    s_c = jnp.dot(q, jnp.concatenate([kc, bias], axis=0), preferred_element_type=jnp.float32)
    pad = jnp.zeros((PACK, kf.shape[1]), kf.dtype)
    s_f = jnp.dot(q, jnp.concatenate([kf, pad], axis=0), preferred_element_type=jnp.float32)
    row = lax.rem(lax.broadcasted_iota(jnp.int32, (count, 1), 0) + (first + shift), tokens)
    col = lax.rem(lax.broadcasted_iota(jnp.int32, (1, tokens), 1) + shift, tokens)
    return s_c, jnp.where(col <= row, s_f, MASKED)


def mixture(scores, vc, vf):
    s_c, s_f = scores
    top = jnp.maximum(jnp.max(s_c, axis=1, keepdims=True), jnp.max(s_f, axis=1, keepdims=True))
    p_c = jnp.exp(s_c - top)
    p_f = jnp.exp(s_f - top)
    totals = jnp.sum(p_c, axis=1, keepdims=True) + jnp.sum(p_f, axis=1, keepdims=True)
    mixed = lax.dot_general(p_c.astype(jnp.bfloat16), vc, NT, preferred_element_type=jnp.float32)
    mixed = mixed + lax.dot_general(
        p_f.astype(jnp.bfloat16), vf, NT, preferred_element_type=jnp.float32
    )
    return mixed / totals


def attend_heads(heads, make_scores, make_mixture, attended):
    mixed = []
    ahead = make_scores(0)
    for g in range(heads):
        now = ahead
        if g + 1 < heads:
            ahead = make_scores(g + 1)
        mixed.append(make_mixture(g, now))
    attended[pl.program_id(0)] = jnp.concatenate(mixed, axis=1).astype(jnp.bfloat16)


def widened(q):
    count = q.shape[1]
    ones = jnp.where(lax.broadcasted_iota(jnp.int32, (PACK, count), 0) == 0, 1.0, 0.0)
    return jnp.concatenate([q, ones], axis=0).T.astype(jnp.bfloat16)


def head_slice(g):
    return slice(g * HEAD, (g + 1) * HEAD)


def attention_kernel(
    share,
    scalars,
    hidden_ref,
    gain_ref,
    w_ref,
    cos_ref,
    sin_ref,
    kc_ref,
    vc_ref,
    wo_ref,
    *rest,
):
    *out_refs, normed, attended, total = rest
    tokens, width = hidden_ref.shape
    blocks = tokens // share
    rows_here = kc_ref.shape[0]
    heads = rows_here // HEAD
    length, shift = scalars[0], scalars[1] * share

    @pl.when(pl.program_id(0) == 0)
    def _():
        for k in range(0, blocks, 2):
            pair = []
            for i in range(2):
                start = pl.multiple_of(lax.rem(scalars[1] + k + i, blocks) * share, share)
                rows = hidden_ref[pl.ds(start, share), :].astype(jnp.float32)
                pair.append(normalize(rows, gain_ref[...]))
            normed[:, k * share : (k + 2) * share] = jnp.concatenate(pair, axis=0).T.astype(
                jnp.bfloat16
            )

    weights = w_ref[...].reshape(3 * rows_here, width)
    projected = jnp.dot(weights, normed[...], preferred_element_type=jnp.float32)
    cosine, sine_part = cos_ref[...], sin_ref[...]

    def make_scores(g):
        q = rotate_rows(projected[head_slice(g)], cosine, sine_part).astype(jnp.bfloat16)
        q = widened(q.astype(jnp.float32) * HEAD**-0.5)
        kf = rotate_rows(projected[head_slice(heads + g)], cosine, sine_part).astype(jnp.bfloat16)
        return scores_of(0, tokens, length, shift, tokens, q, kc_ref[head_slice(g), :], kf)

    def make_mixture(g, scores):
        vf = projected[head_slice(2 * heads + g)].astype(jnp.bfloat16)
        return mixture(scores, vc_ref[head_slice(g), :], vf)

    attend_heads(heads, make_scores, make_mixture, attended)

    @pl.when(pl.program_id(0) == pl.num_programs(0) - 1)
    def _():
        steps = attended.shape[0]
        total[...] = sum(
            jnp.dot(
                attended[i],
                wo_ref[i * rows_here : (i + 1) * rows_here, :],
                preferred_element_type=jnp.float32,
            )
            for i in range(steps)
        )
        for i, out_ref in enumerate(out_refs):
            ahead = (i + 1) % blocks
            first = width - blocks * SLICE
            place = lax.rem(scalars[1] + i, blocks) * SLICE + first
            lanes = pl.ds(pl.multiple_of(place, SLICE), SLICE)
            out_ref[:, :first] = total[i * share : (i + 1) * share, :first].astype(out_ref.dtype)
            for j in range(blocks):
                start = (ahead + j - 1) % blocks * share
                out_ref[:, first + j * SLICE : first + (j + 1) * SLICE] = total[
                    start : start + share, lanes
                ].astype(out_ref.dtype)


def merge_kernel(share, pieces, scalars, *refs):
    piece_refs = refs[:pieces]
    hidden_ref, gain_ref, router_ref = refs[pieces : pieces + 3]
    first_ref, slice_ref, first_raw_ref, slice_raw_ref, *term_refs = refs[pieces + 3 :]
    tp = len(term_refs)
    me = scalars[0]
    first = first_ref.shape[1]
    exact = functools.partial(
        lax.dot_general,
        dimension_numbers=NT,
        precision=lax.Precision.HIGHEST,
        preferred_element_type=jnp.float32,
    )

    def terms_of(rows, lanes):
        weights = router_ref[:, lanes].astype(jnp.float32) * gain_ref[:, lanes]
        return jnp.concatenate(
            [exact(weights, rows), exact(jnp.ones_like(weights), rows * rows)], axis=0
        )

    def block_start(j):
        return pl.multiple_of(lax.rem(me + j, tp) * share, share)

    total = piece_refs[0][...].astype(jnp.float32)
    for ref in piece_refs[1:]:
        total = total + ref[...].astype(jnp.float32)
    own = hidden_ref[pl.ds(block_start(0), share), :first].astype(jnp.float32) + total[:, :first]
    first_ref[...] = own
    first_raw_ref[...] = own.astype(jnp.bfloat16)
    lanes = pl.ds(pl.multiple_of(first + me * SLICE, SLICE), SLICE)
    terms = []
    for j in range(tp):
        rows = hidden_ref[pl.ds(block_start(j), share), lanes].astype(jnp.float32)
        rows = rows + total[:, first + j * SLICE : first + (j + 1) * SLICE]
        slice_ref[j * share : (j + 1) * share, :] = rows
        slice_raw_ref[j * share : (j + 1) * share, :] = rows.astype(jnp.bfloat16)
        terms.append(terms_of(rows, lanes))
    terms[0] = terms[0] + terms_of(own, slice(0, first))
    for k in range(tp):
        for j in range(tp):
            term_refs[k][j] = terms[(j + k) % tp]


def merge(me_tp, pieces, hidden_in, gain, router_t):
    share, width = pieces[0].shape
    tp = len(pieces)
    tokens = hidden_in.shape[0]
    first = width - tp * SLICE
    experts = router_t.shape[0]
    terms = jax.ShapeDtypeStruct((tp, 2 * experts, share), jnp.float32)
    return pl.pallas_call(
        functools.partial(merge_kernel, share, tp),
        grid_spec=pltpu.PrefetchScalarGridSpec(
            num_scalar_prefetch=1,
            grid=(1,),
            in_specs=[pl.BlockSpec(p.shape, lambda i, s: (0, 0)) for p in pieces]
            + [pl.BlockSpec(a.shape, lambda i, s: (0, 0)) for a in (hidden_in, gain, router_t)],
            out_specs=[
                pl.BlockSpec((share, first), lambda i, s: (0, 0)),
                pl.BlockSpec((tokens, SLICE), lambda i, s: (0, 0)),
            ]
            * 2
            + [pl.BlockSpec(terms.shape, lambda i, s: (0, 0, 0))] * tp,
        ),
        out_shape=[
            jax.ShapeDtypeStruct((share, first), jnp.float32),
            jax.ShapeDtypeStruct((tokens, SLICE), jnp.float32),
            jax.ShapeDtypeStruct((share, first), jnp.bfloat16),
            jax.ShapeDtypeStruct((tokens, SLICE), jnp.bfloat16),
        ]
        + [terms] * tp,
        compiler_params=pltpu.CompilerParams(vmem_limit_bytes=32 * 1024 * 1024),
        cost_estimate=pl.CostEstimate(
            flops=8 * tp * share * width,
            bytes_accessed=2 * tokens * width + 4 * share * width * tp,
            transcendentals=0,
        ),
    )(me_tp.reshape(1), *pieces, hidden_in, gain, router_t)


def assemble_kernel(slices, scalars, first_ref, *refs):
    slice_refs = refs[:slices]
    gain_ref, out_ref = refs[slices:]
    first = first_ref.shape[1]
    width = out_ref.shape[1]
    rows = first_ref[...].astype(jnp.float32)
    parts = [ref[...].astype(jnp.float32) for ref in slice_refs]
    squares = jnp.sum(rows * rows, axis=1, keepdims=True)
    for part in parts:
        squares = squares + jnp.sum(part * part, axis=1, keepdims=True)
    scale = lax.rsqrt(squares / width + EPSILON)
    out_ref[:, :first] = (rows * scale * gain_ref[:, :first]).astype(jnp.bfloat16)
    for k, part in enumerate(parts):
        place = lax.rem(scalars[0] + k, slices) * SLICE + first
        lanes = pl.ds(pl.multiple_of(place, SLICE), SLICE)
        out_ref[:, lanes] = (part * scale * gain_ref[:, lanes]).astype(jnp.bfloat16)


def assemble(me_tp, first_rows, slices, gain):
    rows, first = first_rows.shape
    width = first + SLICE * len(slices)
    tile = 2 * CAP

    def tiles(n):
        return pl.BlockSpec((tile, n), lambda i, s: (i, 0))

    return pl.pallas_call(
        functools.partial(assemble_kernel, len(slices)),
        grid_spec=pltpu.PrefetchScalarGridSpec(
            num_scalar_prefetch=1,
            grid=(rows // tile,),
            in_specs=[tiles(first)]
            + [tiles(SLICE)] * len(slices)
            + [pl.BlockSpec((1, width), lambda i, s: (0, 0))],
            out_specs=tiles(width),
        ),
        out_shape=jax.ShapeDtypeStruct((rows, width), jnp.bfloat16),
        compiler_params=pltpu.CompilerParams(vmem_limit_bytes=16 * 1024 * 1024),
        cost_estimate=pl.CostEstimate(
            flops=8 * rows * width, bytes_accessed=4 * rows * width, transcendentals=rows
        ),
    )(me_tp.reshape(1), first_rows, *slices, gain)


def combine_kernel(width, copies, terms, rows_ref, routes_ref, places_ref, base_ref, *refs):
    term_refs, out_refs = refs[:terms], refs[terms:]
    tp = len(out_refs)
    total = term_refs[0][...]
    for ref in term_refs[1:]:
        total = total + ref[...]
    experts = total.shape[1] // 2
    total = jnp.concatenate([total[j] for j in range(tp)], axis=1).T
    tokens = total.shape[0]
    share = tokens // tp
    scale = lax.rsqrt(total[:, experts : experts + 1] / width + EPSILON)
    logits = total[:, :experts] * scale
    ids = lax.broadcasted_iota(jnp.int32, (tokens, experts), 1)
    slots = lax.broadcasted_iota(jnp.int32, (tokens, rows_ref.shape[0]), 1)
    rows = rows_ref[...]
    chosen, picked = [], []
    for k in range(TOP):
        match = routes_ref[:, k : k + 1] == ids
        chosen.append(jnp.sum(jnp.where(match, logits, 0.0), axis=1, keepdims=True))
        place = places_ref[:, k : k + 1]
        hit = slots == place
        for c in range(1, copies):
            hit = hit | (slots == place + c * CAP)
        picked.append(
            jnp.dot(
                jnp.where(hit, 1.0, 0.0).astype(jnp.bfloat16),
                rows,
                preferred_element_type=jnp.float32,
            )
        )
    first_gate = 1.0 / (1.0 + jnp.exp(chosen[1] - chosen[0]))
    second_gate = 1.0 / (1.0 + jnp.exp(chosen[0] - chosen[1]))
    mixed = first_gate * picked[0] + second_gate * picked[1]
    for k, out_ref in enumerate(out_refs):
        block = mixed[k * share : (k + 1) * share]
        if k * share < base_ref.shape[0]:
            block = block + base_ref[k * share : (k + 1) * share, :]
        out_ref[...] = block.astype(out_ref.dtype)


def combine(width, copies, rows, routes, places, base, terms, kinds):
    tokens = routes.shape[0]
    share = tokens // len(kinds)
    columns = rows.shape[1]

    def full(array):
        return pl.BlockSpec(array.shape, lambda i: (0,) * array.ndim)

    operands = [rows, routes, places, base, *terms]
    return pl.pallas_call(
        functools.partial(combine_kernel, width, copies, len(terms)),
        grid=(1,),
        in_specs=[full(a) for a in operands],
        out_specs=[pl.BlockSpec((share, columns), lambda i: (0, 0))] * len(kinds),
        out_shape=[jax.ShapeDtypeStruct((share, columns), kind) for kind in kinds],
        compiler_params=pltpu.CompilerParams(vmem_limit_bytes=40 * 1024 * 1024),
        cost_estimate=pl.CostEstimate(
            flops=4 * tokens * rows.shape[0] * columns,
            bytes_accessed=2 * rows.shape[0] * columns + 8 * tokens * columns,
            transcendentals=4 * tokens,
        ),
    )(*operands)


def per_device(
    hidden_in,
    cache_lengths,
    key_cache,
    value_cache,
    attn_norm,
    w_qkv,
    w_out,
    ffn_norm,
    router,
    routes,
    expert_gate,
    expert_up,
    expert_down,
):
    token_count, model_width = hidden_in.shape
    local_lanes = w_qkv.shape[2]
    local_heads = local_lanes // HEAD
    cache_len = key_cache.shape[1]
    tp = lax.axis_size("tp")
    me_tp = lax.axis_index("tp")
    req = lax.axis_size("req")
    expert_count = router.shape[1]
    copies = req // expert_count
    share = token_count // tp
    first_width = model_width - tp * SLICE

    def to_block(array, k):
        return lax.ppermute(array, "tp", [(i, (i + k) % tp) for i in range(tp)])

    def from_block(array, k):
        return lax.ppermute(array, "tp", [(i, (i - k) % tp) for i in range(tp)])

    def exchanged(rows):
        blocks = rows.reshape(req, CAP, -1)
        blocks = lax.all_to_all(blocks, "req", split_axis=0, concat_axis=0, tiled=True)
        return blocks.reshape(req * CAP, -1)

    def to_experts(tokens):
        packed = jnp.dot(placing, tokens, preferred_element_type=jnp.float32).astype(jnp.bfloat16)
        packed = packed.reshape(expert_count, 1, CAP, -1)
        return exchanged(
            jnp.broadcast_to(packed, (expert_count, copies, CAP, packed.shape[-1]))
        )

    def from_own(array):
        twice = jnp.concatenate([array, array], axis=0)
        return lax.dynamic_slice_in_dim(twice, me_tp * share, token_count, 0)

    expert_ids = jnp.arange(expert_count, dtype=jnp.int32)
    has = jnp.any(routes[:, :, None] == expert_ids[None, None, :], axis=1)
    token_ids = jnp.arange(token_count, dtype=jnp.int32)
    earlier = (token_ids[None, :] < token_ids[:, None]).astype(jnp.bfloat16)
    rank = jnp.dot(earlier, has.astype(jnp.bfloat16), preferred_element_type=jnp.float32).astype(
        jnp.int32
    )
    slot = from_own(jnp.where(has, rank, -1))
    rolled = from_own(routes)
    named = rolled[:, :, None] == expert_ids[None, None, :]
    slots = jnp.arange(CAP, dtype=jnp.int32)
    placing = (
        (slot.T[:, None, :] == slots[None, :, None])
        .astype(jnp.bfloat16)
        .reshape(expert_count * CAP, token_count)
    )
    places = jnp.sum(jnp.where(named, slot[:, None, :], 0), axis=2) + rolled * (copies * CAP)

    length = cache_lengths[0]
    scalars = jnp.stack([length, (me_tp + 1) % tp]).astype(jnp.int32)
    positions = length + (token_ids + scalars[1] * share) % token_count
    positions = positions.astype(jnp.float32)
    half = HEAD // 2
    frequency = jnp.exp(jnp.arange(half, dtype=jnp.float32) * (-2.0 * math.log(10000.0) / HEAD))
    angles = frequency[:, None] * positions[None, :]
    cosine = jnp.cos(angles)
    sine_part = jnp.sin(angles)
    keys_t = jnp.swapaxes(key_cache[0], 0, 1)
    values_t = jnp.swapaxes(value_cache[0], 0, 1)
    w_t = jnp.swapaxes(w_qkv, 1, 2)
    group = 3 if local_heads % 3 == 0 else 1

    def whole(*shape):
        return pl.BlockSpec(shape, lambda h, s: (0,) * len(shape))

    def head_rows(n):
        return pl.BlockSpec((group * HEAD, n), lambda h, s: (h, 0))

    *sent, own_partial = pl.pallas_call(
        functools.partial(attention_kernel, share),
        grid_spec=pltpu.PrefetchScalarGridSpec(
            num_scalar_prefetch=1,
            grid=(local_heads // group,),
            in_specs=[
                whole(token_count, model_width),
                whole(model_width),
                pl.BlockSpec((3, group * HEAD, model_width), lambda h, s: (0, h, 0)),
                whole(half, token_count),
                whole(half, token_count),
                head_rows(cache_len),
                head_rows(cache_len),
                whole(local_lanes, model_width),
            ],
            out_specs=[whole(share, model_width)] * tp,
            scratch_shapes=[
                pltpu.VMEM((model_width, token_count), jnp.bfloat16),
                pltpu.VMEM((local_heads // group, token_count, group * HEAD), jnp.bfloat16),
                pltpu.VMEM((token_count, model_width), jnp.float32),
            ],
        ),
        out_shape=[jax.ShapeDtypeStruct((share, model_width), jnp.bfloat16)] * tp,
        compiler_params=pltpu.CompilerParams(vmem_limit_bytes=62 * 1024 * 1024),
        cost_estimate=pl.CostEstimate(
            flops=token_count * local_lanes * (8 * model_width + 4 * (cache_len + token_count)),
            bytes_accessed=2 * local_lanes * (4 * model_width + 2 * cache_len),
            transcendentals=token_count * (cache_len + token_count) * local_heads,
        ),
    )(
        scalars,
        hidden_in,
        attn_norm,
        w_t,
        cosine,
        sine_part,
        keys_t,
        values_t,
        w_out,
    )
    arrived = [to_block(piece, k + 1) for k, piece in enumerate(sent)]

    gain = ffn_norm.reshape(1, model_width)
    first_residual, slice_residual, first_raw, slice_raw, *terms = merge(
        me_tp, [own_partial, *arrived], hidden_in, gain, jnp.swapaxes(router, 0, 1)
    )

    slice_downs = lax.optimization_barrier(
        [
            lax.dynamic_slice_in_dim(
                expert_down[0], first_width + (me_tp + k) % tp * SLICE, SLICE, 1
            )
            for k in range(tp)
        ]
    )

    gathered = jnp.concatenate(
        [first_raw] + [from_block(first_raw, k) for k in range(1, tp)], axis=0
    )
    slice_rows = to_experts(slice_raw)

    first_rows = to_experts(gathered)
    slices = [slice_rows] + [from_block(slice_rows, k) for k in range(1, tp)]
    token_rows = assemble(me_tp, first_rows, slices, gain)

    token_rows, *terms = lax.optimization_barrier((token_rows, *terms))
    terms = [terms[0]] + [to_block(terms[k], k) for k in range(1, tp)]

    gate_proj = jnp.dot(token_rows, expert_gate[0], preferred_element_type=jnp.float32)
    up_proj = jnp.dot(token_rows, expert_up[0], preferred_element_type=jnp.float32)
    activation = (jax.nn.silu(gate_proj) * up_proj).astype(jnp.bfloat16)
    activation = lax.optimization_barrier(activation)

    def down(rows, weights):
        return jnp.dot(rows, weights, preferred_element_type=jnp.float32).astype(jnp.bfloat16)

    slice_terms = lax.optimization_barrier([down(activation, w) for w in slice_downs])
    coming = [to_block(slice_terms[k], k) for k in range(1, tp)]
    activation, _ = lax.optimization_barrier((activation, slice_terms[tp - 1]))
    first_back = exchanged(down(activation, expert_down[0, :, :first_width]))
    slice_sum = slice_terms[0].astype(jnp.float32)
    for term in coming:
        slice_sum = slice_sum + term.astype(jnp.float32)
    slice_sum, first_back = lax.optimization_barrier((slice_sum.astype(jnp.bfloat16), first_back))

    kinds = [jnp.bfloat16] * tp
    first_out, *first_shares = combine(
        model_width,
        copies,
        first_back,
        rolled,
        places,
        first_residual,
        terms,
        [jnp.float32, *kinds[1:]],
    )
    for k, piece in enumerate(first_shares):
        first_out = first_out + to_block(piece, k + 1).astype(jnp.float32)
    slice_outs = combine(
        model_width,
        copies,
        exchanged(slice_sum),
        rolled,
        places,
        slice_residual,
        terms,
        kinds,
    )
    slice_outs = [slice_outs[0]] + [to_block(slice_outs[k], k) for k in range(1, tp)]
    slice_outs = jnp.stack(slice_outs[::-1] * 2)
    slice_outs = lax.dynamic_slice_in_dim(slice_outs, (2 * tp - 1 - me_tp) % tp, tp, 0)
    return jnp.concatenate(
        [first_out.astype(jnp.bfloat16)] + [slice_outs[j] for j in range(tp)], axis=1
    )


def solution(mesh):
    return jax.shard_map(
        per_device,
        mesh=mesh,
        in_specs=(
            P("req", None),
            P("req"),
            P("req", None, "tp"),
            P("req", None, "tp"),
            P(),
            P(None, None, "tp"),
            P("tp", None),
            P(),
            P(),
            P("req", None),
            P("req", None, "tp"),
            P("req", None, "tp"),
            P("req", "tp", None),
        ),
        out_specs=P(("req", "tp"), None),
        check_vma=False,
    )
```

time: 290 us -> 223 us (0.77); the launches traced: 286 us -> 223 us
  starting transfers between devices: 3.71 us -> 67.5 us
  blocking collectives: 45.5 us -> 0 us
  matrix products: 67.9 us -> 26.7 us
  Pallas kernels: 0 us -> 27.1 us
  waiting for transfers between devices: 112 us -> 88.1 us
  other arithmetic: 23.7 us -> 4.24 us
  between operations: 14.9 us -> 1.06 us
  local copies, waits for them, and re-layouts: 18.4 us -> 7.93 us
    ppermute x0 -> x21, waiting for transfers between devices: none -> 88.1 us  [the longest x6 44.5 us: from_block(): return lax.ppermute(array, 'tp', [(i, (i - k) % tp) for i in range(tp)])]
    psum x1 -> x0, waiting for transfers between devices: 55.7 us -> none  [per_device(): lax.psum(jnp.dot(attended, w_out, preferred_element_type=jnp.float32).ast...]
    ppermute x0 -> x21, starting transfers between devices: none -> 52.1 us  [the longest x15 40 us: to_block(): return lax.ppermute(array, 'tp', [(i, (i + k) % tp) for i in range(tp)])]
    all_to_all x1 -> x0, blocking collectives: 45.5 us -> none  [per_device(): lax.all_to_all(outgoing, 'req', split_axis=0, concat_axis=0, tiled=True)]
    dot_general x7 -> x9, matrix products: 60.8 us -> 19.1 us  [the longest x5 10 us: down(): jnp.dot(rows, weights, preferred_element_type=jnp.float32)]
    all_to_all x1 -> x4, waiting for transfers between devices: 29.4 us -> 0.01 us  [exchanged(): lax.all_to_all(blocks, 'req', split_axis=0, concat_axis=0, tiled=True)]
    pallas_call x0 -> x5, Pallas kernels: none -> 27.1 us  [the longest x1 21.5 us: per_device(): pl.pallas_call(functools.partial(attention_kernel, share), grid_spec=pltp...]
    reduce_scatter x1 -> x0, waiting for transfers between devices: 27.1 us -> none  [per_device(): lax.psum_scatter(local_sum.astype(jnp.bfloat16), 'tp', scatter_dimension=...]
  transfers between devices with their start and end apart: 3 -> 25, of which waited for: 3 -> 12; matrix products, arithmetic and copies ran while one was open for 5% -> 4% of each run, Pallas kernels for 0% -> 1%
where the time goes in v1:
time: 223 us
  waiting for transfers between devices  88.1 us (40%)
  starting transfers between devices  67.5 us (30%)
  Pallas kernels  27.1 us (12%)
  matrix products  26.7 us (12%)
  local copies, waits for them, and re-layouts  7.93 us (4%)
  other arithmetic  4.24 us (2%)
    ppermute x6, waiting for transfers between devices, from_block(): return lax.ppermute(array, 'tp', [(i, (i - k) % tp) for i in range(tp)])  44.5 us
    ppermute x15, waiting for transfers between devices, to_block(): return lax.ppermute(array, 'tp', [(i, (i + k) % tp) for i in range(tp)])  43.6 us
    ppermute x15, starting transfers between devices, to_block(): return lax.ppermute(array, 'tp', [(i, (i + k) % tp) for i in range(tp)])  40 us
    pallas_call x1, Pallas kernels, per_device(): pl.pallas_call(functools.partial(attention_kernel, share), grid_spec=pltp...  21.5 us
    all_to_all x4, starting transfers between devices, exchanged(): lax.all_to_all(blocks, 'req', split_axis=0, concat_axis=0, tiled=True)  15.4 us
    ppermute x6, starting transfers between devices, from_block(): return lax.ppermute(array, 'tp', [(i, (i - k) % tp) for i in range(tp)])  12.1 us
    dot_general x5, matrix products, down(): jnp.dot(rows, weights, preferred_element_type=jnp.float32)  10 us
    dot_general x1, matrix products, per_device(): jnp.dot(token_rows, expert_gate[0], preferred_element_type=jnp.float32)  7.65 us
  transfers between devices with their start and end apart: 25, of which 12 were waited for; matrix products, arithmetic and copies ran while one was open for 4% of the time, Pallas kernels for 1%

profile of v1, /device:TPU:0, one launch (start us, length us, event | category | flops | bytes accessed | tf_op | source)
XLA Modules:
  0.0 222.7 jit_solution(3588854908998623247)
XLA Ops:
  2.2 21.5 %shard_map.127 = (bf16[64,2304]{1,0:T(8,128)(2,1)}, bf16[64,2304]{1,0:T(8,128)(2,1)}, bf16[64,2304]{1,0:T(8,128)(2,1)}, bf16[64,2304]{1,0:T(8,128)(2,1)}) custom-call(s32[2]{0:T(128)} %pad_add_fusion.scalars, bf16[256,2304]{1,0:T(8,128)(2,1)} %refs_4_.1, f32[2304]{0:T(1024)} %gain_ref.1, bf16[3,576,2304]{2,1,0:T(8,128)(2,1)} %bitcast.96, ...), custom_call_target="tpu_custom_call" | custom-call | flops 4076863488 | bytes 15335424 | tf_op jit(solution)/shard_map/pallas_call | solution.py:433
  23.7 3.0 %collective-permute-start = (bf16[64,2304]{1,0:T(8,128)(2,1)}, bf16[64,2304]{1,0:T(8,128)(2,1)S(1)}, u32[]{:S(2)}, u32[]{:S(2)}) collective-permute-start(bf16[64,2304]{1,0:T(8,128)(2,1)} %get-tuple-element.42), channel_id=1, source_target_pairs={{0,1},{1,2},{2,3},{3,0},{4,5},{5,6},{6,7},{7,4},{8,9},{9,10},{10,1... | collective-permute-start | bytes 884744 | tf_op jit(solution)/shard_map/ppermute | solution.py:374
  26.7 2.6 %collective-permute-start.1 = (bf16[64,2304]{1,0:T(8,128)(2,1)}, bf16[64,2304]{1,0:T(8,128)(2,1)S(1)}, u32[]{:S(2)}, u32[]{:S(2)}) collective-permute-start(bf16[64,2304]{1,0:T(8,128)(2,1)} %get-tuple-element.43), channel_id=1, source_target_pairs={{0,2},{1,3},{2,0},{3,1},{4,6},{5,7},{6,4},{7,5},{8,10},{9,11},{10,... | collective-permute-start | bytes 884744 | tf_op jit(solution)/shard_map/ppermute | solution.py:374
  29.3 1.4 collective-permute-start.2
  31.3 5.7 %collective-permute-done.refs_1_ = bf16[64,2304]{1,0:T(8,128)(2,1)S(1)} collective-permute-done((bf16[64,2304]{1,0:T(8,128)(2,1)}, bf16[64,2304]{1,0:T(8,128)(2,1)S(1)}, u32[]{:S(2)}, u32[]{:S(2)}) %collective-permute-start) | collective-permute-done | bytes 294944 | tf_op jit(solution)/shard_map/ppermute | solution.py:374
  37.0 11.8 %collective-permute-done.1.refs_2_ = bf16[64,2304]{1,0:T(8,128)(2,1)S(1)} collective-permute-done((bf16[64,2304]{1,0:T(8,128)(2,1)}, bf16[64,2304]{1,0:T(8,128)(2,1)S(1)}, u32[]{:S(2)}, u32[]{:S(2)}) %collective-permute-start.1) | collective-permute-done | bytes 294944 | tf_op jit(solution)/shard_map/ppermute | solution.py:374
  48.8 1.0 copy-done.1
  49.7 1.1 shard_map.128
  51.6 1.0 convolution_convert_fusion.5
  52.6 3.7 %all-to-all-start.1 = ((bf16[8,96,256]{2,1,0:T(8,128)(2,1)}), bf16[8,96,256]{2,1,0:T(8,128)(2,1)S(1)}, u32[]{:S(2)}, u32[]{:S(2)}) async-start(bf16[8,96,256]{2,1,0:T(8,128)(2,1)} %bitcast.13), calls=%async_computation.1 | async-start | bytes 786432 | tf_op jit(solution)/shard_map/all_to_all | solution.py:381
  56.3 7.8 %collective-permute-start.3 = (bf16[64,1280]{1,0:T(8,128)(2,1)S(1)}, bf16[64,1280]{1,0:T(8,128)(2,1)S(1)}, u32[]{:S(2)}, u32[]{:S(2)}) collective-permute-start(bf16[64,1280]{1,0:T(8,128)(2,1)S(1)} %get-tuple-element.45), channel_id=1, source_target_pairs={{0,3},{1,0},{2,1},{3,2},{4,7},{5,4},{6,5},{7,6},{8,11},{9,8},{10,9... | collective-permute-start | bytes 491528 | tf_op jit(solution)/shard_map/ppermute | solution.py:377
  64.8 4.0 %collective-permute-done.3 = bf16[64,1280]{1,0:T(8,128)(2,1)S(1)} collective-permute-done((bf16[64,1280]{1,0:T(8,128)(2,1)S(1)}, bf16[64,1280]{1,0:T(8,128)(2,1)S(1)}, u32[]{:S(2)}, u32[]{:S(2)}) %collective-permute-start.3) | collective-permute-done | bytes 163872 | tf_op jit(solution)/shard_map/ppermute | solution.py:377
  68.7 10.9 %collective-permute-done.4 = bf16[64,1280]{1,0:T(8,128)(2,1)S(1)} collective-permute-done((bf16[64,1280]{1,0:T(8,128)(2,1)S(1)}, bf16[64,1280]{1,0:T(8,128)(2,1)S(1)}, u32[]{:S(2)}, u32[]{:S(2)}) %collective-permute-start.4) | collective-permute-done | bytes 163872 | tf_op jit(solution)/shard_map/ppermute | solution.py:377
  79.7 2.0 convolution_convert_fusion
  81.7 3.9 %all-to-all-start = ((bf16[8,96,1280]{2,1,0:T(8,128)(2,1)}), bf16[8,96,1280]{2,1,0:T(8,128)(2,1)S(1)}, u32[]{:S(2)}, u32[]{:S(2)}) async-start(bf16[8,96,1280]{2,1,0:T(8,128)(2,1)} %bitcast.99), calls=%async_computation | async-start | bytes 3932160 | tf_op jit(solution)/shard_map/all_to_all | solution.py:381
  85.6 1.7 collective-permute-start.7
  87.3 2.0 collective-permute-start.8
  89.2 3.4 %dynamic-slice_bitcast_fusion = (bf16[1440,256]{1,0:T(8,128)(2,1)}, bf16[1440,256]{1,0:T(8,128)(2,1)}, bf16[1440,256]{1,0:T(8,128)(2,1)}, bf16[1440,256]{1,0:T(8,128)(2,1)}) fusion(bf16[1,1440,2304]{2,1,0:T(8,128)(2,1)} %param.25, s32[]{:T(128)S(6)} %select_n.72, s32[]{:T(128)S(6)} %select_n.70, s32[]{:T(128)S(6)} %select_n.68, s32[]{:T(128)S(6)} %select_n.67), kind=kLoop, calls=%fused_computation.19 | loop fusion | bytes 5898256 | tf_op jit(solution)/shard_map/dynamic_slice | solution.py:482
  92.6 4.6 %collective-permute-done.6.refs_1_ = bf16[768,256]{1,0:T(8,128)(2,1)S(1)} collective-permute-done((bf16[768,256]{1,0:T(8,128)(2,1)S(1)}, bf16[768,256]{1,0:T(8,128)(2,1)S(1)}, u32[]{:S(2)}, u32[]{:S(2)}) %collective-permute-start.6) | collective-permute-done | bytes 393248 | tf_op jit(solution)/shard_map/ppermute | solution.py:377
  97.3 25.0 %collective-permute-done.7.refs_2_ = bf16[768,256]{1,0:T(8,128)(2,1)S(1)} collective-permute-done((bf16[768,256]{1,0:T(8,128)(2,1)S(1)}, bf16[768,256]{1,0:T(8,128)(2,1)S(1)}, u32[]{:S(2)}, u32[]{:S(2)}) %collective-permute-start.7) | collective-permute-done | bytes 393248 | tf_op jit(solution)/shard_map/ppermute | solution.py:377
  122.3 1.8 shard_map.129
  124.1 7.6 %fusion.2 = f32[768,1440]{0,1:T(8,128)S(1)} fusion(bf16[768,2304]{1,0:T(8,128)(2,1)S(1)} %shard_map.129, bf16[1,2304,1440]{1,2,0:T(8,128)(2,1)} %param.23), kind=kOutput, calls=%fused_computation.2 | convolution fusion | flops 5096079360 | bytes 14598144 | tf_op jit(solution)/shard_map/dot_general | solution.py:501
  131.8 5.9 %multiply_convert_fusion = bf16[768,1440]{0,1:T(8,128)(2,1)S(1)} fusion(f32[768,1440]{0,1:T(8,128)S(1)} %fusion.2, bf16[768,2304]{1,0:T(8,128)(2,1)S(1)} %shard_map.129, bf16[1,2304,1440]{1,2,0:T(8,128)(2,1)S(1)} %bitcast.105), kind=kOutput, calls=%fused_computation.4 | convolution fusion | flops 5102714880 | bytes 16809984 | tf_op jit(solution)/shard_map/dot_general | solution.py:502
  137.7 1.6 convolution_convert_fusion.1
  139.4 1.6 convolution_convert_fusion.2
  140.9 1.6 convolution_convert_fusion.3
  142.5 0.8 convolution_convert_fusion.4
  143.4 4.5 %fusion.9 = bf16[768,1280]{1,0:T(8,128)(2,1)} fusion(bf16[768,1440]{0,1:T(8,128)(2,1)S(1)} %multiply_convert_fusion, bf16[1,1440,2304]{2,1,0:T(8,128)(2,1)S(1)} %bitcast.103), kind=kOutput, calls=%fused_computation.9 | convolution fusion | flops 2832138240 | bytes 7864320 | tf_op jit(solution)/shard_map/dot_general | solution.py:507
  147.9 4.0 %all-to-all-start.2 = ((bf16[8,96,1280]{2,1,0:T(8,128)(2,1)}), bf16[8,96,1280]{2,1,0:T(8,128)(2,1)S(1)}, u32[]{:S(2)}, u32[]{:S(2)}) async-start(bf16[8,96,1280]{2,1,0:T(8,128)(2,1)} %bitcast.100), calls=%async_computation.2 | async-start | bytes 3932160 | tf_op jit(solution)/shard_map/all_to_all | solution.py:381
  151.8 1.3 collective-permute-start.10
  153.6 1.6 collective-permute-start.9
  155.9 2.6 %collective-permute-start.13 = (f32[4,16,64]{2,1,0:T(8,128)S(1)}, f32[4,16,64]{2,1,0:T(8,128)S(1)}, u32[]{:S(2)}, u32[]{:S(2)}) collective-permute-start(f32[4,16,64]{2,1,0:T(8,128)S(1)} %copy-done.12), channel_id=1, source_target_pairs={{0,2},{1,3},{2,0},{3,1},{4,6},{5,7},{6,4},{7,5},{8,10},{9,11},{10,... | collective-permute-start | bytes 49160 | tf_op jit(solution)/shard_map/ppermute | solution.py:374
  158.6 13.8 %collective-permute-done.10 = bf16[768,256]{1,0:T(8,128)(2,1)} collective-permute-done((bf16[768,256]{1,0:T(8,128)(2,1)}, bf16[768,256]{1,0:T(8,128)(2,1)}, u32[]{:S(2)}, u32[]{:S(2)}) %collective-permute-start.10) | collective-permute-done | bytes 393248 | tf_op jit(solution)/shard_map/ppermute | solution.py:374
  172.4 8.4 %collective-permute-start.14 = (f32[4,16,64]{2,1,0:T(8,128)S(1)}, f32[4,16,64]{2,1,0:T(8,128)S(1)}, u32[]{:S(2)}, u32[]{:S(2)}) collective-permute-start(f32[4,16,64]{2,1,0:T(8,128)S(1)} %copy-done.10), channel_id=1, source_target_pairs={{0,3},{1,0},{2,1},{3,2},{4,7},{5,4},{6,5},{7,6},{8,11},{9,8},{10,9... | collective-permute-start | bytes 49160 | tf_op jit(solution)/shard_map/ppermute | solution.py:374
  180.8 1.8 collective-permute-done.11
  182.6 2.2 add_convert_fusion
  184.8 3.8 %all-to-all-start.3 = ((bf16[8,96,256]{2,1,0:T(8,128)(2,1)}), bf16[8,96,256]{2,1,0:T(8,128)(2,1)S(1)}, u32[]{:S(2)}, u32[]{:S(2)}) async-start(bf16[8,96,256]{2,1,0:T(8,128)(2,1)} %bitcast.101), calls=%async_computation.3 | async-start | bytes 786432 | tf_op jit(solution)/shard_map/all_to_all | solution.py:381
  188.7 2.1 collective-permute-done.13.refs_2_
  190.8 1.0 copy-done.8
  191.8 2.0 shard_map.130
  193.8 6.1 %collective-permute-start.15 = (bf16[64,1280]{1,0:T(8,128)(2,1)}, bf16[64,1280]{1,0:T(8,128)(2,1)S(1)}, u32[]{:S(2)}, u32[]{:S(2)}) collective-permute-start(bf16[64,1280]{1,0:T(8,128)(2,1)} %get-tuple-element.68), channel_id=1, source_target_pairs={{0,1},{1,2},{2,3},{3,0},{4,5},{5,6},{6,7},{7,4},{8,9},{9,10},{10,1... | collective-permute-start | bytes 491528 | tf_op jit(solution)/shard_map/ppermute | solution.py:374
  199.9 2.4 %collective-permute-start.17 = (bf16[64,1280]{1,0:T(8,128)(2,1)S(1)}, bf16[64,1280]{1,0:T(8,128)(2,1)S(1)}, u32[]{:S(2)}, u32[]{:S(2)}) collective-permute-start(bf16[64,1280]{1,0:T(8,128)(2,1)S(1)} %get-tuple-element.70), channel_id=1, source_target_pairs={{0,3},{1,0},{2,1},{3,2},{4,7},{5,4},{6,5},{7,6},{8,11},{9,8},{10,9... | collective-permute-start | bytes 491528 | tf_op jit(solution)/shard_map/ppermute | solution.py:374
  202.9 2.1 collective-permute-start.18
  205.0 5.7 %collective-permute-done.16 = bf16[64,1280]{1,0:T(8,128)(2,1)S(1)} collective-permute-done((bf16[64,1280]{1,0:T(8,128)(2,1)}, bf16[64,1280]{1,0:T(8,128)(2,1)S(1)}, u32[]{:S(2)}, u32[]{:S(2)}) %collective-permute-start.16) | collective-permute-done | bytes 163872 | tf_op jit(solution)/shard_map/ppermute | solution.py:374
  210.6 1.0 collective-permute-done.17
  211.7 2.1 collective-permute-start.19
  213.8 5.8 %collective-permute-start.20 = (bf16[64,256]{1,0:T(8,128)(2,1)S(1)}, bf16[64,256]{1,0:T(8,128)(2,1)S(1)}, u32[]{:S(2)}, u32[]{:S(2)}) collective-permute-start(bf16[64,256]{1,0:T(8,128)(2,1)S(1)} %get-tuple-element.75), channel_id=1, source_target_pairs={{0,1},{1,2},{2,3},{3,0},{4,5},{5,6},{6,7},{7,4},{8,9},{9,10},{10,1... | collective-permute-start | bytes 98312 | tf_op jit(solution)/shard_map/ppermute | solution.py:374
  219.6 1.7 collective-permute-done.20
  (106 shorter events, 6.8 us)
Async XLA Ops:
  2.2 28.5 %copy-start.22 = (f32[2304]{0:T(1024)S(1)}, f32[2304]{0:T(1024)}, u32[]{:S(2)}) copy-start(f32[2304]{0:T(1024)} %param.20) | copy-start | bytes 27652
  2.2 28.5 %copy-start.23 = (s32[256,2]{0,1:T(2,128)S(1)}, s32[256,2]{0,1:T(2,128)}, u32[]{:S(2)}) copy-start(s32[256,2]{0,1:T(2,128)} %param.22) | copy-start | bytes 6148
  2.2 46.6 %copy-start = (bf16[256,2304]{1,0:T(8,128)(2,1)S(1)}, bf16[256,2304]{1,0:T(8,128)(2,1)}, u32[]{:S(2)}) copy-start(bf16[256,2304]{1,0:T(8,128)(2,1)} %refs_4_.1) | copy-start | bytes 3538948
  2.2 46.6 %copy-start.4 = (bf16[2304,8]{0,1:T(8,128)(2,1)S(1)}, bf16[2304,8]{0,1:T(8,128)(2,1)}, u32[]{:S(2)}) copy-start(bf16[2304,8]{0,1:T(8,128)(2,1)} %param.21) | copy-start | bytes 110596
  23.7 13.2 %collective-permute-start = (bf16[64,2304]{1,0:T(8,128)(2,1)}, bf16[64,2304]{1,0:T(8,128)(2,1)S(1)}, u32[]{:S(2)}, u32[]{:S(2)}) collective-permute-start(bf16[64,2304]{1,0:T(8,128)(2,1)} %get-tuple-element.42), channel_id=1, source_target_pairs={{0,1},{1,2},{2,3},{3,0},{4,5},{5,6},{6,7},{7,4},{8,9},{9,10},{10,1... | collective-permute-start | bytes 884744 | tf_op jit(solution)/shard_map/ppermute | solution.py:374
  26.7 22.0 %collective-permute-start.1 = (bf16[64,2304]{1,0:T(8,128)(2,1)}, bf16[64,2304]{1,0:T(8,128)(2,1)S(1)}, u32[]{:S(2)}, u32[]{:S(2)}) collective-permute-start(bf16[64,2304]{1,0:T(8,128)(2,1)} %get-tuple-element.43), channel_id=1, source_target_pairs={{0,2},{1,3},{2,0},{3,1},{4,6},{5,7},{6,4},{7,5},{8,10},{9,11},{10,... | collective-permute-start | bytes 884744 | tf_op jit(solution)/shard_map/ppermute | solution.py:374
  29.3 19.4 %collective-permute-start.2 = (bf16[64,2304]{1,0:T(8,128)(2,1)}, bf16[64,2304]{1,0:T(8,128)(2,1)S(1)}, u32[]{:S(2)}, u32[]{:S(2)}) collective-permute-start(bf16[64,2304]{1,0:T(8,128)(2,1)} %get-tuple-element.44), channel_id=1, source_target_pairs={{0,3},{1,0},{2,1},{3,2},{4,7},{5,4},{6,5},{7,6},{8,11},{9,8},{10,9... | collective-permute-start | bytes 884744 | tf_op jit(solution)/shard_map/ppermute | solution.py:374
  31.0 17.8 %copy-start.20 = (s32[256,8]{0,1:T(8,128)}, s32[256,8]{0,1:T(8,128)S(1)}, u32[]{:S(2)}) copy-start(s32[256,8]{0,1:T(8,128)S(1)} %fusion.12) | copy-start | bytes 24580
  51.6 30.1 %copy-start.7 = (f32[64,1280]{1,0:T(8,128)}, f32[64,1280]{1,0:T(8,128)S(1)}, u32[]{:S(2)}) copy-start(f32[64,1280]{1,0:T(8,128)S(1)} %get-tuple-element.62.base_ref) | copy-start | bytes 983044
  51.6 30.1 %copy-start.9 = (f32[4,16,64]{2,1,0:T(8,128)}, f32[4,16,64]{2,1,0:T(8,128)S(1)}, u32[]{:S(2)}) copy-start(f32[4,16,64]{2,1,0:T(8,128)S(1)} %get-tuple-element.66) | copy-start | bytes 49156
  51.6 30.1 %copy-start.11 = (f32[4,16,64]{2,1,0:T(8,128)}, f32[4,16,64]{2,1,0:T(8,128)S(1)}, u32[]{:S(2)}) copy-start(f32[4,16,64]{2,1,0:T(8,128)S(1)} %get-tuple-element.65) | copy-start | bytes 49156
  51.6 30.1 %copy-start.13 = (f32[4,16,64]{2,1,0:T(8,128)}, f32[4,16,64]{2,1,0:T(8,128)S(1)}, u32[]{:S(2)}) copy-start(f32[4,16,64]{2,1,0:T(8,128)S(1)} %get-tuple-element.64) | copy-start | bytes 49156
  52.6 29.1 %all-to-all-start.1 = ((bf16[8,96,256]{2,1,0:T(8,128)(2,1)}), bf16[8,96,256]{2,1,0:T(8,128)(2,1)S(1)}, u32[]{:S(2)}, u32[]{:S(2)}) async-start(bf16[8,96,256]{2,1,0:T(8,128)(2,1)} %bitcast.13), calls=%async_computation.1 | async-start | bytes 786432 | tf_op jit(solution)/shard_map/all_to_all | solution.py:381
  56.3 12.4 %collective-permute-start.3 = (bf16[64,1280]{1,0:T(8,128)(2,1)S(1)}, bf16[64,1280]{1,0:T(8,128)(2,1)S(1)}, u32[]{:S(2)}, u32[]{:S(2)}) collective-permute-start(bf16[64,1280]{1,0:T(8,128)(2,1)S(1)} %get-tuple-element.45), channel_id=1, source_target_pairs={{0,3},{1,0},{2,1},{3,2},{4,7},{5,4},{6,5},{7,6},{8,11},{9,8},{10,9... | collective-permute-start | bytes 491528 | tf_op jit(solution)/shard_map/ppermute | solution.py:377
  64.1 15.5 %collective-permute-start.4 = (bf16[64,1280]{1,0:T(8,128)(2,1)S(1)}, bf16[64,1280]{1,0:T(8,128)(2,1)S(1)}, u32[]{:S(2)}, u32[]{:S(2)}) collective-permute-start(bf16[64,1280]{1,0:T(8,128)(2,1)S(1)} %get-tuple-element.45), channel_id=1, source_target_pairs={{0,2},{1,3},{2,0},{3,1},{4,6},{5,7},{6,4},{7,5},{8,10},{9,11},{10,... | collective-permute-start | bytes 491528 | tf_op jit(solution)/shard_map/ppermute | solution.py:377
  64.6 15.1 %collective-permute-start.5 = (bf16[64,1280]{1,0:T(8,128)(2,1)S(1)}, bf16[64,1280]{1,0:T(8,128)(2,1)S(1)}, u32[]{:S(2)}, u32[]{:S(2)}) collective-permute-start(bf16[64,1280]{1,0:T(8,128)(2,1)S(1)} %get-tuple-element.45), channel_id=1, source_target_pairs={{0,1},{1,2},{2,3},{3,0},{4,5},{5,6},{6,7},{7,4},{8,9},{9,10},{10,1... | collective-permute-start | bytes 491528 | tf_op jit(solution)/shard_map/ppermute | solution.py:377
  81.7 40.6 %all-to-all-start = ((bf16[8,96,1280]{2,1,0:T(8,128)(2,1)}), bf16[8,96,1280]{2,1,0:T(8,128)(2,1)S(1)}, u32[]{:S(2)}, u32[]{:S(2)}) async-start(bf16[8,96,1280]{2,1,0:T(8,128)(2,1)} %bitcast.99), calls=%async_computation | async-start | bytes 3932160 | tf_op jit(solution)/shard_map/all_to_all | solution.py:381
  85.5 11.7 %collective-permute-start.6 = (bf16[768,256]{1,0:T(8,128)(2,1)S(1)}, bf16[768,256]{1,0:T(8,128)(2,1)S(1)}, u32[]{:S(2)}, u32[]{:S(2)}) collective-permute-start(bf16[768,256]{1,0:T(8,128)(2,1)S(1)} %bitcast.90), channel_id=1, source_target_pairs={{0,3},{1,0},{2,1},{3,2},{4,7},{5,4},{6,5},{7,6},{8,11},{9,8},{10,9... | collective-permute-start | bytes 1179656 | tf_op jit(solution)/shard_map/ppermute | solution.py:377
  85.6 36.7 %collective-permute-start.7 = (bf16[768,256]{1,0:T(8,128)(2,1)S(1)}, bf16[768,256]{1,0:T(8,128)(2,1)S(1)}, u32[]{:S(2)}, u32[]{:S(2)}) collective-permute-start(bf16[768,256]{1,0:T(8,128)(2,1)S(1)} %bitcast.91), channel_id=1, source_target_pairs={{0,2},{1,3},{2,0},{3,1},{4,6},{5,7},{6,4},{7,5},{8,10},{9,11},{10,... | collective-permute-start | bytes 1179656 | tf_op jit(solution)/shard_map/ppermute | solution.py:377
  87.3 35.0 %collective-permute-start.8 = (bf16[768,256]{1,0:T(8,128)(2,1)S(1)}, bf16[768,256]{1,0:T(8,128)(2,1)S(1)}, u32[]{:S(2)}, u32[]{:S(2)}) collective-permute-start(bf16[768,256]{1,0:T(8,128)(2,1)S(1)} %bitcast.92), channel_id=1, source_target_pairs={{0,1},{1,2},{2,3},{3,0},{4,5},{5,6},{6,7},{7,4},{8,9},{9,10},{10,1... | collective-permute-start | bytes 1179656 | tf_op jit(solution)/shard_map/ppermute | solution.py:377
  122.3 9.5 %slice-start.2 = ((s8[6635520]{0:T(1024)(128)(4,1)}), s8[4194304]{0:T(1024)(128)(4,1)S(1)}, s32[]{:S(2)}) async-start(s8[6635520]{0:T(1024)(128)(4,1)} %bitcast.104), calls=%async_computation.6 | async-start | bytes 8388608
  124.1 7.7 %slice-start.3 = ((s8[6635520]{0:T(1024)(128)(4,1)}), s8[2441216]{0:T(1024)(128)(4,1)S(1)}, s32[]{:S(2)}) async-start(s8[6635520]{0:T(1024)(128)(4,1)} %bitcast.104), calls=%async_computation.7 | async-start | bytes 4882432
  131.8 5.9 %copy-start.18 = (bf16[1440,256]{1,0:T(8,128)(2,1)S(1)}, bf16[1440,256]{1,0:T(8,128)(2,1)}, u32[]{:S(2)}) copy-start(bf16[1440,256]{1,0:T(8,128)(2,1)} %get-tuple-element.55) | copy-start | bytes 2211844
  137.7 1.6 copy-start.17
  139.3 1.6 copy-start.16
  139.4 4.0 %slice-start = ((s8[6635520]{0:T(1024)(128)(4,1)}), s8[4194304]{0:T(1024)(128)(4,1)S(1)}, s32[]{:S(2)}) async-start(s8[6635520]{0:T(1024)(128)(4,1)} %bitcast.102), calls=%async_computation.4 | async-start | bytes 8388608
  140.9 1.6 copy-start.15
  140.9 2.4 %slice-start.1 = ((s8[6635520]{0:T(1024)(128)(4,1)}), s8[2441216]{0:T(1024)(128)(4,1)S(1)}, s32[]{:S(2)}) async-start(s8[6635520]{0:T(1024)(128)(4,1)} %bitcast.102), calls=%async_computation.5 | async-start | bytes 4882432
  147.8 7.6 %copy-start.21 = (s32[256,8]{0,1:T(8,128)S(1)}, s32[256,8]{0,1:T(8,128)}, u32[]{:S(2)}) copy-start(s32[256,8]{0,1:T(8,128)} %copy-done.20) | copy-start | bytes 24580
  147.8 7.8 %copy-start.14 = (f32[4,16,64]{2,1,0:T(8,128)S(1)}, f32[4,16,64]{2,1,0:T(8,128)}, u32[]{:S(2)}) copy-start(f32[4,16,64]{2,1,0:T(8,128)} %copy-done.13) | copy-start | bytes 49156
  147.8 8.1 %copy-start.12 = (f32[4,16,64]{2,1,0:T(8,128)S(1)}, f32[4,16,64]{2,1,0:T(8,128)}, u32[]{:S(2)}) copy-start(f32[4,16,64]{2,1,0:T(8,128)} %copy-done.11) | copy-start | bytes 49156
  147.8 24.5 %copy-start.10 = (f32[4,16,64]{2,1,0:T(8,128)S(1)}, f32[4,16,64]{2,1,0:T(8,128)}, u32[]{:S(2)}) copy-start(f32[4,16,64]{2,1,0:T(8,128)} %copy-done.9) | copy-start | bytes 49156
  147.8 42.9 %copy-start.6 = (f32[4,16,64]{2,1,0:T(8,128)S(1)}, f32[4,16,64]{2,1,0:T(8,128)}, u32[]{:S(2)}) copy-start(f32[4,16,64]{2,1,0:T(8,128)} %copy-done.5) | copy-start | bytes 49156
  147.9 36.9 %all-to-all-start.2 = ((bf16[8,96,1280]{2,1,0:T(8,128)(2,1)}), bf16[8,96,1280]{2,1,0:T(8,128)(2,1)S(1)}, u32[]{:S(2)}, u32[]{:S(2)}) async-start(bf16[8,96,1280]{2,1,0:T(8,128)(2,1)} %bitcast.100), calls=%async_computation.2 | async-start | bytes 3932160 | tf_op jit(solution)/shard_map/all_to_all | solution.py:381
  151.8 20.5 %collective-permute-start.10 = (bf16[768,256]{1,0:T(8,128)(2,1)}, bf16[768,256]{1,0:T(8,128)(2,1)}, u32[]{:S(2)}, u32[]{:S(2)}) collective-permute-start(bf16[768,256]{1,0:T(8,128)(2,1)} %convolution_convert_fusion.2), channel_id=1, source_target_pairs={{0,2},{1,3},{2,0},{3,1},{4,6},{5,7},{6,4},{7,5},{8,10},{9,11},{10,... | collective-permute-start | bytes 1179656 | tf_op jit(solution)/shard_map/ppermute | solution.py:374
  153.2 29.5 %collective-permute-start.11 = (bf16[768,256]{1,0:T(8,128)(2,1)}, bf16[768,256]{1,0:T(8,128)(2,1)}, u32[]{:S(2)}, u32[]{:S(2)}) collective-permute-start(bf16[768,256]{1,0:T(8,128)(2,1)} %convolution_convert_fusion.1), channel_id=1, source_target_pairs={{0,3},{1,0},{2,1},{3,2},{4,7},{5,4},{6,5},{7,6},{8,11},{9,8},{10,9... | collective-permute-start | bytes 1179656 | tf_op jit(solution)/shard_map/ppermute | solution.py:374
  153.6 29.0 %collective-permute-start.9 = (bf16[768,256]{1,0:T(8,128)(2,1)}, bf16[768,256]{1,0:T(8,128)(2,1)}, u32[]{:S(2)}, u32[]{:S(2)}) collective-permute-start(bf16[768,256]{1,0:T(8,128)(2,1)} %convolution_convert_fusion.3), channel_id=1, source_target_pairs={{0,1},{1,2},{2,3},{3,0},{4,5},{5,6},{6,7},{7,4},{8,9},{9,10},{10,1... | collective-permute-start | bytes 1179656 | tf_op jit(solution)/shard_map/ppermute | solution.py:374
  155.5 46.7 %copy-start.3 = (f32[256,256]{1,0:T(8,128)S(1)}, f32[256,256]{1,0:T(8,128)}, u32[]{:S(2)}) copy-start(f32[256,256]{1,0:T(8,128)} %copy-done.2) | copy-start | bytes 786436
  155.7 33.0 %collective-permute-start.12 = (f32[4,16,64]{2,1,0:T(8,128)S(1)}, f32[4,16,64]{2,1,0:T(8,128)S(1)}, u32[]{:S(2)}, u32[]{:S(2)}) collective-permute-start(f32[4,16,64]{2,1,0:T(8,128)S(1)} %copy-done.14), channel_id=1, source_target_pairs={{0,1},{1,2},{2,3},{3,0},{4,5},{5,6},{6,7},{7,4},{8,9},{9,10},{10,1... | collective-permute-start | bytes 49160 | tf_op jit(solution)/shard_map/ppermute | solution.py:374
  155.9 34.9 %collective-permute-start.13 = (f32[4,16,64]{2,1,0:T(8,128)S(1)}, f32[4,16,64]{2,1,0:T(8,128)S(1)}, u32[]{:S(2)}, u32[]{:S(2)}) collective-permute-start(f32[4,16,64]{2,1,0:T(8,128)S(1)} %copy-done.12), channel_id=1, source_target_pairs={{0,2},{1,3},{2,0},{3,1},{4,6},{5,7},{6,4},{7,5},{8,10},{9,11},{10,... | collective-permute-start | bytes 49160 | tf_op jit(solution)/shard_map/ppermute | solution.py:374
  172.4 18.4 %collective-permute-start.14 = (f32[4,16,64]{2,1,0:T(8,128)S(1)}, f32[4,16,64]{2,1,0:T(8,128)S(1)}, u32[]{:S(2)}, u32[]{:S(2)}) collective-permute-start(f32[4,16,64]{2,1,0:T(8,128)S(1)} %copy-done.10), channel_id=1, source_target_pairs={{0,3},{1,0},{2,1},{3,2},{4,7},{5,4},{6,5},{7,6},{8,11},{9,8},{10,9... | collective-permute-start | bytes 49160 | tf_op jit(solution)/shard_map/ppermute | solution.py:374
  184.8 17.4 %all-to-all-start.3 = ((bf16[8,96,256]{2,1,0:T(8,128)(2,1)}), bf16[8,96,256]{2,1,0:T(8,128)(2,1)S(1)}, u32[]{:S(2)}, u32[]{:S(2)}) async-start(bf16[8,96,256]{2,1,0:T(8,128)(2,1)} %bitcast.101), calls=%async_computation.3 | async-start | bytes 786432 | tf_op jit(solution)/shard_map/all_to_all | solution.py:381
  193.8 11.2 %collective-permute-start.15 = (bf16[64,1280]{1,0:T(8,128)(2,1)}, bf16[64,1280]{1,0:T(8,128)(2,1)S(1)}, u32[]{:S(2)}, u32[]{:S(2)}) collective-permute-start(bf16[64,1280]{1,0:T(8,128)(2,1)} %get-tuple-element.68), channel_id=1, source_target_pairs={{0,1},{1,2},{2,3},{3,0},{4,5},{5,6},{6,7},{7,4},{8,9},{9,10},{10,1... | collective-permute-start | bytes 491528 | tf_op jit(solution)/shard_map/ppermute | solution.py:374
  199.9 10.8 %collective-permute-start.16 = (bf16[64,1280]{1,0:T(8,128)(2,1)}, bf16[64,1280]{1,0:T(8,128)(2,1)S(1)}, u32[]{:S(2)}, u32[]{:S(2)}) collective-permute-start(bf16[64,1280]{1,0:T(8,128)(2,1)} %get-tuple-element.69), channel_id=1, source_target_pairs={{0,2},{1,3},{2,0},{3,1},{4,6},{5,7},{6,4},{7,5},{8,10},{9,11},{10,... | collective-permute-start | bytes 491528 | tf_op jit(solution)/shard_map/ppermute | solution.py:374
  199.9 11.8 %collective-permute-start.17 = (bf16[64,1280]{1,0:T(8,128)(2,1)S(1)}, bf16[64,1280]{1,0:T(8,128)(2,1)S(1)}, u32[]{:S(2)}, u32[]{:S(2)}) collective-permute-start(bf16[64,1280]{1,0:T(8,128)(2,1)S(1)} %get-tuple-element.70), channel_id=1, source_target_pairs={{0,3},{1,0},{2,1},{3,2},{4,7},{5,4},{6,5},{7,6},{8,11},{9,8},{10,9... | collective-permute-start | bytes 491528 | tf_op jit(solution)/shard_map/ppermute | solution.py:374
  202.9 16.7 %collective-permute-start.18 = (bf16[64,256]{1,0:T(8,128)(2,1)S(1)}, bf16[64,256]{1,0:T(8,128)(2,1)S(1)}, u32[]{:S(2)}, u32[]{:S(2)}) collective-permute-start(bf16[64,256]{1,0:T(8,128)(2,1)S(1)} %get-tuple-element.73), channel_id=1, source_target_pairs={{0,3},{1,0},{2,1},{3,2},{4,7},{5,4},{6,5},{7,6},{8,11},{9,8},{10,9... | collective-permute-start | bytes 98312 | tf_op jit(solution)/shard_map/ppermute | solution.py:374
  211.7 7.9 %collective-permute-start.19 = (bf16[64,256]{1,0:T(8,128)(2,1)S(1)}, bf16[64,256]{1,0:T(8,128)(2,1)S(1)}, u32[]{:S(2)}, u32[]{:S(2)}) collective-permute-start(bf16[64,256]{1,0:T(8,128)(2,1)S(1)} %get-tuple-element.74), channel_id=1, source_target_pairs={{0,2},{1,3},{2,0},{3,1},{4,6},{5,7},{6,4},{7,5},{8,10},{9,11},{10,... | collective-permute-start | bytes 98312 | tf_op jit(solution)/shard_map/ppermute | solution.py:374
  213.8 7.4 %collective-permute-start.20 = (bf16[64,256]{1,0:T(8,128)(2,1)S(1)}, bf16[64,256]{1,0:T(8,128)(2,1)S(1)}, u32[]{:S(2)}, u32[]{:S(2)}) collective-permute-start(bf16[64,256]{1,0:T(8,128)(2,1)S(1)} %get-tuple-element.75), channel_id=1, source_target_pairs={{0,1},{1,2},{2,3},{3,0},{4,5},{5,6},{6,7},{7,4},{8,9},{9,10},{10,1... | collective-permute-start | bytes 98312 | tf_op jit(solution)/shard_map/ppermute | solution.py:374
  (5 other events, 4.4 us)

commit v2 on v1

--- a/solution.py
+++ b/solution.py
@@ -12,10 +12,12 @@
 TOP = 2
 CAP = 96
 PACK = 16
+KEYS = 256
 SLICE = 256
 MASKED = -1e30
 EPSILON = 1e-05
 NT = (((1,), (1,)), ((), ()))
+AHEAD = pl.CostEstimate(flops=1 << 37, bytes_accessed=1 << 20, transcendentals=0)
 
 
 def normalize(inputs, scale_gain):
@@ -36,41 +38,36 @@
     )
 
 
-def scores_of(first, count, length, shift, tokens, q, kc, kf):
-    cache_len = kc.shape[1]
-    slots = lax.broadcasted_iota(jnp.int32, (PACK, cache_len), 1)
-    top_row = lax.broadcasted_iota(jnp.int32, (PACK, cache_len), 0) == 0
-    bias = jnp.where(top_row & (slots >= length), MASKED, 0.0).astype(jnp.bfloat16)
-    s_c = jnp.dot(q, jnp.concatenate([kc, bias], axis=0), preferred_element_type=jnp.float32)
-    pad = jnp.zeros((PACK, kf.shape[1]), kf.dtype)
-    s_f = jnp.dot(q, jnp.concatenate([kf, pad], axis=0), preferred_element_type=jnp.float32)
-    row = lax.rem(lax.broadcasted_iota(jnp.int32, (count, 1), 0) + (first + shift), tokens)
-    col = lax.rem(lax.broadcasted_iota(jnp.int32, (1, tokens), 1) + shift, tokens)
-    return s_c, jnp.where(col <= row, s_f, MASKED)
-
-
-def mixture(scores, vc, vf):
-    s_c, s_f = scores
-    top = jnp.maximum(jnp.max(s_c, axis=1, keepdims=True), jnp.max(s_f, axis=1, keepdims=True))
-    p_c = jnp.exp(s_c - top)
-    p_f = jnp.exp(s_f - top)
-    totals = jnp.sum(p_c, axis=1, keepdims=True) + jnp.sum(p_f, axis=1, keepdims=True)
-    mixed = lax.dot_general(p_c.astype(jnp.bfloat16), vc, NT, preferred_element_type=jnp.float32)
-    mixed = mixed + lax.dot_general(
-        p_f.astype(jnp.bfloat16), vf, NT, preferred_element_type=jnp.float32
-    )
-    return mixed / totals
-
-
-def attend_heads(heads, make_scores, make_mixture, attended):
-    mixed = []
-    ahead = make_scores(0)
+def lane_halves(chunk, join):
+    half = chunk.shape[1] // 2
+    return join(chunk[:, :half], chunk[:, half:])
+
+
+def attend_heads(heads, chunks, score, value):
+    def row_top(scores):
+        top = lane_halves(scores[0], jnp.maximum)
+        for chunk in scores[1:]:
+            top = jnp.maximum(top, lane_halves(chunk, jnp.maximum))
+        return jnp.max(top, axis=1, keepdims=True)
+
+    outputs = []
+    ahead = [score(0, c) for c in range(chunks)]
     for g in range(heads):
-        now = ahead
-        if g + 1 < heads:
-            ahead = make_scores(g + 1)
-        mixed.append(make_mixture(g, now))
-    attended[pl.program_id(0)] = jnp.concatenate(mixed, axis=1).astype(jnp.bfloat16)
+        now, ahead = ahead, []
+        top = row_top(now)
+        totals = mixed = None
+        for c in range(chunks):
+            if g + 1 < heads:
+                ahead.append(score(g + 1, c))
+            probs = jnp.exp(now[c] - top)
+            part = lane_halves(probs, jnp.add)
+            totals = part if totals is None else totals + part
+            part = lax.dot_general(
+                probs.astype(jnp.bfloat16), value(g, c), NT, preferred_element_type=jnp.float32
+            )
+            mixed = part if mixed is None else mixed + part
+        outputs.append(mixed / jnp.sum(totals, axis=1, keepdims=True))
+    return outputs
 
 
 def widened(q):
@@ -119,17 +116,38 @@
     projected = jnp.dot(weights, normed[...], preferred_element_type=jnp.float32)
     cosine, sine_part = cos_ref[...], sin_ref[...]
 
-    def make_scores(g):
+    cache_len = kc_ref.shape[1]
+    cached = cache_len // KEYS
+    pad = jnp.zeros((PACK, tokens), jnp.bfloat16)
+    queries, keys, values = [], [], []
+    for g in range(heads):
         q = rotate_rows(projected[head_slice(g)], cosine, sine_part).astype(jnp.bfloat16)
-        q = widened(q.astype(jnp.float32) * HEAD**-0.5)
+        queries.append(widened(q.astype(jnp.float32) * HEAD**-0.5))
         kf = rotate_rows(projected[head_slice(heads + g)], cosine, sine_part).astype(jnp.bfloat16)
-        return scores_of(0, tokens, length, shift, tokens, q, kc_ref[head_slice(g), :], kf)
-
-    def make_mixture(g, scores):
-        vf = projected[head_slice(2 * heads + g)].astype(jnp.bfloat16)
-        return mixture(scores, vc_ref[head_slice(g), :], vf)
-
-    attend_heads(heads, make_scores, make_mixture, attended)
+        keys.append(jnp.concatenate([kf, pad], axis=0))
+        values.append(projected[head_slice(2 * heads + g)].astype(jnp.bfloat16))
+    slots = lax.broadcasted_iota(jnp.int32, (PACK, KEYS), 1)
+    top_row = lax.broadcasted_iota(jnp.int32, (PACK, KEYS), 0) == 0
+    row = lax.rem(lax.broadcasted_iota(jnp.int32, (tokens, 1), 0) + shift, tokens)
+    col = lax.rem(lax.broadcasted_iota(jnp.int32, (1, tokens), 1) + shift, tokens)
+
+    def chunk_of(c):
+        return slice(c * KEYS, (c + 1) * KEYS)
+
+    def score(g, c):
+        if c == cached:
+            scores = jnp.dot(queries[g], keys[g], preferred_element_type=jnp.float32)
+            return jnp.where(col <= row, scores, MASKED)
+        dead = top_row & (slots + c * KEYS >= length)
+        bias = jnp.where(dead, MASKED, 0.0).astype(jnp.bfloat16)
+        kc = jnp.concatenate([kc_ref[head_slice(g), chunk_of(c)], bias], axis=0)
+        return jnp.dot(queries[g], kc, preferred_element_type=jnp.float32)
+
+    def value(g, c):
+        return values[g] if c == cached else vc_ref[head_slice(g), chunk_of(c)]
+
+    outputs = attend_heads(heads, cached + 1, score, value)
+    attended[pl.program_id(0)] = jnp.concatenate(outputs, axis=1).astype(jnp.bfloat16)
 
     @pl.when(pl.program_id(0) == pl.num_programs(0) - 1)
     def _():
@@ -158,8 +176,8 @@
 def merge_kernel(share, pieces, scalars, *refs):
     piece_refs = refs[:pieces]
     hidden_ref, gain_ref, router_ref = refs[pieces : pieces + 3]
-    first_ref, slice_ref, first_raw_ref, slice_raw_ref, *term_refs = refs[pieces + 3 :]
-    tp = len(term_refs)
+    first_ref, slice_ref, slice_raw_ref, *message_refs = refs[pieces + 3 :]
+    tp = len(message_refs)
     me = scalars[0]
     first = first_ref.shape[1]
     exact = functools.partial(
@@ -171,9 +189,20 @@
 
     def terms_of(rows, lanes):
         weights = router_ref[:, lanes].astype(jnp.float32) * gain_ref[:, lanes]
-        return jnp.concatenate(
-            [exact(weights, rows), exact(jnp.ones_like(weights), rows * rows)], axis=0
-        )
+        return exact(weights, rows), exact(jnp.ones_like(weights), rows * rows)
+
+    def in_parts(logits, squares):
+        row = lax.broadcasted_iota(jnp.int32, squares.shape, 0)
+        last = jnp.zeros_like(squares)
+        parts = []
+        for p in range(3):
+            part = logits.astype(jnp.bfloat16).astype(jnp.float32)
+            logits = logits - part
+            parts.append(part)
+            part = squares.astype(jnp.bfloat16).astype(jnp.float32)
+            squares = squares - part
+            last = jnp.where(row == p, part, last)
+        return jnp.concatenate([*parts, last], axis=0)
 
     def block_start(j):
         return pl.multiple_of(lax.rem(me + j, tp) * share, share)
@@ -183,7 +212,6 @@
         total = total + ref[...].astype(jnp.float32)
     own = hidden_ref[pl.ds(block_start(0), share), :first].astype(jnp.float32) + total[:, :first]
     first_ref[...] = own
-    first_raw_ref[...] = own.astype(jnp.bfloat16)
     lanes = pl.ds(pl.multiple_of(first + me * SLICE, SLICE), SLICE)
     terms = []
     for j in range(tp):
@@ -192,10 +220,12 @@
         slice_ref[j * share : (j + 1) * share, :] = rows
         slice_raw_ref[j * share : (j + 1) * share, :] = rows.astype(jnp.bfloat16)
         terms.append(terms_of(rows, lanes))
-    terms[0] = terms[0] + terms_of(own, slice(0, first))
-    for k in range(tp):
-        for j in range(tp):
-            term_refs[k][j] = terms[(j + k) % tp]
+    terms[0] = [a + b for a, b in zip(terms[0], terms_of(own, slice(0, first)))]
+    terms = [in_parts(*t) for t in terms]
+    for k, message_ref in enumerate(message_refs):
+        message_ref[:, :first] = own.astype(jnp.bfloat16)
+        told = jnp.concatenate([terms[(j - k) % tp] for j in range(tp)], axis=0)
+        message_ref[:, first:] = told.T.astype(jnp.bfloat16)
 
 
 def merge(me_tp, pieces, hidden_in, gain, router_t):
@@ -203,8 +233,7 @@
     tp = len(pieces)
     tokens = hidden_in.shape[0]
     first = width - tp * SLICE
-    experts = router_t.shape[0]
-    terms = jax.ShapeDtypeStruct((tp, 2 * experts, share), jnp.float32)
+    length = first + tp * 4 * router_t.shape[0]
     return pl.pallas_call(
         functools.partial(merge_kernel, share, tp),
         grid_spec=pltpu.PrefetchScalarGridSpec(
@@ -215,17 +244,16 @@
             out_specs=[
                 pl.BlockSpec((share, first), lambda i, s: (0, 0)),
                 pl.BlockSpec((tokens, SLICE), lambda i, s: (0, 0)),
+                pl.BlockSpec((tokens, SLICE), lambda i, s: (0, 0)),
             ]
-            * 2
-            + [pl.BlockSpec(terms.shape, lambda i, s: (0, 0, 0))] * tp,
+            + [pl.BlockSpec((share, length), lambda i, s: (0, 0))] * tp,
         ),
         out_shape=[
             jax.ShapeDtypeStruct((share, first), jnp.float32),
             jax.ShapeDtypeStruct((tokens, SLICE), jnp.float32),
-            jax.ShapeDtypeStruct((share, first), jnp.bfloat16),
             jax.ShapeDtypeStruct((tokens, SLICE), jnp.bfloat16),
         ]
-        + [terms] * tp,
+        + [jax.ShapeDtypeStruct((share, length), jnp.bfloat16)] * tp,
         compiler_params=pltpu.CompilerParams(vmem_limit_bytes=32 * 1024 * 1024),
         cost_estimate=pl.CostEstimate(
             flops=8 * tp * share * width,
@@ -235,62 +263,55 @@
     )(me_tp.reshape(1), *pieces, hidden_in, gain, router_t)
 
 
-def assemble_kernel(slices, scalars, first_ref, *refs):
-    slice_refs = refs[:slices]
-    gain_ref, out_ref = refs[slices:]
+def assemble_kernel(first_ref, rest_ref, gain_ref, out_ref):
     first = first_ref.shape[1]
     width = out_ref.shape[1]
     rows = first_ref[...].astype(jnp.float32)
-    parts = [ref[...].astype(jnp.float32) for ref in slice_refs]
+    rest = rest_ref[...].astype(jnp.float32)
     squares = jnp.sum(rows * rows, axis=1, keepdims=True)
-    for part in parts:
-        squares = squares + jnp.sum(part * part, axis=1, keepdims=True)
+    squares = squares + jnp.sum(rest * rest, axis=1, keepdims=True)
     scale = lax.rsqrt(squares / width + EPSILON)
     out_ref[:, :first] = (rows * scale * gain_ref[:, :first]).astype(jnp.bfloat16)
-    for k, part in enumerate(parts):
-        place = lax.rem(scalars[0] + k, slices) * SLICE + first
-        lanes = pl.ds(pl.multiple_of(place, SLICE), SLICE)
-        out_ref[:, lanes] = (part * scale * gain_ref[:, lanes]).astype(jnp.bfloat16)
-
-
-def assemble(me_tp, first_rows, slices, gain):
+    out_ref[:, first:] = (rest * scale * gain_ref[:, first:]).astype(jnp.bfloat16)
+
+
+def assemble(first_rows, rest, gain):
     rows, first = first_rows.shape
-    width = first + SLICE * len(slices)
+    width = first + rest.shape[1]
     tile = 2 * CAP
 
     def tiles(n):
-        return pl.BlockSpec((tile, n), lambda i, s: (i, 0))
+        return pl.BlockSpec((tile, n), lambda i: (i, 0))
 
     return pl.pallas_call(
-        functools.partial(assemble_kernel, len(slices)),
-        grid_spec=pltpu.PrefetchScalarGridSpec(
-            num_scalar_prefetch=1,
-            grid=(rows // tile,),
-            in_specs=[tiles(first)]
-            + [tiles(SLICE)] * len(slices)
-            + [pl.BlockSpec((1, width), lambda i, s: (0, 0))],
-            out_specs=tiles(width),
-        ),
+        assemble_kernel,
+        grid=(rows // tile,),
+        in_specs=[tiles(first), tiles(width - first), pl.BlockSpec((1, width), lambda i: (0, 0))],
+        out_specs=tiles(width),
         out_shape=jax.ShapeDtypeStruct((rows, width), jnp.bfloat16),
         compiler_params=pltpu.CompilerParams(vmem_limit_bytes=16 * 1024 * 1024),
         cost_estimate=pl.CostEstimate(
             flops=8 * rows * width, bytes_accessed=4 * rows * width, transcendentals=rows
         ),
-    )(me_tp.reshape(1), first_rows, *slices, gain)
+    )(first_rows, rest, gain)
 
 
 def combine_kernel(width, copies, terms, rows_ref, routes_ref, places_ref, base_ref, *refs):
     term_refs, out_refs = refs[:terms], refs[terms:]
     tp = len(out_refs)
-    total = term_refs[0][...]
+    total = term_refs[0][...].astype(jnp.float32)
     for ref in term_refs[1:]:
-        total = total + ref[...]
-    experts = total.shape[1] // 2
-    total = jnp.concatenate([total[j] for j in range(tp)], axis=1).T
-    tokens = total.shape[0]
-    share = tokens // tp
-    scale = lax.rsqrt(total[:, experts : experts + 1] / width + EPSILON)
-    logits = total[:, :experts] * scale
+        total = total + ref[...].astype(jnp.float32)
+    share = total.shape[0]
+    tokens = tp * share
+    experts = total.shape[1] // (4 * tp)
+    logits = []
+    for j in range(tp):
+        start = 4 * experts * j
+        group = [total[:, start + p * experts : start + (p + 1) * experts] for p in range(4)]
+        squares = group[3][:, 0:1] + group[3][:, 1:2] + group[3][:, 2:3]
+        logits.append((group[0] + group[1] + group[2]) * lax.rsqrt(squares / width + EPSILON))
+    logits = jnp.concatenate(logits, axis=0)
     ids = lax.broadcasted_iota(jnp.int32, (tokens, experts), 1)
     slots = lax.broadcasted_iota(jnp.int32, (tokens, rows_ref.shape[0]), 1)
     rows = rows_ref[...]
@@ -327,11 +348,13 @@
     def full(array):
         return pl.BlockSpec(array.shape, lambda i: (0,) * array.ndim)
 
+    told = terms[0].shape[1] - width + len(kinds) * SLICE
+    term = pl.BlockSpec((share, told), lambda i: (0, terms[0].shape[1] // told - 1))
     operands = [rows, routes, places, base, *terms]
     return pl.pallas_call(
         functools.partial(combine_kernel, width, copies, len(terms)),
         grid=(1,),
-        in_specs=[full(a) for a in operands],
+        in_specs=[full(a) for a in operands[:4]] + [term] * len(terms),
         out_specs=[pl.BlockSpec((share, columns), lambda i: (0, 0))] * len(kinds),
         out_shape=[jax.ShapeDtypeStruct((share, columns), kind) for kind in kinds],
         compiler_params=pltpu.CompilerParams(vmem_limit_bytes=40 * 1024 * 1024),
@@ -341,6 +364,79 @@
             transcendentals=4 * tokens,
         ),
     )(*operands)
+
+
+def place_kernel(scalars, *refs):
+    piece_refs, out_ref = refs[:-1], refs[-1]
+    tp = len(piece_refs)
+    for k, ref in enumerate(piece_refs):
+        lanes = pl.ds(pl.multiple_of(lax.rem(scalars[0] + k, tp) * SLICE, SLICE), SLICE)
+        out_ref[:, lanes] = ref[...]
+
+
+def place(first, slices, tile, cost=None):
+    rows = slices[0].shape[0]
+    width = SLICE * len(slices)
+    return pl.pallas_call(
+        place_kernel,
+        grid_spec=pltpu.PrefetchScalarGridSpec(
+            num_scalar_prefetch=1,
+            grid=(rows // tile,),
+            in_specs=[pl.BlockSpec((tile, SLICE), lambda i, s: (i, 0))] * len(slices),
+            out_specs=pl.BlockSpec((tile, width), lambda i, s: (i, 0)),
+        ),
+        out_shape=jax.ShapeDtypeStruct((rows, width), slices[0].dtype),
+        cost_estimate=cost,
+    )(first.reshape(1), *slices)
+
+
+def sum_kernel(*refs):
+    *piece_refs, out_ref = refs
+    total = piece_refs[0][...].astype(jnp.float32)
+    for ref in piece_refs[1:]:
+        total = total + ref[...].astype(jnp.float32)
+    out_ref[...] = total.astype(out_ref.dtype)
+
+
+def sum_of(pieces, tile):
+    rows, columns = pieces[0].shape
+    block = pl.BlockSpec((tile, columns), lambda i: (i, 0))
+    return pl.pallas_call(
+        sum_kernel,
+        grid=(rows // tile,),
+        in_specs=[block] * len(pieces),
+        out_specs=block,
+        out_shape=jax.ShapeDtypeStruct((rows, columns), jnp.bfloat16),
+        cost_estimate=AHEAD,
+    )(*pieces)
+
+
+def same_kernel(*_):
+    pass
+
+
+def after(value, *arrivals):
+    return pl.pallas_call(
+        same_kernel,
+        in_specs=[pl.BlockSpec(memory_space=pl.ANY)] * (1 + len(arrivals)),
+        out_specs=pl.BlockSpec(memory_space=pl.ANY),
+        out_shape=jax.ShapeDtypeStruct(value.shape, value.dtype),
+        input_output_aliases={0: 0},
+    )(value, *arrivals)
+
+
+def joined_kernel(first_ref, rest_ref, out_ref):
+    first = first_ref.shape[1]
+    out_ref[:, :first] = first_ref[...]
+    out_ref[:, first:] = rest_ref[...]
+
+
+def joined(first, rest):
+    rows = first.shape[0]
+    return pl.pallas_call(
+        joined_kernel,
+        out_shape=jax.ShapeDtypeStruct((rows, first.shape[1] + rest.shape[1]), first.dtype),
+    )(first, rest)
 
 
 def per_device(
@@ -473,48 +569,47 @@
     arrived = [to_block(piece, k + 1) for k, piece in enumerate(sent)]
 
     gain = ffn_norm.reshape(1, model_width)
-    first_residual, slice_residual, first_raw, slice_raw, *terms = merge(
+    first_residual, slice_residual, slice_raw, *messages = merge(
         me_tp, [own_partial, *arrived], hidden_in, gain, jnp.swapaxes(router, 0, 1)
     )
 
     slice_downs = lax.optimization_barrier(
-        [
-            lax.dynamic_slice_in_dim(
-                expert_down[0], first_width + (me_tp + k) % tp * SLICE, SLICE, 1
-            )
-            for k in range(tp)
-        ]
-    )
-
-    gathered = jnp.concatenate(
-        [first_raw] + [from_block(first_raw, k) for k in range(1, tp)], axis=0
-    )
+        jnp.stack(
+            [
+                lax.dynamic_slice_in_dim(
+                    expert_down[0], first_width + (me_tp + k) % tp * SLICE, SLICE, 1
+                )
+                for k in range(tp)
+            ]
+        )
+    )
+
+    messages = [messages[0]] + [from_block(messages[k], k) for k in range(1, tp)]
     slice_rows = to_experts(slice_raw)
 
+    gathered = jnp.concatenate([m[:, :first_width] for m in messages], axis=0)
+    gathered, slice_rows = lax.optimization_barrier((gathered, slice_rows))
+    slices = [slice_rows] + [from_block(slice_rows, k) for k in range(1, tp)]
     first_rows = to_experts(gathered)
-    slices = [slice_rows] + [from_block(slice_rows, k) for k in range(1, tp)]
-    token_rows = assemble(me_tp, first_rows, slices, gain)
-
-    token_rows, *terms = lax.optimization_barrier((token_rows, *terms))
-    terms = [terms[0]] + [to_block(terms[k], k) for k in range(1, tp)]
+    token_rows = assemble(first_rows, place(me_tp, slices, 2 * CAP, AHEAD), gain)
 
     gate_proj = jnp.dot(token_rows, expert_gate[0], preferred_element_type=jnp.float32)
     up_proj = jnp.dot(token_rows, expert_up[0], preferred_element_type=jnp.float32)
     activation = (jax.nn.silu(gate_proj) * up_proj).astype(jnp.bfloat16)
     activation = lax.optimization_barrier(activation)
 
-    def down(rows, weights):
-        return jnp.dot(rows, weights, preferred_element_type=jnp.float32).astype(jnp.bfloat16)
-
-    slice_terms = lax.optimization_barrier([down(activation, w) for w in slice_downs])
-    coming = [to_block(slice_terms[k], k) for k in range(1, tp)]
-    activation, _ = lax.optimization_barrier((activation, slice_terms[tp - 1]))
-    first_back = exchanged(down(activation, expert_down[0, :, :first_width]))
-    slice_sum = slice_terms[0].astype(jnp.float32)
-    for term in coming:
-        slice_sum = slice_sum + term.astype(jnp.float32)
-    slice_sum, first_back = lax.optimization_barrier((slice_sum.astype(jnp.bfloat16), first_back))
-
+    first_terms = jnp.dot(
+        activation, expert_down[0, :, :first_width], preferred_element_type=jnp.float32
+    )
+    first_back = exchanged(first_terms.astype(jnp.bfloat16))
+    slice_terms = jnp.einsum(
+        "rh,khs->krs", activation, slice_downs, preferred_element_type=jnp.float32
+    ).astype(jnp.bfloat16)
+    slice_sum = sum_of(
+        [slice_terms[0]] + [to_block(slice_terms[k], k) for k in range(1, tp)], 2 * CAP
+    )
+
+    slice_back = exchanged(after(slice_sum, first_back))
     kinds = [jnp.bfloat16] * tp
     first_out, *first_shares = combine(
         model_width,
@@ -523,27 +618,18 @@
         rolled,
         places,
         first_residual,
-        terms,
+        messages,
         [jnp.float32, *kinds[1:]],
     )
-    for k, piece in enumerate(first_shares):
-        first_out = first_out + to_block(piece, k + 1).astype(jnp.float32)
+    first_out = sum_of(
+        [first_out] + [to_block(piece, k + 1) for k, piece in enumerate(first_shares)], share
+    )
     slice_outs = combine(
-        model_width,
-        copies,
-        exchanged(slice_sum),
-        rolled,
-        places,
-        slice_residual,
-        terms,
-        kinds,
+        model_width, copies, slice_back, rolled, places, slice_residual, messages, kinds
     )
     slice_outs = [slice_outs[0]] + [to_block(slice_outs[k], k) for k in range(1, tp)]
-    slice_outs = jnp.stack(slice_outs[::-1] * 2)
-    slice_outs = lax.dynamic_slice_in_dim(slice_outs, (2 * tp - 1 - me_tp) % tp, tp, 0)
-    return jnp.concatenate(
-        [first_out.astype(jnp.bfloat16)] + [slice_outs[j] for j in range(tp)], axis=1
-    )
+    slice_outs = [slice_outs[0], *slice_outs[:0:-1]]
+    return joined(first_out, place(me_tp, slice_outs, share))
 
 
 def solution(mesh):

time: 223 us -> 206 us (0.924)
  starting transfers between devices: 67.5 us -> 51.4 us
  waiting for transfers between devices: 88.1 us -> 75.2 us
  Pallas kernels: 27.1 us -> 38.4 us
  local copies, waits for them, and re-layouts: 7.93 us -> 11.1 us
  matrix products: 26.7 us -> 23.9 us
    ppermute x15 -> x12, starting transfers between devices: 40 us -> 24.9 us  [to_block(): return lax.ppermute(array, 'tp', [(i, (i + k) % tp) for i in range(tp)])]
    pallas_call x1 -> x7, Pallas kernels: 1.84 us -> 13.7 us  [the longest x2 5.39 us: sum_of(): pl.pallas_call(sum_kernel, grid=(rows // tile,), in_specs=[block] * len(p...]
    ppermute x15 -> x12, waiting for transfers between devices: 43.6 us -> 32 us  [to_block(): return lax.ppermute(array, 'tp', [(i, (i + k) % tp) for i in range(tp)])]
    ppermute x6, waiting for transfers between devices: 44.5 us -> 36.2 us  [from_block(): return lax.ppermute(array, 'tp', [(i, (i - k) % tp) for i in range(tp)])]
    all_to_all x4, waiting for transfers between devices: 0.01 us -> 6.95 us  [exchanged(): lax.all_to_all(blocks, 'req', split_axis=0, concat_axis=0, tiled=True)]
    unnamed x67 -> x69, local copies, waits for them, and re-layouts: 3.65 us -> 7.15 us
    dot_general x5 -> x2, matrix products: 10 us -> 7.19 us  [the longest x1 4.48 us: per_device(): jnp.dot(activation, expert_down[0, :, :first_width], preferred_element_ty...]
  transfers between devices with their start and end apart: 25 -> 22, of which waited for: 12 -> 11; matrix products, arithmetic and copies ran while one was open for 4% -> 7% of each run, Pallas kernels for 1% -> 5%
where the time goes in v2:
time: 206 us; the launch traced here: 205 us
  waiting for transfers between devices  75.2 us (37%)
  starting transfers between devices  51.4 us (25%)
  Pallas kernels  38.4 us (19%)
  matrix products  23.9 us (12%)
  local copies, waits for them, and re-layouts  11.1 us (5%)
  other arithmetic  3.8 us (2%)
    ppermute x6, waiting for transfers between devices, from_block(): return lax.ppermute(array, 'tp', [(i, (i - k) % tp) for i in range(tp)])  36.2 us
    ppermute x12, waiting for transfers between devices, to_block(): return lax.ppermute(array, 'tp', [(i, (i + k) % tp) for i in range(tp)])  32 us
    ppermute x12, starting transfers between devices, to_block(): return lax.ppermute(array, 'tp', [(i, (i + k) % tp) for i in range(tp)])  24.9 us
    pallas_call x1, Pallas kernels, per_device(): pl.pallas_call(functools.partial(attention_kernel, share), grid_spec=pltp...  20.9 us
    all_to_all x4, starting transfers between devices, exchanged(): lax.all_to_all(blocks, 'req', split_axis=0, concat_axis=0, tiled=True)  15.2 us
    ppermute x6, starting transfers between devices, from_block(): return lax.ppermute(array, 'tp', [(i, (i - k) % tp) for i in range(tp)])  11.3 us
    dot_general x1, matrix products, per_device(): jnp.dot(token_rows, expert_gate[0], preferred_element_type=jnp.float32)  7.65 us
    unnamed x69, local copies, waits for them, and re-layouts  7.15 us
  transfers between devices with their start and end apart: 22, of which 11 were waited for; matrix products, arithmetic and copies ran while one was open for 7% of the time, Pallas kernels for 5%

profile of v2, /device:TPU:0, one launch (start us, length us, event | category | flops | bytes accessed | tf_op | source)
XLA Modules:
  0.0 204.9 jit_solution(5861955878799682962)
XLA Ops:
  1.3 0.8 multiply_sine_fusion
  2.1 20.9 %shard_map.127 = (bf16[64,2304]{1,0:T(8,128)(2,1)}, bf16[64,2304]{1,0:T(8,128)(2,1)}, bf16[64,2304]{1,0:T(8,128)(2,1)}, bf16[64,2304]{1,0:T(8,128)(2,1)}) custom-call(s32[2]{0:T(128)} %pad_add_fusion.scalars, bf16[256,2304]{1,0:T(8,128)(2,1)} %refs_4_.1, f32[2304]{0:T(1024)} %gain_ref.1, bf16[3,576,2304]{2,1,0:T(8,128)(2,1)} %bitcast.68, ...), custom_call_target="tpu_custom_call" | custom-call | flops 4076863488 | bytes 15335424 | tf_op jit(solution)/shard_map/pallas_call | solution.py:529
  23.0 3.0 %collective-permute-start = (bf16[64,2304]{1,0:T(8,128)(2,1)}, bf16[64,2304]{1,0:T(8,128)(2,1)S(1)}, u32[]{:S(2)}, u32[]{:S(2)}) collective-permute-start(bf16[64,2304]{1,0:T(8,128)(2,1)} %get-tuple-element.27), channel_id=1, source_target_pairs={{0,1},{1,2},{2,3},{3,0},{4,5},{5,6},{6,7},{7,4},{8,9},{9,10},{10,1... | collective-permute-start | bytes 884744 | tf_op jit(solution)/shard_map/ppermute | solution.py:470
  26.0 2.6 %collective-permute-start.1 = (bf16[64,2304]{1,0:T(8,128)(2,1)}, bf16[64,2304]{1,0:T(8,128)(2,1)S(1)}, u32[]{:S(2)}, u32[]{:S(2)}) collective-permute-start(bf16[64,2304]{1,0:T(8,128)(2,1)} %get-tuple-element.28), channel_id=1, source_target_pairs={{0,2},{1,3},{2,0},{3,1},{4,6},{5,7},{6,4},{7,5},{8,10},{9,11},{10,... | collective-permute-start | bytes 884744 | tf_op jit(solution)/shard_map/ppermute | solution.py:470
  28.6 1.4 collective-permute-start.2
  30.1 2.0 constant_dynamic-slice_fusion.3
  32.1 1.8 pad_maximum_fusion
  35.3 1.0 collective-permute-done.refs_1_
  36.3 11.8 %collective-permute-done.1.refs_2_ = bf16[64,2304]{1,0:T(8,128)(2,1)S(1)} collective-permute-done((bf16[64,2304]{1,0:T(8,128)(2,1)}, bf16[64,2304]{1,0:T(8,128)(2,1)S(1)}, u32[]{:S(2)}, u32[]{:S(2)}) %collective-permute-start.1) | collective-permute-done | bytes 294944 | tf_op jit(solution)/shard_map/ppermute | solution.py:470
  48.1 2.0 shard_map.128
  50.1 7.8 %collective-permute-start.3 = (bf16[64,1408]{1,0:T(8,128)(2,1)}, bf16[64,1408]{1,0:T(8,128)(2,1)S(1)}, u32[]{:S(2)}, u32[]{:S(2)}) collective-permute-start(bf16[64,1408]{1,0:T(8,128)(2,1)} %get-tuple-element.31), channel_id=1, source_target_pairs={{0,3},{1,0},{2,1},{3,2},{4,7},{5,4},{6,5},{7,6},{8,11},{9,8},{10,9... | collective-permute-start | bytes 540680 | tf_op jit(solution)/shard_map/ppermute | solution.py:473
  58.4 1.0 convolution_convert_fusion.1
  59.5 4.2 %all-to-all-start = ((bf16[8,96,256]{2,1,0:T(8,128)(2,1)}), bf16[8,96,256]{2,1,0:T(8,128)(2,1)}, u32[]{:S(2)}, u32[]{:S(2)}) async-start(bf16[8,96,256]{2,1,0:T(8,128)(2,1)} %bitcast.11), calls=%async_computation | async-start | bytes 786432 | tf_op jit(solution)/shard_map/all_to_all | solution.py:477
  63.8 10.7 %collective-permute-done.4.refs_2_ = bf16[64,1408]{1,0:T(8,128)(2,1)S(1)} collective-permute-done((bf16[64,1408]{1,0:T(8,128)(2,1)}, bf16[64,1408]{1,0:T(8,128)(2,1)S(1)}, u32[]{:S(2)}, u32[]{:S(2)}) %collective-permute-start.4) | collective-permute-done | bytes 180256 | tf_op jit(solution)/shard_map/ppermute | solution.py:473
  74.7 1.1 collective-permute-start.6
  76.4 1.1 collective-permute-start.8
  78.4 2.0 convolution_convert_fusion
  80.4 3.8 %all-to-all-start.1 = ((bf16[8,96,1280]{2,1,0:T(8,128)(2,1)}), bf16[8,96,1280]{2,1,0:T(8,128)(2,1)S(1)}, u32[]{:S(2)}, u32[]{:S(2)}) async-start(bf16[8,96,1280]{2,1,0:T(8,128)(2,1)} %bitcast.69), calls=%async_computation.1 | async-start | bytes 3932160 | tf_op jit(solution)/shard_map/all_to_all | solution.py:477
  84.2 2.6 %collective-permute-done.6.refs_1_ = bf16[768,256]{1,0:T(8,128)(2,1)S(1)} collective-permute-done((bf16[768,256]{1,0:T(8,128)(2,1)}, bf16[768,256]{1,0:T(8,128)(2,1)S(1)}, u32[]{:S(2)}, u32[]{:S(2)}) %collective-permute-start.6) | collective-permute-done | bytes 393248 | tf_op jit(solution)/shard_map/ppermute | solution.py:473
  86.8 23.0 %collective-permute-done.7.refs_2_ = bf16[768,256]{1,0:T(8,128)(2,1)} collective-permute-done((bf16[768,256]{1,0:T(8,128)(2,1)}, bf16[768,256]{1,0:T(8,128)(2,1)}, u32[]{:S(2)}, u32[]{:S(2)}) %collective-permute-start.7) | collective-permute-done | bytes 393248 | tf_op jit(solution)/shard_map/ppermute | solution.py:473
  109.7 3.7 %shard_map.129.rest_ref = bf16[768,1024]{1,0:T(8,128)(2,1)} custom-call(s32[1]{0:T(128)} %bitcast.2.scalars, bf16[768,256]{1,0:T(8,128)(2,1)} %bitcast.12.refs_0_, bf16[768,256]{1,0:T(8,128)(2,1)} %copy-done.26, bf16[768,256]{1,0:T(8,128)(2,1)} %collective-permute-done.7.refs_2_, bf16[768,256]{1,0:T(8,128)(2,1)} %collective-permute-done.8.refs_3_), custom_call_target="tpu_custom_call" | custom-call | flops 137438953472 | bytes 1048576 | tf_op jit(solution)/shard_map/pallas_call | solution.py:380
  113.4 1.4 copy-done.3
  114.8 1.4 shard_map.130
  116.3 7.6 %fusion.2 = f32[768,1440]{0,1:T(8,128)S(1)} fusion(bf16[768,2304]{1,0:T(8,128)(2,1)S(1)} %shard_map.130, bf16[1,2304,1440]{1,2,0:T(8,128)(2,1)} %param.23), kind=kOutput, calls=%fused_computation.2 | convolution fusion | flops 5096079360 | bytes 14598144 | tf_op jit(solution)/shard_map/dot_general | solution.py:596
  124.0 5.9 %multiply_convert_fusion = bf16[768,1440]{0,1:T(8,128)(2,1)S(1)} fusion(f32[768,1440]{0,1:T(8,128)S(1)} %fusion.2, bf16[768,2304]{1,0:T(8,128)(2,1)S(1)} %shard_map.130, bf16[1,2304,1440]{1,2,0:T(8,128)(2,1)S(1)} %bitcast.77), kind=kOutput, calls=%fused_computation.4 | convolution fusion | flops 5102714880 | bytes 16809984 | tf_op jit(solution)/shard_map/dot_general | solution.py:597
  129.9 2.7 %fusion.15 = bf16[4,768,256]{2,1,0:T(8,128)(2,1)S(1)} fusion(bf16[4,1440,256]{2,1,0:T(8,128)(2,1)S(1)} %copy-done.17, bf16[768,1440]{0,1:T(8,128)(2,1)S(1)} %multiply_convert_fusion), kind=kOutput, calls=%fused_computation.14 | convolution fusion | flops 2265710592 | bytes 6733824 | tf_op jit(solution)/shard_map/rh,khs->krs/dot_general | solution.py:605
  132.6 1.0 slice_bitcast_fusion
  133.7 1.9 collective-permute-start.13
  135.6 2.9 %collective-permute-start.14 = (bf16[768,256]{1,0:T(8,128)(2,1)S(1)}, bf16[768,256]{1,0:T(8,128)(2,1)}, u32[]{:S(2)}, u32[]{:S(2)}) collective-permute-start(bf16[768,256]{1,0:T(8,128)(2,1)S(1)} %get-tuple-element.51), channel_id=1, source_target_pairs={{0,3},{1,0},{2,1},{3,2},{4,7},{5,4},{6,5},{7,6},{8,11},{9,8},{10,9... | collective-permute-start | bytes 1179656 | tf_op jit(solution)/shard_map/ppermute | solution.py:470
  138.6 4.5 %fusion.7 = bf16[768,1280]{1,0:T(8,128)(2,1)} fusion(bf16[768,1440]{0,1:T(8,128)(2,1)S(1)} %multiply_convert_fusion, bf16[1,1440,2304]{2,1,0:T(8,128)(2,1)S(1)} %bitcast.75), kind=kOutput, calls=%fused_computation.9 | convolution fusion | flops 2832138240 | bytes 7864320 | tf_op jit(solution)/shard_map/dot_general | solution.py:601
  143.0 3.7 %all-to-all-start.2 = ((bf16[8,96,1280]{2,1,0:T(8,128)(2,1)}), bf16[8,96,1280]{2,1,0:T(8,128)(2,1)S(1)}, u32[]{:S(2)}, u32[]{:S(2)}) async-start(bf16[8,96,1280]{2,1,0:T(8,128)(2,1)} %bitcast.72), calls=%async_computation.2 | async-start | bytes 3932160 | tf_op jit(solution)/shard_map/all_to_all | solution.py:477
  146.8 1.1 collective-permute-done.12.refs_1_
  147.9 13.6 %collective-permute-done.13.refs_2_ = bf16[768,256]{1,0:T(8,128)(2,1)} collective-permute-done((bf16[768,256]{1,0:T(8,128)(2,1)S(1)}, bf16[768,256]{1,0:T(8,128)(2,1)}, u32[]{:S(2)}, u32[]{:S(2)}) %collective-permute-start.13) | collective-permute-done | bytes 393248 | tf_op jit(solution)/shard_map/ppermute | solution.py:470
  161.6 3.5 %shard_map.133.__0_ = bf16[768,256]{1,0:T(8,128)(2,1)} custom-call(bf16[768,256]{1,0:T(8,128)(2,1)} %get-tuple-element.54.refs_0_, bf16[768,256]{1,0:T(8,128)(2,1)} %collective-permute-done.12.refs_1_, bf16[768,256]{1,0:T(8,128)(2,1)} %collective-permute-done.13.refs_2_, bf16[768,256]{1,0:T(8,128)(2,1)} %collective-permute-done.14.refs_3_), custom_call_target="tpu_custom_call" | custom-call | flops 137438953472 | bytes 1048576 | tf_op jit(solution)/shard_map/pallas_call | solution.py:404
  165.1 6.9 %all-to-all-done.2 = bf16[8,96,1280]{2,1,0:T(8,128)(2,1)S(1)} async-done(((bf16[8,96,1280]{2,1,0:T(8,128)(2,1)}), bf16[8,96,1280]{2,1,0:T(8,128)(2,1)S(1)}, u32[]{:S(2)}, u32[]{:S(2)}) %all-to-all-start.2) | async-done | bytes 1966112 | tf_op jit(solution)/shard_map/all_to_all | solution.py:477
  172.0 1.3 copy-done
  173.3 3.5 %all-to-all-start.3 = ((bf16[8,96,256]{2,1,0:T(8,128)(2,1)}), bf16[8,96,256]{2,1,0:T(8,128)(2,1)S(1)}, u32[]{:S(2)}, u32[]{:S(2)}) async-start(bf16[8,96,256]{2,1,0:T(8,128)(2,1)} %bitcast.73), calls=%async_computation.3 | async-start | bytes 786432 | tf_op jit(solution)/shard_map/all_to_all | solution.py:477
  176.9 1.5 copy-done.1
  178.4 1.3 shard_map.131
  180.4 2.0 collective-permute-start.10
  182.4 3.5 %collective-permute-start.11 = (bf16[64,1280]{1,0:T(8,128)(2,1)S(1)}, bf16[64,1280]{1,0:T(8,128)(2,1)S(1)}, u32[]{:S(2)}, u32[]{:S(2)}) collective-permute-start(bf16[64,1280]{1,0:T(8,128)(2,1)S(1)} %get-tuple-element.41), channel_id=1, source_target_pairs={{0,3},{1,0},{2,1},{3,2},{4,7},{5,4},{6,5},{7,6},{8,11},{9,8},{10,9... | collective-permute-start | bytes 491528 | tf_op jit(solution)/shard_map/ppermute | solution.py:470
  186.5 4.2 %collective-permute-start.15 = (bf16[64,256]{1,0:T(8,128)(2,1)S(1)}, bf16[64,256]{1,0:T(8,128)(2,1)S(1)}, u32[]{:S(2)}, u32[]{:S(2)}) collective-permute-start(bf16[64,256]{1,0:T(8,128)(2,1)S(1)} %get-tuple-element.44), channel_id=1, source_target_pairs={{0,3},{1,0},{2,1},{3,2},{4,7},{5,4},{6,5},{7,6},{8,11},{9,8},{10,9... | collective-permute-start | bytes 98312 | tf_op jit(solution)/shard_map/ppermute | solution.py:470
  190.7 1.1 collective-permute-done.10.refs_2_
  191.9 3.4 %collective-permute-start.17 = (bf16[64,256]{1,0:T(8,128)(2,1)S(1)}, bf16[64,256]{1,0:T(8,128)(2,1)S(1)}, u32[]{:S(2)}, u32[]{:S(2)}) collective-permute-start(bf16[64,256]{1,0:T(8,128)(2,1)S(1)} %get-tuple-element.46), channel_id=1, source_target_pairs={{0,1},{1,2},{2,3},{3,0},{4,5},{5,6},{6,7},{7,4},{8,9},{9,10},{10,1... | collective-permute-start | bytes 98312 | tf_op jit(solution)/shard_map/ppermute | solution.py:470
  195.2 2.7 %collective-permute-done.9.refs_1_ = bf16[64,1280]{1,0:T(8,128)(2,1)S(1)} collective-permute-done((bf16[64,1280]{1,0:T(8,128)(2,1)S(1)}, bf16[64,1280]{1,0:T(8,128)(2,1)S(1)}, u32[]{:S(2)}, u32[]{:S(2)}) %collective-permute-start.9) | collective-permute-done | bytes 163872 | tf_op jit(solution)/shard_map/ppermute | solution.py:470
  198.6 1.9 shard_map.132.first_ref
  201.7 1.5 shard_map.136.rest_ref
  203.2 1.7 shard_map.137
  (108 shorter events, 7.8 us)
Async XLA Ops:
  2.1 27.9 %copy-start.24 = (f32[2304]{0:T(1024)S(1)}, f32[2304]{0:T(1024)}, u32[]{:S(2)}) copy-start(f32[2304]{0:T(1024)} %param.20) | copy-start | bytes 27652
  2.1 27.9 %copy-start.25 = (s32[256,2]{0,1:T(2,128)S(1)}, s32[256,2]{0,1:T(2,128)}, u32[]{:S(2)}) copy-start(s32[256,2]{0,1:T(2,128)} %param.22) | copy-start | bytes 6148
  23.0 13.2 %collective-permute-start = (bf16[64,2304]{1,0:T(8,128)(2,1)}, bf16[64,2304]{1,0:T(8,128)(2,1)S(1)}, u32[]{:S(2)}, u32[]{:S(2)}) collective-permute-start(bf16[64,2304]{1,0:T(8,128)(2,1)} %get-tuple-element.27), channel_id=1, source_target_pairs={{0,1},{1,2},{2,3},{3,0},{4,5},{5,6},{6,7},{7,4},{8,9},{9,10},{10,1... | collective-permute-start | bytes 884744 | tf_op jit(solution)/shard_map/ppermute | solution.py:470
  26.0 22.0 %collective-permute-start.1 = (bf16[64,2304]{1,0:T(8,128)(2,1)}, bf16[64,2304]{1,0:T(8,128)(2,1)S(1)}, u32[]{:S(2)}, u32[]{:S(2)}) collective-permute-start(bf16[64,2304]{1,0:T(8,128)(2,1)} %get-tuple-element.28), channel_id=1, source_target_pairs={{0,2},{1,3},{2,0},{3,1},{4,6},{5,7},{6,4},{7,5},{8,10},{9,11},{10,... | collective-permute-start | bytes 884744 | tf_op jit(solution)/shard_map/ppermute | solution.py:470
  28.6 19.4 %collective-permute-start.2 = (bf16[64,2304]{1,0:T(8,128)(2,1)}, bf16[64,2304]{1,0:T(8,128)(2,1)S(1)}, u32[]{:S(2)}, u32[]{:S(2)}) collective-permute-start(bf16[64,2304]{1,0:T(8,128)(2,1)} %get-tuple-element.29), channel_id=1, source_target_pairs={{0,3},{1,0},{2,1},{3,2},{4,7},{5,4},{6,5},{7,6},{8,11},{9,8},{10,9... | collective-permute-start | bytes 884744 | tf_op jit(solution)/shard_map/ppermute | solution.py:470
  32.1 15.9 %copy-start.2 = (bf16[256,2304]{1,0:T(8,128)(2,1)S(1)}, bf16[256,2304]{1,0:T(8,128)(2,1)}, u32[]{:S(2)}) copy-start(bf16[256,2304]{1,0:T(8,128)(2,1)} %refs_4_.1) | copy-start | bytes 3538948
  32.1 15.9 %copy-start.13 = (bf16[64,2304]{1,0:T(8,128)(2,1)S(1)}, bf16[64,2304]{1,0:T(8,128)(2,1)}, u32[]{:S(2)}) copy-start(bf16[64,2304]{1,0:T(8,128)(2,1)} %get-tuple-element.26.refs_0_) | copy-start | bytes 884740
  32.1 15.9 %copy-start.14 = (bf16[2304,8]{0,1:T(8,128)(2,1)S(1)}, bf16[2304,8]{0,1:T(8,128)(2,1)}, u32[]{:S(2)}) copy-start(bf16[2304,8]{0,1:T(8,128)(2,1)} %param.21) | copy-start | bytes 110596
  35.3 24.2 %copy-start.18 = (pred[768,256]{1,0:T(32,128)(4,1)}, pred[768,256]{1,0:T(32,128)(4,1)S(1)}, u32[]{:S(2)}) copy-start(pred[768,256]{1,0:T(32,128)(4,1)S(1)} %bitcast_compare_fusion) | copy-start | bytes 589828
  50.1 30.3 %copy-start.5 = (bf16[64,1408]{1,0:T(8,128)(2,1)}, bf16[64,1408]{1,0:T(8,128)(2,1)S(1)}, u32[]{:S(2)}) copy-start(bf16[64,1408]{1,0:T(8,128)(2,1)S(1)} %get-tuple-element.30.refs_0_) | copy-start | bytes 540676
  50.1 13.8 %collective-permute-start.3 = (bf16[64,1408]{1,0:T(8,128)(2,1)}, bf16[64,1408]{1,0:T(8,128)(2,1)S(1)}, u32[]{:S(2)}, u32[]{:S(2)}) collective-permute-start(bf16[64,1408]{1,0:T(8,128)(2,1)} %get-tuple-element.31), channel_id=1, source_target_pairs={{0,3},{1,0},{2,1},{3,2},{4,7},{5,4},{6,5},{7,6},{8,11},{9,8},{10,9... | collective-permute-start | bytes 540680 | tf_op jit(solution)/shard_map/ppermute | solution.py:473
  57.9 16.7 %collective-permute-start.4 = (bf16[64,1408]{1,0:T(8,128)(2,1)}, bf16[64,1408]{1,0:T(8,128)(2,1)S(1)}, u32[]{:S(2)}, u32[]{:S(2)}) collective-permute-start(bf16[64,1408]{1,0:T(8,128)(2,1)} %get-tuple-element.32), channel_id=1, source_target_pairs={{0,2},{1,3},{2,0},{3,1},{4,6},{5,7},{6,4},{7,5},{8,10},{9,11},{10,... | collective-permute-start | bytes 540680 | tf_op jit(solution)/shard_map/ppermute | solution.py:473
  58.3 16.3 %collective-permute-start.5 = (bf16[64,1408]{1,0:T(8,128)(2,1)}, bf16[64,1408]{1,0:T(8,128)(2,1)S(1)}, u32[]{:S(2)}, u32[]{:S(2)}) collective-permute-start(bf16[64,1408]{1,0:T(8,128)(2,1)} %get-tuple-element.33), channel_id=1, source_target_pairs={{0,1},{1,2},{2,3},{3,0},{4,5},{5,6},{6,7},{7,4},{8,9},{9,10},{10,1... | collective-permute-start | bytes 540680 | tf_op jit(solution)/shard_map/ppermute | solution.py:473
  59.5 18.9 %copy-start.19 = (pred[768,256]{1,0:T(32,128)(4,1)S(1)}, pred[768,256]{1,0:T(32,128)(4,1)}, u32[]{:S(2)}) copy-start(pred[768,256]{1,0:T(32,128)(4,1)} %copy-done.18) | copy-start | bytes 589828
  59.5 15.2 %all-to-all-start = ((bf16[8,96,256]{2,1,0:T(8,128)(2,1)}), bf16[8,96,256]{2,1,0:T(8,128)(2,1)}, u32[]{:S(2)}, u32[]{:S(2)}) async-start(bf16[8,96,256]{2,1,0:T(8,128)(2,1)} %bitcast.11), calls=%async_computation | async-start | bytes 786432 | tf_op jit(solution)/shard_map/all_to_all | solution.py:477
  63.8 16.6 %copy-start.7 = (bf16[64,1408]{1,0:T(8,128)(2,1)}, bf16[64,1408]{1,0:T(8,128)(2,1)S(1)}, u32[]{:S(2)}) copy-start(bf16[64,1408]{1,0:T(8,128)(2,1)S(1)} %collective-permute-done.3.refs_1_) | copy-start | bytes 540676
  74.5 5.8 %copy-start.9 = (bf16[64,1408]{1,0:T(8,128)(2,1)}, bf16[64,1408]{1,0:T(8,128)(2,1)S(1)}, u32[]{:S(2)}) copy-start(bf16[64,1408]{1,0:T(8,128)(2,1)S(1)} %collective-permute-done.4.refs_2_) | copy-start | bytes 540676
  74.6 5.8 %copy-start.11 = (bf16[64,1408]{1,0:T(8,128)(2,1)}, bf16[64,1408]{1,0:T(8,128)(2,1)S(1)}, u32[]{:S(2)}) copy-start(bf16[64,1408]{1,0:T(8,128)(2,1)S(1)} %collective-permute-done.5.refs_3_) | copy-start | bytes 540676
  74.7 12.1 %collective-permute-start.6 = (bf16[768,256]{1,0:T(8,128)(2,1)}, bf16[768,256]{1,0:T(8,128)(2,1)S(1)}, u32[]{:S(2)}, u32[]{:S(2)}) collective-permute-start(bf16[768,256]{1,0:T(8,128)(2,1)} %bitcast.12.refs_0_), channel_id=1, source_target_pairs={{0,3},{1,0},{2,1},{3,2},{4,7},{5,4},{6,5},{7,6},{8,11},{9,8},{10,9... | collective-permute-start | bytes 1179656 | tf_op jit(solution)/shard_map/ppermute | solution.py:473
  75.7 34.0 %collective-permute-start.7 = (bf16[768,256]{1,0:T(8,128)(2,1)}, bf16[768,256]{1,0:T(8,128)(2,1)}, u32[]{:S(2)}, u32[]{:S(2)}) collective-permute-start(bf16[768,256]{1,0:T(8,128)(2,1)} %bitcast.12.refs_0_), channel_id=1, source_target_pairs={{0,2},{1,3},{2,0},{3,1},{4,6},{5,7},{6,4},{7,5},{8,10},{9,11},{10,... | collective-permute-start | bytes 1179656 | tf_op jit(solution)/shard_map/ppermute | solution.py:473
  76.4 33.3 %collective-permute-start.8 = (bf16[768,256]{1,0:T(8,128)(2,1)}, bf16[768,256]{1,0:T(8,128)(2,1)}, u32[]{:S(2)}, u32[]{:S(2)}) collective-permute-start(bf16[768,256]{1,0:T(8,128)(2,1)} %bitcast.12.refs_0_), channel_id=1, source_target_pairs={{0,1},{1,2},{2,3},{3,0},{4,5},{5,6},{6,7},{7,4},{8,9},{9,10},{10,1... | collective-permute-start | bytes 1179656 | tf_op jit(solution)/shard_map/ppermute | solution.py:473
  80.4 33.0 %all-to-all-start.1 = ((bf16[8,96,1280]{2,1,0:T(8,128)(2,1)}), bf16[8,96,1280]{2,1,0:T(8,128)(2,1)S(1)}, u32[]{:S(2)}, u32[]{:S(2)}) async-start(bf16[8,96,1280]{2,1,0:T(8,128)(2,1)} %bitcast.69), calls=%async_computation.1 | async-start | bytes 3932160 | tf_op jit(solution)/shard_map/all_to_all | solution.py:477
  86.8 23.0 %copy-start.26 = (bf16[768,256]{1,0:T(8,128)(2,1)}, bf16[768,256]{1,0:T(8,128)(2,1)S(1)}, u32[]{:S(2)}) copy-start(bf16[768,256]{1,0:T(8,128)(2,1)S(1)} %collective-permute-done.6.refs_1_) | copy-start | bytes 1179652
  114.8 9.1 %slice-start.2 = ((s8[6635520]{0:T(1024)(128)(4,1)}), s8[4194304]{0:T(1024)(128)(4,1)S(1)}, s32[]{:S(2)}) async-start(s8[6635520]{0:T(1024)(128)(4,1)} %bitcast.76), calls=%async_computation.6 | async-start | bytes 8388608
  116.3 7.7 %slice-start.3 = ((s8[6635520]{0:T(1024)(128)(4,1)}), s8[2441216]{0:T(1024)(128)(4,1)S(1)}, s32[]{:S(2)}) async-start(s8[6635520]{0:T(1024)(128)(4,1)} %bitcast.76), calls=%async_computation.7 | async-start | bytes 4882432
  116.3 22.3 %slice-start = ((s8[6635520]{0:T(1024)(128)(4,1)}), s8[4194304]{0:T(1024)(128)(4,1)S(1)}, s32[]{:S(2)}) async-start(s8[6635520]{0:T(1024)(128)(4,1)} %bitcast.74), calls=%async_computation.4 | async-start | bytes 8388608
  124.0 5.9 %copy-start.17 = (bf16[4,1440,256]{2,1,0:T(8,128)(2,1)S(1)}, bf16[4,1440,256]{2,1,0:T(8,128)(2,1)}, u32[]{:S(2)}) copy-start(bf16[4,1440,256]{2,1,0:T(8,128)(2,1)} %pad_maximum_fusion) | copy-start | bytes 8847364
  124.0 14.6 %slice-start.1 = ((s8[6635520]{0:T(1024)(128)(4,1)}), s8[2441216]{0:T(1024)(128)(4,1)S(1)}, s32[]{:S(2)}) async-start(s8[6635520]{0:T(1024)(128)(4,1)} %bitcast.74), calls=%async_computation.5 | async-start | bytes 4882432
  133.6 14.3 %collective-permute-start.12 = (bf16[768,256]{1,0:T(8,128)(2,1)}, bf16[768,256]{1,0:T(8,128)(2,1)}, u32[]{:S(2)}, u32[]{:S(2)}) collective-permute-start(bf16[768,256]{1,0:T(8,128)(2,1)} %get-tuple-element.53), channel_id=1, source_target_pairs={{0,1},{1,2},{2,3},{3,0},{4,5},{5,6},{6,7},{7,4},{8,9},{9,10},{10,1... | collective-permute-start | bytes 1179656 | tf_op jit(solution)/shard_map/ppermute | solution.py:470
  133.7 27.8 %collective-permute-start.13 = (bf16[768,256]{1,0:T(8,128)(2,1)S(1)}, bf16[768,256]{1,0:T(8,128)(2,1)}, u32[]{:S(2)}, u32[]{:S(2)}) collective-permute-start(bf16[768,256]{1,0:T(8,128)(2,1)S(1)} %get-tuple-element.52), channel_id=1, source_target_pairs={{0,2},{1,3},{2,0},{3,1},{4,6},{5,7},{6,4},{7,5},{8,10},{9,11},{10,... | collective-permute-start | bytes 1179656 | tf_op jit(solution)/shard_map/ppermute | solution.py:470
  135.6 25.9 %collective-permute-start.14 = (bf16[768,256]{1,0:T(8,128)(2,1)S(1)}, bf16[768,256]{1,0:T(8,128)(2,1)}, u32[]{:S(2)}, u32[]{:S(2)}) collective-permute-start(bf16[768,256]{1,0:T(8,128)(2,1)S(1)} %get-tuple-element.51), channel_id=1, source_target_pairs={{0,3},{1,0},{2,1},{3,2},{4,7},{5,4},{6,5},{7,6},{8,11},{9,8},{10,9... | collective-permute-start | bytes 1179656 | tf_op jit(solution)/shard_map/ppermute | solution.py:470
  143.0 29.0 %all-to-all-start.2 = ((bf16[8,96,1280]{2,1,0:T(8,128)(2,1)}), bf16[8,96,1280]{2,1,0:T(8,128)(2,1)S(1)}, u32[]{:S(2)}, u32[]{:S(2)}) async-start(bf16[8,96,1280]{2,1,0:T(8,128)(2,1)} %bitcast.72), calls=%async_computation.2 | async-start | bytes 3932160 | tf_op jit(solution)/shard_map/all_to_all | solution.py:477
  165.0 11.8 %copy-start.4 = (s32[256,2]{1,0:T(8,128)S(1)}, s32[256,2]{1,0:T(8,128)}, u32[]{:S(2)}) copy-start(s32[256,2]{1,0:T(8,128)} %copy.29.routes_ref) | copy-start | bytes 6148
  165.0 11.8 %copy-start.20 = (s32[256,2]{1,0:T(8,128)S(1)}, s32[256,2]{1,0:T(8,128)}, u32[]{:S(2)}) copy-start(s32[256,2]{1,0:T(8,128)} %copy.26) | copy-start | bytes 6148
  165.0 11.8 %copy-start.6 = (bf16[64,1408]{1,0:T(8,128)(2,1)S(1)}, bf16[64,1408]{1,0:T(8,128)(2,1)}, u32[]{:S(2)}) copy-start(bf16[64,1408]{1,0:T(8,128)(2,1)} %copy-done.5) | copy-start | bytes 540676
  165.0 11.8 %copy-start.8 = (bf16[64,1408]{1,0:T(8,128)(2,1)S(1)}, bf16[64,1408]{1,0:T(8,128)(2,1)}, u32[]{:S(2)}) copy-start(bf16[64,1408]{1,0:T(8,128)(2,1)} %copy-done.7) | copy-start | bytes 540676
  165.0 11.8 %copy-start.10 = (bf16[64,1408]{1,0:T(8,128)(2,1)S(1)}, bf16[64,1408]{1,0:T(8,128)(2,1)}, u32[]{:S(2)}) copy-start(bf16[64,1408]{1,0:T(8,128)(2,1)} %copy-done.9) | copy-start | bytes 540676
  165.1 11.8 %copy-start.12 = (bf16[64,1408]{1,0:T(8,128)(2,1)S(1)}, bf16[64,1408]{1,0:T(8,128)(2,1)}, u32[]{:S(2)}) copy-start(bf16[64,1408]{1,0:T(8,128)(2,1)} %copy-done.11) | copy-start | bytes 540676
  173.3 12.6 %all-to-all-start.3 = ((bf16[8,96,256]{2,1,0:T(8,128)(2,1)}), bf16[8,96,256]{2,1,0:T(8,128)(2,1)S(1)}, u32[]{:S(2)}, u32[]{:S(2)}) async-start(bf16[8,96,256]{2,1,0:T(8,128)(2,1)} %bitcast.73), calls=%async_computation.3 | async-start | bytes 786432 | tf_op jit(solution)/shard_map/all_to_all | solution.py:477
  180.4 11.5 %collective-permute-start.10 = (bf16[64,1280]{1,0:T(8,128)(2,1)S(1)}, bf16[64,1280]{1,0:T(8,128)(2,1)S(1)}, u32[]{:S(2)}, u32[]{:S(2)}) collective-permute-start(bf16[64,1280]{1,0:T(8,128)(2,1)S(1)} %get-tuple-element.40), channel_id=1, source_target_pairs={{0,2},{1,3},{2,0},{3,1},{4,6},{5,7},{6,4},{7,5},{8,10},{9,11},{10,... | collective-permute-start | bytes 491528 | tf_op jit(solution)/shard_map/ppermute | solution.py:470
  182.4 12.8 %collective-permute-start.11 = (bf16[64,1280]{1,0:T(8,128)(2,1)S(1)}, bf16[64,1280]{1,0:T(8,128)(2,1)S(1)}, u32[]{:S(2)}, u32[]{:S(2)}) collective-permute-start(bf16[64,1280]{1,0:T(8,128)(2,1)S(1)} %get-tuple-element.41), channel_id=1, source_target_pairs={{0,3},{1,0},{2,1},{3,2},{4,7},{5,4},{6,5},{7,6},{8,11},{9,8},{10,9... | collective-permute-start | bytes 491528 | tf_op jit(solution)/shard_map/ppermute | solution.py:470
  185.9 12.1 %collective-permute-start.9 = (bf16[64,1280]{1,0:T(8,128)(2,1)S(1)}, bf16[64,1280]{1,0:T(8,128)(2,1)S(1)}, u32[]{:S(2)}, u32[]{:S(2)}) collective-permute-start(bf16[64,1280]{1,0:T(8,128)(2,1)S(1)} %get-tuple-element.39), channel_id=1, source_target_pairs={{0,1},{1,2},{2,3},{3,0},{4,5},{5,6},{6,7},{7,4},{8,9},{9,10},{10,1... | collective-permute-start | bytes 491528 | tf_op jit(solution)/shard_map/ppermute | solution.py:470
  186.5 14.0 %copy-start.15 = (bf16[64,256]{1,0:T(8,128)(2,1)}, bf16[64,256]{1,0:T(8,128)(2,1)S(1)}, u32[]{:S(2)}) copy-start(bf16[64,256]{1,0:T(8,128)(2,1)S(1)} %get-tuple-element.43.refs_0_) | copy-start | bytes 98308
  186.5 14.0 %collective-permute-start.15 = (bf16[64,256]{1,0:T(8,128)(2,1)S(1)}, bf16[64,256]{1,0:T(8,128)(2,1)S(1)}, u32[]{:S(2)}, u32[]{:S(2)}) collective-permute-start(bf16[64,256]{1,0:T(8,128)(2,1)S(1)} %get-tuple-element.44), channel_id=1, source_target_pairs={{0,3},{1,0},{2,1},{3,2},{4,7},{5,4},{6,5},{7,6},{8,11},{9,8},{10,9... | collective-permute-start | bytes 98312 | tf_op jit(solution)/shard_map/ppermute | solution.py:470
  190.7 10.4 %collective-permute-start.16 = (bf16[64,256]{1,0:T(8,128)(2,1)S(1)}, bf16[64,256]{1,0:T(8,128)(2,1)S(1)}, u32[]{:S(2)}, u32[]{:S(2)}) collective-permute-start(bf16[64,256]{1,0:T(8,128)(2,1)S(1)} %get-tuple-element.45), channel_id=1, source_target_pairs={{0,2},{1,3},{2,0},{3,1},{4,6},{5,7},{6,4},{7,5},{8,10},{9,11},{10,... | collective-permute-start | bytes 98312 | tf_op jit(solution)/shard_map/ppermute | solution.py:470
  191.9 6.1 %copy-start.27 = (bf16[64,1280]{1,0:T(8,128)(2,1)}, bf16[64,1280]{1,0:T(8,128)(2,1)S(1)}, u32[]{:S(2)}) copy-start(bf16[64,1280]{1,0:T(8,128)(2,1)S(1)} %collective-permute-done.10.refs_2_) | copy-start | bytes 491524
  191.9 9.3 %collective-permute-start.17 = (bf16[64,256]{1,0:T(8,128)(2,1)S(1)}, bf16[64,256]{1,0:T(8,128)(2,1)S(1)}, u32[]{:S(2)}, u32[]{:S(2)}) collective-permute-start(bf16[64,256]{1,0:T(8,128)(2,1)S(1)} %get-tuple-element.46), channel_id=1, source_target_pairs={{0,1},{1,2},{2,3},{3,0},{4,5},{5,6},{6,7},{7,4},{8,9},{9,10},{10,1... | collective-permute-start | bytes 98312 | tf_op jit(solution)/shard_map/ppermute | solution.py:470
  195.2 2.7 %copy-start.28 = (bf16[64,1280]{1,0:T(8,128)(2,1)}, bf16[64,1280]{1,0:T(8,128)(2,1)S(1)}, u32[]{:S(2)}) copy-start(bf16[64,1280]{1,0:T(8,128)(2,1)S(1)} %collective-permute-done.11.refs_3_) | copy-start | bytes 491524
  (8 other events, 7.5 us)

commit v3 on v2

--- a/solution.py
+++ b/solution.py
@@ -17,6 +17,7 @@
 MASKED = -1e30
 EPSILON = 1e-05
 NT = (((1,), (1,)), ((), ()))
+GRANT = pltpu.CompilerParams(vmem_limit_bytes=24 * 1024 * 1024)
 AHEAD = pl.CostEstimate(flops=1 << 37, bytes_accessed=1 << 20, transcendentals=0)
 
 
@@ -93,7 +94,8 @@
     wo_ref,
     *rest,
 ):
-    *out_refs, normed, attended, total = rest
+    *out_refs, normed, attended, total, weights_out, copied = rest
+    bring = pltpu.make_async_copy(wo_ref, weights_out, copied)
     tokens, width = hidden_ref.shape
     blocks = tokens // share
     rows_here = kc_ref.shape[0]
@@ -102,6 +104,7 @@
 
     @pl.when(pl.program_id(0) == 0)
     def _():
+        bring.start()
         for k in range(0, blocks, 2):
             pair = []
             for i in range(2):
@@ -151,11 +154,12 @@
 
     @pl.when(pl.program_id(0) == pl.num_programs(0) - 1)
     def _():
+        bring.wait()
         steps = attended.shape[0]
         total[...] = sum(
             jnp.dot(
                 attended[i],
-                wo_ref[i * rows_here : (i + 1) * rows_here, :],
+                weights_out[i * rows_here : (i + 1) * rows_here, :],
                 preferred_element_type=jnp.float32,
             )
             for i in range(steps)
@@ -254,7 +258,7 @@
             jax.ShapeDtypeStruct((tokens, SLICE), jnp.bfloat16),
         ]
         + [jax.ShapeDtypeStruct((share, length), jnp.bfloat16)] * tp,
-        compiler_params=pltpu.CompilerParams(vmem_limit_bytes=32 * 1024 * 1024),
+        compiler_params=GRANT,
         cost_estimate=pl.CostEstimate(
             flops=8 * tp * share * width,
             bytes_accessed=2 * tokens * width + 4 * share * width * tp,
@@ -263,37 +267,48 @@
     )(me_tp.reshape(1), *pieces, hidden_in, gain, router_t)
 
 
-def assemble_kernel(first_ref, rest_ref, gain_ref, out_ref):
+def assemble_kernel(slices, scalars, first_ref, *refs):
+    slice_refs = refs[:slices]
+    gain_ref, out_ref = refs[slices:]
     first = first_ref.shape[1]
     width = out_ref.shape[1]
     rows = first_ref[...].astype(jnp.float32)
-    rest = rest_ref[...].astype(jnp.float32)
+    parts = [ref[...].astype(jnp.float32) for ref in slice_refs]
     squares = jnp.sum(rows * rows, axis=1, keepdims=True)
-    squares = squares + jnp.sum(rest * rest, axis=1, keepdims=True)
+    for part in parts:
+        squares = squares + jnp.sum(part * part, axis=1, keepdims=True)
     scale = lax.rsqrt(squares / width + EPSILON)
     out_ref[:, :first] = (rows * scale * gain_ref[:, :first]).astype(jnp.bfloat16)
-    out_ref[:, first:] = (rest * scale * gain_ref[:, first:]).astype(jnp.bfloat16)
-
-
-def assemble(first_rows, rest, gain):
+    for k, part in enumerate(parts):
+        place = lax.rem(scalars[0] + k, slices) * SLICE + first
+        lanes = pl.ds(pl.multiple_of(place, SLICE), SLICE)
+        out_ref[:, lanes] = (part * scale * gain_ref[:, lanes]).astype(jnp.bfloat16)
+
+
+def assemble(me_tp, first_rows, slices, gain):
     rows, first = first_rows.shape
-    width = first + rest.shape[1]
+    width = first + SLICE * len(slices)
     tile = 2 * CAP
 
     def tiles(n):
-        return pl.BlockSpec((tile, n), lambda i: (i, 0))
+        return pl.BlockSpec((tile, n), lambda i, s: (i, 0))
 
     return pl.pallas_call(
-        assemble_kernel,
-        grid=(rows // tile,),
-        in_specs=[tiles(first), tiles(width - first), pl.BlockSpec((1, width), lambda i: (0, 0))],
-        out_specs=tiles(width),
+        functools.partial(assemble_kernel, len(slices)),
+        grid_spec=pltpu.PrefetchScalarGridSpec(
+            num_scalar_prefetch=1,
+            grid=(rows // tile,),
+            in_specs=[tiles(first)]
+            + [tiles(SLICE)] * len(slices)
+            + [pl.BlockSpec((1, width), lambda i, s: (0, 0))],
+            out_specs=tiles(width),
+        ),
         out_shape=jax.ShapeDtypeStruct((rows, width), jnp.bfloat16),
-        compiler_params=pltpu.CompilerParams(vmem_limit_bytes=16 * 1024 * 1024),
+        compiler_params=GRANT,
         cost_estimate=pl.CostEstimate(
             flops=8 * rows * width, bytes_accessed=4 * rows * width, transcendentals=rows
         ),
-    )(first_rows, rest, gain)
+    )(me_tp.reshape(1), first_rows, *slices, gain)
 
 
 def combine_kernel(width, copies, terms, rows_ref, routes_ref, places_ref, base_ref, *refs):
@@ -366,30 +381,6 @@
     )(*operands)
 
 
-def place_kernel(scalars, *refs):
-    piece_refs, out_ref = refs[:-1], refs[-1]
-    tp = len(piece_refs)
-    for k, ref in enumerate(piece_refs):
-        lanes = pl.ds(pl.multiple_of(lax.rem(scalars[0] + k, tp) * SLICE, SLICE), SLICE)
-        out_ref[:, lanes] = ref[...]
-
-
-def place(first, slices, tile, cost=None):
-    rows = slices[0].shape[0]
-    width = SLICE * len(slices)
-    return pl.pallas_call(
-        place_kernel,
-        grid_spec=pltpu.PrefetchScalarGridSpec(
-            num_scalar_prefetch=1,
-            grid=(rows // tile,),
-            in_specs=[pl.BlockSpec((tile, SLICE), lambda i, s: (i, 0))] * len(slices),
-            out_specs=pl.BlockSpec((tile, width), lambda i, s: (i, 0)),
-        ),
-        out_shape=jax.ShapeDtypeStruct((rows, width), slices[0].dtype),
-        cost_estimate=cost,
-    )(first.reshape(1), *slices)
-
-
 def sum_kernel(*refs):
     *piece_refs, out_ref = refs
     total = piece_refs[0][...].astype(jnp.float32)
@@ -398,15 +389,16 @@
     out_ref[...] = total.astype(out_ref.dtype)
 
 
-def sum_of(pieces, tile):
+def sum_of(pieces):
     rows, columns = pieces[0].shape
-    block = pl.BlockSpec((tile, columns), lambda i: (i, 0))
+    block = pl.BlockSpec((rows, columns), lambda i: (0, 0))
     return pl.pallas_call(
         sum_kernel,
-        grid=(rows // tile,),
+        grid=(1,),
         in_specs=[block] * len(pieces),
         out_specs=block,
         out_shape=jax.ShapeDtypeStruct((rows, columns), jnp.bfloat16),
+        compiler_params=GRANT,
         cost_estimate=AHEAD,
     )(*pieces)
 
@@ -415,28 +407,51 @@
     pass
 
 
-def after(value, *arrivals):
+def after(value, *arrivals, cost=None):
     return pl.pallas_call(
         same_kernel,
         in_specs=[pl.BlockSpec(memory_space=pl.ANY)] * (1 + len(arrivals)),
         out_specs=pl.BlockSpec(memory_space=pl.ANY),
         out_shape=jax.ShapeDtypeStruct(value.shape, value.dtype),
         input_output_aliases={0: 0},
+        cost_estimate=cost,
     )(value, *arrivals)
 
 
-def joined_kernel(first_ref, rest_ref, out_ref):
-    first = first_ref.shape[1]
-    out_ref[:, :first] = first_ref[...]
-    out_ref[:, first:] = rest_ref[...]
-
-
-def joined(first, rest):
-    rows = first.shape[0]
+def finish_kernel(terms, scalars, *refs):
+    term_refs, slice_refs, out_ref = refs[:terms], refs[terms:-1], refs[-1]
+    tp = len(slice_refs)
+    first = out_ref.shape[1] - tp * SLICE
+    total = term_refs[0][...]
+    for ref in term_refs[1:]:
+        total = total + ref[...].astype(jnp.float32)
+    out_ref[:, :first] = total.astype(jnp.bfloat16)
+    for k, ref in enumerate(slice_refs):
+        place = lax.rem(scalars[0] + tp - k, tp) * SLICE + first
+        out_ref[:, pl.ds(pl.multiple_of(place, SLICE), SLICE)] = ref[...]
+
+
+def finish(me_tp, terms, slices):
+    rows, first = terms[0].shape
+    width = first + len(slices) * SLICE
+
+    def full(array):
+        return pl.BlockSpec(array.shape, lambda i, s: (0, 0))
+
     return pl.pallas_call(
-        joined_kernel,
-        out_shape=jax.ShapeDtypeStruct((rows, first.shape[1] + rest.shape[1]), first.dtype),
-    )(first, rest)
+        functools.partial(finish_kernel, len(terms)),
+        grid_spec=pltpu.PrefetchScalarGridSpec(
+            num_scalar_prefetch=1,
+            grid=(1,),
+            in_specs=[full(a) for a in [*terms, *slices]],
+            out_specs=pl.BlockSpec((rows, width), lambda i, s: (0, 0)),
+        ),
+        out_shape=jax.ShapeDtypeStruct((rows, width), jnp.bfloat16),
+        compiler_params=GRANT,
+        cost_estimate=pl.CostEstimate(
+            flops=4 * rows * width, bytes_accessed=10 * rows * width, transcendentals=0
+        ),
+    )(me_tp.reshape(1), *terms, *slices)
 
 
 def per_device(
@@ -539,13 +554,15 @@
                 whole(half, token_count),
                 head_rows(cache_len),
                 head_rows(cache_len),
-                whole(local_lanes, model_width),
+                pl.BlockSpec(memory_space=pl.ANY),
             ],
             out_specs=[whole(share, model_width)] * tp,
             scratch_shapes=[
                 pltpu.VMEM((model_width, token_count), jnp.bfloat16),
                 pltpu.VMEM((local_heads // group, token_count, group * HEAD), jnp.bfloat16),
                 pltpu.VMEM((token_count, model_width), jnp.float32),
+                pltpu.VMEM((local_lanes, model_width), jnp.bfloat16),
+                pltpu.SemaphoreType.DMA,
             ],
         ),
         out_shape=[jax.ShapeDtypeStruct((share, model_width), jnp.bfloat16)] * tp,
@@ -589,9 +606,10 @@
 
     gathered = jnp.concatenate([m[:, :first_width] for m in messages], axis=0)
     gathered, slice_rows = lax.optimization_barrier((gathered, slice_rows))
-    slices = [slice_rows] + [from_block(slice_rows, k) for k in range(1, tp)]
+    slices = [from_block(slice_rows, k) for k in range(1, tp)]
+    slices = [after(slice_rows, *slices, cost=AHEAD), *slices]
     first_rows = to_experts(gathered)
-    token_rows = assemble(first_rows, place(me_tp, slices, 2 * CAP, AHEAD), gain)
+    token_rows = assemble(me_tp, first_rows, slices, gain)
 
     gate_proj = jnp.dot(token_rows, expert_gate[0], preferred_element_type=jnp.float32)
     up_proj = jnp.dot(token_rows, expert_up[0], preferred_element_type=jnp.float32)
@@ -606,7 +624,7 @@
         "rh,khs->krs", activation, slice_downs, preferred_element_type=jnp.float32
     ).astype(jnp.bfloat16)
     slice_sum = sum_of(
-        [slice_terms[0]] + [to_block(slice_terms[k], k) for k in range(1, tp)], 2 * CAP
+        [slice_terms[0]] + [to_block(slice_terms[k], k) for k in range(1, tp)]
     )
 
     slice_back = exchanged(after(slice_sum, first_back))
@@ -621,15 +639,13 @@
         messages,
         [jnp.float32, *kinds[1:]],
     )
-    first_out = sum_of(
-        [first_out] + [to_block(piece, k + 1) for k, piece in enumerate(first_shares)], share
-    )
+    first_shares = [to_block(piece, k + 1) for k, piece in enumerate(first_shares)]
+    first_out = after(first_out, *first_shares, cost=AHEAD)
     slice_outs = combine(
         model_width, copies, slice_back, rolled, places, slice_residual, messages, kinds
     )
     slice_outs = [slice_outs[0]] + [to_block(slice_outs[k], k) for k in range(1, tp)]
-    slice_outs = [slice_outs[0], *slice_outs[:0:-1]]
-    return joined(first_out, place(me_tp, slice_outs, share))
+    return finish(me_tp, [first_out, *first_shares], slice_outs)
 
 
 def solution(mesh):

time: 206 us -> 205 us (level)
  Pallas kernels: 38.4 us -> 25.9 us
  local copies, waits for them, and re-layouts: 11.1 us -> 19.8 us
  waiting for transfers between devices: 75.2 us -> 79.2 us
    pallas_call x6 -> x3, Pallas kernels: 13.7 us -> 2.79 us  [the longest x1 1.81 us: assemble(): pl.pallas_call(functools.partial(assemble_kernel, len(slices)), grid_spec...]
    unnamed x69 -> x89, local copies, waits for them, and re-layouts: 7.15 us -> 15.8 us
    all_to_all x4, waiting for transfers between devices: 6.95 us -> 9.52 us  [exchanged(): lax.all_to_all(blocks, 'req', split_axis=0, concat_axis=0, tiled=True)]
    ppermute x12, waiting for transfers between devices: 32 us -> 34.4 us  [to_block(): return lax.ppermute(array, 'tp', [(i, (i + k) % tp) for i in range(tp)])]
  transfers between devices with their start and end apart: 22 -> 22, of which waited for: 11 -> 11; matrix products, arithmetic and copies ran while one was open for 7% -> 7% of each run, Pallas kernels for 5% -> 1%
where the time goes in v3:
time: 205 us; the launch traced here: 204 us
  waiting for transfers between devices  79.2 us (39%)
  starting transfers between devices  49.4 us (24%)
  Pallas kernels  25.9 us (13%)
  matrix products  24.9 us (12%)
  local copies, waits for them, and re-layouts  19.8 us (10%)
  other arithmetic  3.79 us (2%)
    ppermute x6, waiting for transfers between devices, from_block(): return lax.ppermute(array, 'tp', [(i, (i - k) % tp) for i in range(tp)])  35.3 us
    ppermute x12, waiting for transfers between devices, to_block(): return lax.ppermute(array, 'tp', [(i, (i + k) % tp) for i in range(tp)])  34.4 us
    ppermute x12, starting transfers between devices, to_block(): return lax.ppermute(array, 'tp', [(i, (i + k) % tp) for i in range(tp)])  23.5 us
    pallas_call x1, Pallas kernels, per_device(): pl.pallas_call(functools.partial(attention_kernel, share), grid_spec=pltp...  20 us
    unnamed x89, local copies, waits for them, and re-layouts  15.8 us
    all_to_all x4, starting transfers between devices, exchanged(): lax.all_to_all(blocks, 'req', split_axis=0, concat_axis=0, tiled=True)  14.7 us
    ppermute x6, starting transfers between devices, from_block(): return lax.ppermute(array, 'tp', [(i, (i - k) % tp) for i in range(tp)])  11.3 us
    all_to_all x4, waiting for transfers between devices, exchanged(): lax.all_to_all(blocks, 'req', split_axis=0, concat_axis=0, tiled=True)  9.52 us
  transfers between devices with their start and end apart: 22, of which 11 were waited for; matrix products, arithmetic and copies ran while one was open for 7% of the time, Pallas kernels for 1%

profile of v3, /device:TPU:0, one launch (start us, length us, event | category | flops | bytes accessed | tf_op | source)
XLA Modules:
  0.0 204.2 jit_solution(7664682073452992535)
XLA Ops:
  2.1 20.0 %shard_map.127 = (bf16[64,2304]{1,0:T(8,128)(2,1)}, bf16[64,2304]{1,0:T(8,128)(2,1)}, bf16[64,2304]{1,0:T(8,128)(2,1)}, bf16[64,2304]{1,0:T(8,128)(2,1)}) custom-call(s32[2]{0:T(128)} %pad_add_fusion.scalars, bf16[256,2304]{1,0:T(8,128)(2,1)} %refs_4_.1, f32[2304]{0:T(1024)} %gain_ref.1, bf16[3,576,2304]{2,1,0:T(8,128)(2,1)} %bitcast.73, ...), custom_call_target="tpu_custom_call" | custom-call | flops 4076863488 | bytes 15335424 | tf_op jit(solution)/shard_map/pallas_call | solution.py:544
  22.2 3.1 %collective-permute-start = (bf16[64,2304]{1,0:T(8,128)(2,1)}, bf16[64,2304]{1,0:T(8,128)(2,1)S(1)}, u32[]{:S(2)}, u32[]{:S(2)}) collective-permute-start(bf16[64,2304]{1,0:T(8,128)(2,1)} %get-tuple-element.27), channel_id=1, source_target_pairs={{0,1},{1,2},{2,3},{3,0},{4,5},{5,6},{6,7},{7,4},{8,9},{9,10},{10,1... | collective-permute-start | bytes 884744 | tf_op jit(solution)/shard_map/ppermute | solution.py:485
  25.2 2.6 %collective-permute-start.1 = (bf16[64,2304]{1,0:T(8,128)(2,1)}, bf16[64,2304]{1,0:T(8,128)(2,1)S(1)}, u32[]{:S(2)}, u32[]{:S(2)}) collective-permute-start(bf16[64,2304]{1,0:T(8,128)(2,1)} %get-tuple-element.28), channel_id=1, source_target_pairs={{0,2},{1,3},{2,0},{3,1},{4,6},{5,7},{6,4},{7,5},{8,10},{9,11},{10,... | collective-permute-start | bytes 884744 | tf_op jit(solution)/shard_map/ppermute | solution.py:485
  27.8 1.4 collective-permute-start.2
  29.3 2.0 constant_dynamic-slice_fusion.3
  31.3 1.8 pad_maximum_fusion
  34.5 1.0 collective-permute-done.refs_1_
  35.5 11.8 %collective-permute-done.1.refs_2_ = bf16[64,2304]{1,0:T(8,128)(2,1)S(1)} collective-permute-done((bf16[64,2304]{1,0:T(8,128)(2,1)}, bf16[64,2304]{1,0:T(8,128)(2,1)S(1)}, u32[]{:S(2)}, u32[]{:S(2)}) %collective-permute-start.1) | collective-permute-done | bytes 294944 | tf_op jit(solution)/shard_map/ppermute | solution.py:485
  47.3 1.2 shard_map.128
  49.2 7.8 %collective-permute-start.3 = (bf16[64,1408]{1,0:T(8,128)(2,1)S(1)}, bf16[64,1408]{1,0:T(8,128)(2,1)S(1)}, u32[]{:S(2)}, u32[]{:S(2)}) collective-permute-start(bf16[64,1408]{1,0:T(8,128)(2,1)S(1)} %get-tuple-element.31), channel_id=1, source_target_pairs={{0,3},{1,0},{2,1},{3,2},{4,7},{5,4},{6,5},{7,6},{8,11},{9,8},{10,9... | collective-permute-start | bytes 540680 | tf_op jit(solution)/shard_map/ppermute | solution.py:488
  57.6 1.0 convolution_convert_fusion.1
  58.6 3.7 %all-to-all-start = ((bf16[8,96,256]{2,1,0:T(8,128)(2,1)}), bf16[8,96,256]{2,1,0:T(8,128)(2,1)S(1)}, u32[]{:S(2)}, u32[]{:S(2)}) async-start(bf16[8,96,256]{2,1,0:T(8,128)(2,1)} %bitcast.11), calls=%async_computation | async-start | bytes 786432 | tf_op jit(solution)/shard_map/all_to_all | solution.py:492
  62.5 11.0 %collective-permute-done.4.refs_2_ = bf16[64,1408]{1,0:T(8,128)(2,1)S(1)} collective-permute-done((bf16[64,1408]{1,0:T(8,128)(2,1)S(1)}, bf16[64,1408]{1,0:T(8,128)(2,1)S(1)}, u32[]{:S(2)}, u32[]{:S(2)}) %collective-permute-start.4) | collective-permute-done | bytes 180256 | tf_op jit(solution)/shard_map/ppermute | solution.py:488
  75.0 1.4 collective-permute-start.8
  77.3 2.9 %convolution_convert_fusion = bf16[768,1280]{1,0:T(8,128)(2,1)} fusion(pred[768,256]{1,0:T(32,128)(4,1)} %copy-done.36, bf16[256,1280]{1,0:T(8,128)(2,1)S(1)} %pad_maximum_fusion.1), kind=kOutput, calls=%fused_computation.8 | convolution fusion | flops 504299520 | bytes 2818048 | tf_op jit(solution)/shard_map/dot_general | solution.py:496
  80.3 3.8 %all-to-all-start.1 = ((bf16[8,96,1280]{2,1,0:T(8,128)(2,1)}), bf16[8,96,1280]{2,1,0:T(8,128)(2,1)S(1)}, u32[]{:S(2)}, u32[]{:S(2)}) async-start(bf16[8,96,1280]{2,1,0:T(8,128)(2,1)} %bitcast.74), calls=%async_computation.1 | async-start | bytes 3932160 | tf_op jit(solution)/shard_map/all_to_all | solution.py:492
  84.1 1.2 collective-permute-done.6.__1_.refs_1_
  85.3 23.1 %collective-permute-done.7.__2_.refs_2_ = bf16[768,256]{1,0:T(8,128)(2,1)S(1)} collective-permute-done((bf16[768,256]{1,0:T(8,128)(2,1)S(1)}, bf16[768,256]{1,0:T(8,128)(2,1)S(1)}, u32[]{:S(2)}, u32[]{:S(2)}) %collective-permute-start.7) | collective-permute-done | bytes 393248 | tf_op jit(solution)/shard_map/ppermute | solution.py:488
  109.9 1.0 copy-done.4
  110.9 1.0 copy-done.16
  111.9 1.0 copy-done.18
  112.9 1.0 copy-done.20
  113.8 1.8 shard_map.130
  115.7 7.6 %fusion.2 = f32[768,1440]{0,1:T(8,128)S(1)} fusion(bf16[768,2304]{1,0:T(8,128)(2,1)S(1)} %shard_map.130, bf16[1,2304,1440]{1,2,0:T(8,128)(2,1)} %param.23), kind=kOutput, calls=%fused_computation.2 | convolution fusion | flops 5096079360 | bytes 14598144 | tf_op jit(solution)/shard_map/dot_general | solution.py:614
  123.4 5.9 %multiply_convert_fusion = bf16[768,1440]{0,1:T(8,128)(2,1)S(1)} fusion(f32[768,1440]{0,1:T(8,128)S(1)} %fusion.2, bf16[768,2304]{1,0:T(8,128)(2,1)S(1)} %shard_map.130, bf16[1,2304,1440]{1,2,0:T(8,128)(2,1)S(1)} %bitcast.81), kind=kOutput, calls=%fused_computation.4 | convolution fusion | flops 5102714880 | bytes 16809984 | tf_op jit(solution)/shard_map/dot_general | solution.py:615
  129.3 2.7 %fusion.15 = bf16[4,768,256]{2,1,0:T(8,128)(2,1)S(1)} fusion(bf16[4,1440,256]{2,1,0:T(8,128)(2,1)S(1)} %copy-done.35, bf16[768,1440]{0,1:T(8,128)(2,1)S(1)} %multiply_convert_fusion), kind=kOutput, calls=%fused_computation.14 | convolution fusion | flops 2265710592 | bytes 6733824 | tf_op jit(solution)/shard_map/rh,khs->krs/dot_general | solution.py:623
  132.0 1.0 slice_bitcast_fusion
  133.6 1.6 collective-permute-start.13
  135.2 2.3 %collective-permute-start.14 = (bf16[768,256]{1,0:T(8,128)(2,1)}, bf16[768,256]{1,0:T(8,128)(2,1)S(1)}, u32[]{:S(2)}, u32[]{:S(2)}) collective-permute-start(bf16[768,256]{1,0:T(8,128)(2,1)} %get-tuple-element.51), channel_id=1, source_target_pairs={{0,3},{1,0},{2,1},{3,2},{4,7},{5,4},{6,5},{7,6},{8,11},{9,8},{10,9... | collective-permute-start | bytes 1179656 | tf_op jit(solution)/shard_map/ppermute | solution.py:485
  137.5 4.5 %fusion.7 = bf16[768,1280]{1,0:T(8,128)(2,1)} fusion(bf16[768,1440]{0,1:T(8,128)(2,1)S(1)} %multiply_convert_fusion, bf16[1,1440,2304]{2,1,0:T(8,128)(2,1)S(1)} %bitcast.79), kind=kOutput, calls=%fused_computation.9 | convolution fusion | flops 2832138240 | bytes 7864320 | tf_op jit(solution)/shard_map/dot_general | solution.py:619
  142.0 3.6 %all-to-all-start.2 = ((bf16[8,96,1280]{2,1,0:T(8,128)(2,1)}), bf16[8,96,1280]{2,1,0:T(8,128)(2,1)S(1)}, u32[]{:S(2)}, u32[]{:S(2)}) async-start(bf16[8,96,1280]{2,1,0:T(8,128)(2,1)} %bitcast.77), calls=%async_computation.2 | async-start | bytes 3932160 | tf_op jit(solution)/shard_map/all_to_all | solution.py:492
  145.6 1.6 collective-permute-done.12.refs_1_
  147.2 14.0 %collective-permute-done.13.refs_2_ = bf16[768,256]{1,0:T(8,128)(2,1)S(1)} collective-permute-done((bf16[768,256]{1,0:T(8,128)(2,1)}, bf16[768,256]{1,0:T(8,128)(2,1)S(1)}, u32[]{:S(2)}, u32[]{:S(2)}) %collective-permute-start.13) | collective-permute-done | bytes 393248 | tf_op jit(solution)/shard_map/ppermute | solution.py:485
  162.2 8.6 %all-to-all-done.2 = bf16[8,96,1280]{2,1,0:T(8,128)(2,1)S(1)} async-done(((bf16[8,96,1280]{2,1,0:T(8,128)(2,1)}), bf16[8,96,1280]{2,1,0:T(8,128)(2,1)S(1)}, u32[]{:S(2)}, u32[]{:S(2)}) %all-to-all-start.2) | async-done | bytes 1966112 | tf_op jit(solution)/shard_map/all_to_all | solution.py:492
  170.8 1.3 copy-done
  172.1 3.6 %all-to-all-start.3 = ((bf16[8,96,256]{2,1,0:T(8,128)(2,1)}), bf16[8,96,256]{2,1,0:T(8,128)(2,1)S(1)}, u32[]{:S(2)}, u32[]{:S(2)}) async-start(bf16[8,96,256]{2,1,0:T(8,128)(2,1)} %bitcast.71), calls=%async_computation.3 | async-start | bytes 786432 | tf_op jit(solution)/shard_map/all_to_all | solution.py:492
  175.8 1.5 copy-done.1
  177.3 1.3 shard_map.131
  179.3 1.6 collective-permute-start.10
  180.9 1.4 collective-permute-start.11
  183.0 1.0 all-to-all-done.3
  185.3 2.2 %collective-permute-start.16 = (bf16[64,256]{1,0:T(8,128)(2,1)S(1)}, bf16[64,256]{1,0:T(8,128)(2,1)S(1)}, u32[]{:S(2)}, u32[]{:S(2)}) collective-permute-start(bf16[64,256]{1,0:T(8,128)(2,1)S(1)} %get-tuple-element.45), channel_id=1, source_target_pairs={{0,2},{1,3},{2,0},{3,1},{4,6},{5,7},{6,4},{7,5},{8,10},{9,11},{10,... | collective-permute-start | bytes 98312 | tf_op jit(solution)/shard_map/ppermute | solution.py:485
  187.5 3.4 %collective-permute-done.10.__2_.refs_2_ = bf16[64,1280]{1,0:T(8,128)(2,1)S(1)} collective-permute-done((bf16[64,1280]{1,0:T(8,128)(2,1)S(1)}, bf16[64,1280]{1,0:T(8,128)(2,1)S(1)}, u32[]{:S(2)}, u32[]{:S(2)}) %collective-permute-start.10) | collective-permute-done | bytes 163872 | tf_op jit(solution)/shard_map/ppermute | solution.py:485
  190.9 5.4 %collective-permute-start.17 = (bf16[64,256]{1,0:T(8,128)(2,1)S(1)}, bf16[64,256]{1,0:T(8,128)(2,1)S(1)}, u32[]{:S(2)}, u32[]{:S(2)}) collective-permute-start(bf16[64,256]{1,0:T(8,128)(2,1)S(1)} %get-tuple-element.46), channel_id=1, source_target_pairs={{0,3},{1,0},{2,1},{3,2},{4,7},{5,4},{6,5},{7,6},{8,11},{9,8},{10,9... | collective-permute-start | bytes 98312 | tf_op jit(solution)/shard_map/ppermute | solution.py:485
  197.1 2.5 %collective-permute-done.16.refs_6_ = bf16[64,256]{1,0:T(8,128)(2,1)S(1)} collective-permute-done((bf16[64,256]{1,0:T(8,128)(2,1)S(1)}, bf16[64,256]{1,0:T(8,128)(2,1)S(1)}, u32[]{:S(2)}, u32[]{:S(2)}) %collective-permute-start.16) | collective-permute-done | bytes 32800 | tf_op jit(solution)/shard_map/ppermute | solution.py:485
  199.6 1.0 copy-done.22
  200.6 0.9 copy-done.27
  201.5 0.9 copy-done.29
  (127 shorter events, 14.9 us)
Async XLA Ops:
  2.1 27.1 %copy-start.38 = (f32[2304]{0:T(1024)S(1)}, f32[2304]{0:T(1024)}, u32[]{:S(2)}) copy-start(f32[2304]{0:T(1024)} %param.20) | copy-start | bytes 27652
  2.1 27.1 %copy-start.39 = (s32[256,2]{0,1:T(2,128)S(1)}, s32[256,2]{0,1:T(2,128)}, u32[]{:S(2)}) copy-start(s32[256,2]{0,1:T(2,128)} %param.22) | copy-start | bytes 6148
  22.2 13.3 %collective-permute-start = (bf16[64,2304]{1,0:T(8,128)(2,1)}, bf16[64,2304]{1,0:T(8,128)(2,1)S(1)}, u32[]{:S(2)}, u32[]{:S(2)}) collective-permute-start(bf16[64,2304]{1,0:T(8,128)(2,1)} %get-tuple-element.27), channel_id=1, source_target_pairs={{0,1},{1,2},{2,3},{3,0},{4,5},{5,6},{6,7},{7,4},{8,9},{9,10},{10,1... | collective-permute-start | bytes 884744 | tf_op jit(solution)/shard_map/ppermute | solution.py:485
  25.2 22.0 %collective-permute-start.1 = (bf16[64,2304]{1,0:T(8,128)(2,1)}, bf16[64,2304]{1,0:T(8,128)(2,1)S(1)}, u32[]{:S(2)}, u32[]{:S(2)}) collective-permute-start(bf16[64,2304]{1,0:T(8,128)(2,1)} %get-tuple-element.28), channel_id=1, source_target_pairs={{0,2},{1,3},{2,0},{3,1},{4,6},{5,7},{6,4},{7,5},{8,10},{9,11},{10,... | collective-permute-start | bytes 884744 | tf_op jit(solution)/shard_map/ppermute | solution.py:485
  27.8 19.4 %collective-permute-start.2 = (bf16[64,2304]{1,0:T(8,128)(2,1)}, bf16[64,2304]{1,0:T(8,128)(2,1)S(1)}, u32[]{:S(2)}, u32[]{:S(2)}) collective-permute-start(bf16[64,2304]{1,0:T(8,128)(2,1)} %get-tuple-element.29), channel_id=1, source_target_pairs={{0,3},{1,0},{2,1},{3,2},{4,7},{5,4},{6,5},{7,6},{8,11},{9,8},{10,9... | collective-permute-start | bytes 884744 | tf_op jit(solution)/shard_map/ppermute | solution.py:485
  31.3 16.0 %copy-start.2 = (bf16[256,2304]{1,0:T(8,128)(2,1)S(1)}, bf16[256,2304]{1,0:T(8,128)(2,1)}, u32[]{:S(2)}) copy-start(bf16[256,2304]{1,0:T(8,128)(2,1)} %refs_4_.1) | copy-start | bytes 3538948
  31.3 15.9 %copy-start.23 = (bf16[64,2304]{1,0:T(8,128)(2,1)S(1)}, bf16[64,2304]{1,0:T(8,128)(2,1)}, u32[]{:S(2)}) copy-start(bf16[64,2304]{1,0:T(8,128)(2,1)} %get-tuple-element.26.refs_0_) | copy-start | bytes 884740
  31.3 15.9 %copy-start.32 = (bf16[2304,8]{0,1:T(8,128)(2,1)S(1)}, bf16[2304,8]{0,1:T(8,128)(2,1)}, u32[]{:S(2)}) copy-start(bf16[2304,8]{0,1:T(8,128)(2,1)} %param.21) | copy-start | bytes 110596
  34.5 39.1 %copy-start.36 = (pred[768,256]{1,0:T(32,128)(4,1)}, pred[768,256]{1,0:T(32,128)(4,1)S(1)}, u32[]{:S(2)}) copy-start(pred[768,256]{1,0:T(32,128)(4,1)S(1)} %bitcast_compare_fusion) | copy-start | bytes 589828
  49.2 9.4 %copy-start.33 = (f32[64,1280]{1,0:T(8,128)}, f32[64,1280]{1,0:T(8,128)S(1)}, u32[]{:S(2)}) copy-start(f32[64,1280]{1,0:T(8,128)S(1)} %get-tuple-element.37.base_ref) | copy-start | bytes 983044
  49.2 31.1 %copy-start.7 = (bf16[64,1408]{1,0:T(8,128)(2,1)}, bf16[64,1408]{1,0:T(8,128)(2,1)S(1)}, u32[]{:S(2)}) copy-start(bf16[64,1408]{1,0:T(8,128)(2,1)S(1)} %get-tuple-element.30.refs_0_) | copy-start | bytes 540676
  49.2 13.2 %collective-permute-start.3 = (bf16[64,1408]{1,0:T(8,128)(2,1)S(1)}, bf16[64,1408]{1,0:T(8,128)(2,1)S(1)}, u32[]{:S(2)}, u32[]{:S(2)}) collective-permute-start(bf16[64,1408]{1,0:T(8,128)(2,1)S(1)} %get-tuple-element.31), channel_id=1, source_target_pairs={{0,3},{1,0},{2,1},{3,2},{4,7},{5,4},{6,5},{7,6},{8,11},{9,8},{10,9... | collective-permute-start | bytes 540680 | tf_op jit(solution)/shard_map/ppermute | solution.py:488
  57.0 16.5 %collective-permute-start.4 = (bf16[64,1408]{1,0:T(8,128)(2,1)S(1)}, bf16[64,1408]{1,0:T(8,128)(2,1)S(1)}, u32[]{:S(2)}, u32[]{:S(2)}) collective-permute-start(bf16[64,1408]{1,0:T(8,128)(2,1)S(1)} %get-tuple-element.32), channel_id=1, source_target_pairs={{0,2},{1,3},{2,0},{3,1},{4,6},{5,7},{6,4},{7,5},{8,10},{9,11},{10,... | collective-permute-start | bytes 540680 | tf_op jit(solution)/shard_map/ppermute | solution.py:488
  57.4 16.1 %collective-permute-start.5 = (bf16[64,1408]{1,0:T(8,128)(2,1)S(1)}, bf16[64,1408]{1,0:T(8,128)(2,1)S(1)}, u32[]{:S(2)}, u32[]{:S(2)}) collective-permute-start(bf16[64,1408]{1,0:T(8,128)(2,1)S(1)} %get-tuple-element.33), channel_id=1, source_target_pairs={{0,1},{1,2},{2,3},{3,0},{4,5},{5,6},{6,7},{7,4},{8,9},{9,10},{10,1... | collective-permute-start | bytes 540680 | tf_op jit(solution)/shard_map/ppermute | solution.py:488
  58.6 15.0 %all-to-all-start = ((bf16[8,96,256]{2,1,0:T(8,128)(2,1)}), bf16[8,96,256]{2,1,0:T(8,128)(2,1)S(1)}, u32[]{:S(2)}, u32[]{:S(2)}) async-start(bf16[8,96,256]{2,1,0:T(8,128)(2,1)} %bitcast.11), calls=%async_computation | async-start | bytes 786432 | tf_op jit(solution)/shard_map/all_to_all | solution.py:492
  62.4 17.8 %copy-start.9 = (bf16[64,1408]{1,0:T(8,128)(2,1)}, bf16[64,1408]{1,0:T(8,128)(2,1)S(1)}, u32[]{:S(2)}) copy-start(bf16[64,1408]{1,0:T(8,128)(2,1)S(1)} %collective-permute-done.3.refs_1_) | copy-start | bytes 540676
  73.5 6.8 %copy-start.11 = (bf16[64,1408]{1,0:T(8,128)(2,1)}, bf16[64,1408]{1,0:T(8,128)(2,1)S(1)}, u32[]{:S(2)}) copy-start(bf16[64,1408]{1,0:T(8,128)(2,1)S(1)} %collective-permute-done.4.refs_2_) | copy-start | bytes 540676
  73.5 6.8 %copy-start.13 = (bf16[64,1408]{1,0:T(8,128)(2,1)}, bf16[64,1408]{1,0:T(8,128)(2,1)S(1)}, u32[]{:S(2)}) copy-start(bf16[64,1408]{1,0:T(8,128)(2,1)S(1)} %collective-permute-done.5.refs_3_) | copy-start | bytes 540676
  73.6 6.7 %copy-start.3 = (bf16[8,96,256]{2,1,0:T(8,128)(2,1)}, bf16[8,96,256]{2,1,0:T(8,128)(2,1)S(1)}, u32[]{:S(2)}) copy-start(bf16[8,96,256]{2,1,0:T(8,128)(2,1)S(1)} %all-to-all-done) | copy-start | bytes 1179652
  73.6 11.7 %collective-permute-start.6 = (bf16[768,256]{1,0:T(8,128)(2,1)S(1)}, bf16[768,256]{1,0:T(8,128)(2,1)S(1)}, u32[]{:S(2)}, u32[]{:S(2)}) collective-permute-start(bf16[768,256]{1,0:T(8,128)(2,1)S(1)} %bitcast.66), channel_id=1, source_target_pairs={{0,3},{1,0},{2,1},{3,2},{4,7},{5,4},{6,5},{7,6},{8,11},{9,8},{10,9... | collective-permute-start | bytes 1179656 | tf_op jit(solution)/shard_map/ppermute | solution.py:488
  74.4 34.0 %collective-permute-start.7 = (bf16[768,256]{1,0:T(8,128)(2,1)S(1)}, bf16[768,256]{1,0:T(8,128)(2,1)S(1)}, u32[]{:S(2)}, u32[]{:S(2)}) collective-permute-start(bf16[768,256]{1,0:T(8,128)(2,1)S(1)} %bitcast.67), channel_id=1, source_target_pairs={{0,2},{1,3},{2,0},{3,1},{4,6},{5,7},{6,4},{7,5},{8,10},{9,11},{10,... | collective-permute-start | bytes 1179656 | tf_op jit(solution)/shard_map/ppermute | solution.py:488
  75.0 33.3 %collective-permute-start.8 = (bf16[768,256]{1,0:T(8,128)(2,1)S(1)}, bf16[768,256]{1,0:T(8,128)(2,1)S(1)}, u32[]{:S(2)}, u32[]{:S(2)}) collective-permute-start(bf16[768,256]{1,0:T(8,128)(2,1)S(1)} %bitcast.68), channel_id=1, source_target_pairs={{0,1},{1,2},{2,3},{3,0},{4,5},{5,6},{6,7},{7,4},{8,9},{9,10},{10,1... | collective-permute-start | bytes 1179656 | tf_op jit(solution)/shard_map/ppermute | solution.py:488
  80.3 29.6 %all-to-all-start.1 = ((bf16[8,96,1280]{2,1,0:T(8,128)(2,1)}), bf16[8,96,1280]{2,1,0:T(8,128)(2,1)S(1)}, u32[]{:S(2)}, u32[]{:S(2)}) async-start(bf16[8,96,1280]{2,1,0:T(8,128)(2,1)} %bitcast.74), calls=%async_computation.1 | async-start | bytes 3932160 | tf_op jit(solution)/shard_map/all_to_all | solution.py:492
  85.3 23.1 %copy-start.15 = (bf16[768,256]{1,0:T(8,128)(2,1)}, bf16[768,256]{1,0:T(8,128)(2,1)S(1)}, u32[]{:S(2)}) copy-start(bf16[768,256]{1,0:T(8,128)(2,1)S(1)} %collective-permute-done.6.__1_.refs_1_) | copy-start | bytes 1179652
  113.8 9.5 %slice-start.2 = ((s8[6635520]{0:T(1024)(128)(4,1)}), s8[4194304]{0:T(1024)(128)(4,1)S(1)}, s32[]{:S(2)}) async-start(s8[6635520]{0:T(1024)(128)(4,1)} %bitcast.80), calls=%async_computation.6 | async-start | bytes 8388608
  115.7 7.7 %slice-start.3 = ((s8[6635520]{0:T(1024)(128)(4,1)}), s8[2441216]{0:T(1024)(128)(4,1)S(1)}, s32[]{:S(2)}) async-start(s8[6635520]{0:T(1024)(128)(4,1)} %bitcast.80), calls=%async_computation.7 | async-start | bytes 4882432
  115.7 21.8 %slice-start = ((s8[6635520]{0:T(1024)(128)(4,1)}), s8[4194304]{0:T(1024)(128)(4,1)S(1)}, s32[]{:S(2)}) async-start(s8[6635520]{0:T(1024)(128)(4,1)} %bitcast.78), calls=%async_computation.4 | async-start | bytes 8388608
  123.4 5.9 %copy-start.35 = (bf16[4,1440,256]{2,1,0:T(8,128)(2,1)S(1)}, bf16[4,1440,256]{2,1,0:T(8,128)(2,1)}, u32[]{:S(2)}) copy-start(bf16[4,1440,256]{2,1,0:T(8,128)(2,1)} %pad_maximum_fusion) | copy-start | bytes 8847364
  123.4 14.1 %slice-start.1 = ((s8[6635520]{0:T(1024)(128)(4,1)}), s8[2441216]{0:T(1024)(128)(4,1)S(1)}, s32[]{:S(2)}) async-start(s8[6635520]{0:T(1024)(128)(4,1)} %bitcast.78), calls=%async_computation.5 | async-start | bytes 4882432
  133.1 14.2 %collective-permute-start.12 = (bf16[768,256]{1,0:T(8,128)(2,1)}, bf16[768,256]{1,0:T(8,128)(2,1)S(1)}, u32[]{:S(2)}, u32[]{:S(2)}) collective-permute-start(bf16[768,256]{1,0:T(8,128)(2,1)} %get-tuple-element.53), channel_id=1, source_target_pairs={{0,1},{1,2},{2,3},{3,0},{4,5},{5,6},{6,7},{7,4},{8,9},{9,10},{10,1... | collective-permute-start | bytes 1179656 | tf_op jit(solution)/shard_map/ppermute | solution.py:485
  133.6 27.6 %collective-permute-start.13 = (bf16[768,256]{1,0:T(8,128)(2,1)}, bf16[768,256]{1,0:T(8,128)(2,1)S(1)}, u32[]{:S(2)}, u32[]{:S(2)}) collective-permute-start(bf16[768,256]{1,0:T(8,128)(2,1)} %get-tuple-element.52), channel_id=1, source_target_pairs={{0,2},{1,3},{2,0},{3,1},{4,6},{5,7},{6,4},{7,5},{8,10},{9,11},{10,... | collective-permute-start | bytes 1179656 | tf_op jit(solution)/shard_map/ppermute | solution.py:485
  135.2 26.0 %collective-permute-start.14 = (bf16[768,256]{1,0:T(8,128)(2,1)}, bf16[768,256]{1,0:T(8,128)(2,1)S(1)}, u32[]{:S(2)}, u32[]{:S(2)}) collective-permute-start(bf16[768,256]{1,0:T(8,128)(2,1)} %get-tuple-element.51), channel_id=1, source_target_pairs={{0,3},{1,0},{2,1},{3,2},{4,7},{5,4},{6,5},{7,6},{8,11},{9,8},{10,9... | collective-permute-start | bytes 1179656 | tf_op jit(solution)/shard_map/ppermute | solution.py:485
  142.0 28.8 %all-to-all-start.2 = ((bf16[8,96,1280]{2,1,0:T(8,128)(2,1)}), bf16[8,96,1280]{2,1,0:T(8,128)(2,1)S(1)}, u32[]{:S(2)}, u32[]{:S(2)}) async-start(bf16[8,96,1280]{2,1,0:T(8,128)(2,1)} %bitcast.77), calls=%async_computation.2 | async-start | bytes 3932160 | tf_op jit(solution)/shard_map/all_to_all | solution.py:492
  162.2 13.5 %copy-start.6 = (s32[256,2]{1,0:T(8,128)S(1)}, s32[256,2]{1,0:T(8,128)}, u32[]{:S(2)}) copy-start(s32[256,2]{1,0:T(8,128)} %copy.31.routes_ref) | copy-start | bytes 6148
  162.2 13.5 %copy-start.37 = (s32[256,2]{1,0:T(8,128)S(1)}, s32[256,2]{1,0:T(8,128)}, u32[]{:S(2)}) copy-start(s32[256,2]{1,0:T(8,128)} %copy.28) | copy-start | bytes 6148
  162.2 13.5 %copy-start.8 = (bf16[64,1408]{1,0:T(8,128)(2,1)S(1)}, bf16[64,1408]{1,0:T(8,128)(2,1)}, u32[]{:S(2)}) copy-start(bf16[64,1408]{1,0:T(8,128)(2,1)} %copy-done.7) | copy-start | bytes 540676
  162.2 13.5 %copy-start.10 = (bf16[64,1408]{1,0:T(8,128)(2,1)S(1)}, bf16[64,1408]{1,0:T(8,128)(2,1)}, u32[]{:S(2)}) copy-start(bf16[64,1408]{1,0:T(8,128)(2,1)} %copy-done.9) | copy-start | bytes 540676
  162.2 13.5 %copy-start.12 = (bf16[64,1408]{1,0:T(8,128)(2,1)S(1)}, bf16[64,1408]{1,0:T(8,128)(2,1)}, u32[]{:S(2)}) copy-start(bf16[64,1408]{1,0:T(8,128)(2,1)} %copy-done.11) | copy-start | bytes 540676
  162.2 13.5 %copy-start.14 = (bf16[64,1408]{1,0:T(8,128)(2,1)S(1)}, bf16[64,1408]{1,0:T(8,128)(2,1)}, u32[]{:S(2)}) copy-start(bf16[64,1408]{1,0:T(8,128)(2,1)} %copy-done.13) | copy-start | bytes 540676
  162.2 13.5 %copy-start.34 = (f32[64,1280]{1,0:T(8,128)S(1)}, f32[64,1280]{1,0:T(8,128)}, u32[]{:S(2)}) copy-start(f32[64,1280]{1,0:T(8,128)} %copy-done.33) | copy-start | bytes 983044
  172.1 11.9 %copy-start.25 = (f32[256,256]{1,0:T(8,128)S(1)}, f32[256,256]{1,0:T(8,128)}, u32[]{:S(2)}) copy-start(f32[256,256]{1,0:T(8,128)} %copy-done.24) | copy-start | bytes 786436
  172.1 11.9 %all-to-all-start.3 = ((bf16[8,96,256]{2,1,0:T(8,128)(2,1)}), bf16[8,96,256]{2,1,0:T(8,128)(2,1)S(1)}, u32[]{:S(2)}, u32[]{:S(2)}) async-start(bf16[8,96,256]{2,1,0:T(8,128)(2,1)} %bitcast.71), calls=%async_computation.3 | async-start | bytes 786432 | tf_op jit(solution)/shard_map/all_to_all | solution.py:492
  179.3 11.6 %collective-permute-start.10 = (bf16[64,1280]{1,0:T(8,128)(2,1)S(1)}, bf16[64,1280]{1,0:T(8,128)(2,1)S(1)}, u32[]{:S(2)}, u32[]{:S(2)}) collective-permute-start(bf16[64,1280]{1,0:T(8,128)(2,1)S(1)} %get-tuple-element.40), channel_id=1, source_target_pairs={{0,2},{1,3},{2,0},{3,1},{4,6},{5,7},{6,4},{7,5},{8,10},{9,11},{10,... | collective-permute-start | bytes 491528 | tf_op jit(solution)/shard_map/ppermute | solution.py:485
  180.9 15.4 %collective-permute-start.11 = (bf16[64,1280]{1,0:T(8,128)(2,1)S(1)}, bf16[64,1280]{1,0:T(8,128)(2,1)S(1)}, u32[]{:S(2)}, u32[]{:S(2)}) collective-permute-start(bf16[64,1280]{1,0:T(8,128)(2,1)S(1)} %get-tuple-element.41), channel_id=1, source_target_pairs={{0,3},{1,0},{2,1},{3,2},{4,7},{5,4},{6,5},{7,6},{8,11},{9,8},{10,9... | collective-permute-start | bytes 491528 | tf_op jit(solution)/shard_map/ppermute | solution.py:485
  182.3 14.1 %collective-permute-start.9 = (bf16[64,1280]{1,0:T(8,128)(2,1)S(1)}, bf16[64,1280]{1,0:T(8,128)(2,1)S(1)}, u32[]{:S(2)}, u32[]{:S(2)}) collective-permute-start(bf16[64,1280]{1,0:T(8,128)(2,1)S(1)} %get-tuple-element.39), channel_id=1, source_target_pairs={{0,1},{1,2},{2,3},{3,0},{4,5},{5,6},{6,7},{7,4},{8,9},{9,10},{10,1... | collective-permute-start | bytes 491528 | tf_op jit(solution)/shard_map/ppermute | solution.py:485
  184.6 12.5 %collective-permute-start.15 = (bf16[64,256]{1,0:T(8,128)(2,1)S(1)}, bf16[64,256]{1,0:T(8,128)(2,1)S(1)}, u32[]{:S(2)}, u32[]{:S(2)}) collective-permute-start(bf16[64,256]{1,0:T(8,128)(2,1)S(1)} %get-tuple-element.44), channel_id=1, source_target_pairs={{0,1},{1,2},{2,3},{3,0},{4,5},{5,6},{6,7},{7,4},{8,9},{9,10},{10,1... | collective-permute-start | bytes 98312 | tf_op jit(solution)/shard_map/ppermute | solution.py:485
  185.3 14.3 %collective-permute-start.16 = (bf16[64,256]{1,0:T(8,128)(2,1)S(1)}, bf16[64,256]{1,0:T(8,128)(2,1)S(1)}, u32[]{:S(2)}, u32[]{:S(2)}) collective-permute-start(bf16[64,256]{1,0:T(8,128)(2,1)S(1)} %get-tuple-element.45), channel_id=1, source_target_pairs={{0,2},{1,3},{2,0},{3,1},{4,6},{5,7},{6,4},{7,5},{8,10},{9,11},{10,... | collective-permute-start | bytes 98312 | tf_op jit(solution)/shard_map/ppermute | solution.py:485
  190.9 8.7 %collective-permute-start.17 = (bf16[64,256]{1,0:T(8,128)(2,1)S(1)}, bf16[64,256]{1,0:T(8,128)(2,1)S(1)}, u32[]{:S(2)}, u32[]{:S(2)}) collective-permute-start(bf16[64,256]{1,0:T(8,128)(2,1)S(1)} %get-tuple-element.46), channel_id=1, source_target_pairs={{0,3},{1,0},{2,1},{3,2},{4,7},{5,4},{6,5},{7,6},{8,11},{9,8},{10,9... | collective-permute-start | bytes 98312 | tf_op jit(solution)/shard_map/ppermute | solution.py:485
  (18 other events, 21.1 us)

commit v4 on v3

--- a/solution.py
+++ b/solution.py
@@ -83,7 +83,8 @@
 
 def attention_kernel(
     share,
-    scalars,
+    lengths,
+    places,
     hidden_ref,
     gain_ref,
     w_ref,
@@ -100,7 +101,9 @@
     blocks = tokens // share
     rows_here = kc_ref.shape[0]
     heads = rows_here // HEAD
-    length, shift = scalars[0], scalars[1] * share
+    length = lengths[0]
+    lead = lax.rem(places[0] + 1, blocks)
+    shift = lead * share
 
     @pl.when(pl.program_id(0) == 0)
     def _():
@@ -108,7 +111,7 @@
         for k in range(0, blocks, 2):
             pair = []
             for i in range(2):
-                start = pl.multiple_of(lax.rem(scalars[1] + k + i, blocks) * share, share)
+                start = pl.multiple_of(lax.rem(lead + k + i, blocks) * share, share)
                 rows = hidden_ref[pl.ds(start, share), :].astype(jnp.float32)
                 pair.append(normalize(rows, gain_ref[...]))
             normed[:, k * share : (k + 2) * share] = jnp.concatenate(pair, axis=0).T.astype(
@@ -167,7 +170,7 @@
         for i, out_ref in enumerate(out_refs):
             ahead = (i + 1) % blocks
             first = width - blocks * SLICE
-            place = lax.rem(scalars[1] + i, blocks) * SLICE + first
+            place = lax.rem(lead + i, blocks) * SLICE + first
             lanes = pl.ds(pl.multiple_of(place, SLICE), SLICE)
             out_ref[:, :first] = total[i * share : (i + 1) * share, :first].astype(out_ref.dtype)
             for j in range(blocks):
@@ -414,6 +417,7 @@
         out_specs=pl.BlockSpec(memory_space=pl.ANY),
         out_shape=jax.ShapeDtypeStruct(value.shape, value.dtype),
         input_output_aliases={0: 0},
+        compiler_params=pltpu.CompilerParams(vmem_limit_bytes=1024 * 1024),
         cost_estimate=cost,
     )(value, *arrivals)
 
@@ -522,8 +526,7 @@
     places = jnp.sum(jnp.where(named, slot[:, None, :], 0), axis=2) + rolled * (copies * CAP)
 
     length = cache_lengths[0]
-    scalars = jnp.stack([length, (me_tp + 1) % tp]).astype(jnp.int32)
-    positions = length + (token_ids + scalars[1] * share) % token_count
+    positions = length + (token_ids + (me_tp + 1) * share) % token_count
     positions = positions.astype(jnp.float32)
     half = HEAD // 2
     frequency = jnp.exp(jnp.arange(half, dtype=jnp.float32) * (-2.0 * math.log(10000.0) / HEAD))
@@ -536,20 +539,20 @@
     group = 3 if local_heads % 3 == 0 else 1
 
     def whole(*shape):
-        return pl.BlockSpec(shape, lambda h, s: (0,) * len(shape))
+        return pl.BlockSpec(shape, lambda h, *_: (0,) * len(shape))
 
     def head_rows(n):
-        return pl.BlockSpec((group * HEAD, n), lambda h, s: (h, 0))
+        return pl.BlockSpec((group * HEAD, n), lambda h, *_: (h, 0))
 
     *sent, own_partial = pl.pallas_call(
         functools.partial(attention_kernel, share),
         grid_spec=pltpu.PrefetchScalarGridSpec(
-            num_scalar_prefetch=1,
+            num_scalar_prefetch=2,
             grid=(local_heads // group,),
             in_specs=[
                 whole(token_count, model_width),
                 whole(model_width),
-                pl.BlockSpec((3, group * HEAD, model_width), lambda h, s: (0, h, 0)),
+                pl.BlockSpec((3, group * HEAD, model_width), lambda h, *_: (0, h, 0)),
                 whole(half, token_count),
                 whole(half, token_count),
                 head_rows(cache_len),
@@ -573,7 +576,8 @@
             transcendentals=token_count * (cache_len + token_count) * local_heads,
         ),
     )(
-        scalars,
+        cache_lengths,
+        me_tp.reshape(1),
         hidden_in,
         attn_norm,
         w_t,
@@ -627,7 +631,6 @@
         [slice_terms[0]] + [to_block(slice_terms[k], k) for k in range(1, tp)]
     )
 
-    slice_back = exchanged(after(slice_sum, first_back))
     kinds = [jnp.bfloat16] * tp
     first_out, *first_shares = combine(
         model_width,
@@ -639,6 +642,7 @@
         messages,
         [jnp.float32, *kinds[1:]],
     )
+    slice_back = exchanged(after(slice_sum, first_shares[-1]))
     first_shares = [to_block(piece, k + 1) for k, piece in enumerate(first_shares)]
     first_out = after(first_out, *first_shares, cost=AHEAD)
     slice_outs = combine(

time: 205 us -> 195 us (0.951)
  local copies, waits for them, and re-layouts: 19.8 us -> 9.55 us
  waiting for transfers between devices: 79.2 us -> 73.7 us
  starting transfers between devices: 49.4 us -> 54.2 us
  Pallas kernels: 25.9 us -> 28.5 us
    unnamed x89 -> x63, local copies, waits for them, and re-layouts: 15.8 us -> 6.21 us
    ppermute x12, starting transfers between devices: 23.5 us -> 28.2 us  [to_block(): return lax.ppermute(array, 'tp', [(i, (i + k) % tp) for i in range(tp)])]
    ppermute x12, waiting for transfers between devices: 34.4 us -> 29.7 us  [to_block(): return lax.ppermute(array, 'tp', [(i, (i + k) % tp) for i in range(tp)])]
    all_to_all x4, waiting for transfers between devices: 9.52 us -> 7.04 us  [exchanged(): lax.all_to_all(blocks, 'req', split_axis=0, concat_axis=0, tiled=True)]
  transfers between devices with their start and end apart: 22 -> 22, of which waited for: 11 -> 12; matrix products, arithmetic and copies ran while one was open for 7% -> 6% of each run, Pallas kernels for 1% -> 1%
where the time goes in v4:
time: 195 us; the launch traced here: 194 us
  waiting for transfers between devices  73.7 us (38%)
  starting transfers between devices  54.2 us (28%)
  Pallas kernels  28.5 us (15%)
  matrix products  23.9 us (12%)
  local copies, waits for them, and re-layouts  9.55 us (5%)
  other arithmetic  3.14 us (2%)
    ppermute x6, waiting for transfers between devices, from_block(): return lax.ppermute(array, 'tp', [(i, (i - k) % tp) for i in range(tp)])  37 us
    ppermute x12, waiting for transfers between devices, to_block(): return lax.ppermute(array, 'tp', [(i, (i + k) % tp) for i in range(tp)])  29.7 us
    ppermute x12, starting transfers between devices, to_block(): return lax.ppermute(array, 'tp', [(i, (i + k) % tp) for i in range(tp)])  28.2 us
    pallas_call x1, Pallas kernels, per_device(): pl.pallas_call(functools.partial(attention_kernel, share), grid_spec=pltp...  19.3 us
    all_to_all x4, starting transfers between devices, exchanged(): lax.all_to_all(blocks, 'req', split_axis=0, concat_axis=0, tiled=True)  14.7 us
    ppermute x6, starting transfers between devices, from_block(): return lax.ppermute(array, 'tp', [(i, (i - k) % tp) for i in range(tp)])  11.3 us
    dot_general x1, matrix products, per_device(): jnp.dot(token_rows, expert_gate[0], preferred_element_type=jnp.float32)  7.65 us
    all_to_all x4, waiting for transfers between devices, exchanged(): lax.all_to_all(blocks, 'req', split_axis=0, concat_axis=0, tiled=True)  7.04 us
  transfers between devices with their start and end apart: 22, of which 12 were waited for; matrix products, arithmetic and copies ran while one was open for 6% of the time, Pallas kernels for 1%

profile of v4, /device:TPU:0, one launch (start us, length us, event | category | flops | bytes accessed | tf_op | source)
XLA Modules:
  0.0 194.1 jit_solution(10159924524191172863)
XLA Ops:
  0.7 0.8 multiply_sine_fusion
  1.5 19.3 %shard_map.127 = (bf16[64,2304]{1,0:T(8,128)(2,1)}, bf16[64,2304]{1,0:T(8,128)(2,1)}, bf16[64,2304]{1,0:T(8,128)(2,1)}, bf16[64,2304]{1,0:T(8,128)(2,1)}) custom-call(s32[1]{0:T(128)} %copy.38.lengths, s32[1]{0:T(128)} %bitcast.places.scalars, bf16[256,2304]{1,0:T(8,128)(2,1)} %refs_4_.1, f32[2304]{0:T(1024)} %gain_ref.1, bf16[3,576,2304]{2,1,0:T(8,128)(2,1)} %bitcast.70, ...), custom_call_target="tpu_custom_call" | custom-call | flops 4076863488 | bytes 15335424 | tf_op jit(solution)/shard_map/pallas_call | solution.py:547
  20.8 3.1 %collective-permute-start = (bf16[64,2304]{1,0:T(8,128)(2,1)}, bf16[64,2304]{1,0:T(8,128)(2,1)S(1)}, u32[]{:S(2)}, u32[]{:S(2)}) collective-permute-start(bf16[64,2304]{1,0:T(8,128)(2,1)} %get-tuple-element.27), channel_id=1, source_target_pairs={{0,1},{1,2},{2,3},{3,0},{4,5},{5,6},{6,7},{7,4},{8,9},{9,10},{10,1... | collective-permute-start | bytes 884744 | tf_op jit(solution)/shard_map/ppermute | solution.py:489
  23.9 2.6 %collective-permute-start.1 = (bf16[64,2304]{1,0:T(8,128)(2,1)}, bf16[64,2304]{1,0:T(8,128)(2,1)S(1)}, u32[]{:S(2)}, u32[]{:S(2)}) collective-permute-start(bf16[64,2304]{1,0:T(8,128)(2,1)} %get-tuple-element.28), channel_id=1, source_target_pairs={{0,2},{1,3},{2,0},{3,1},{4,6},{5,7},{6,4},{7,5},{8,10},{9,11},{10,... | collective-permute-start | bytes 884744 | tf_op jit(solution)/shard_map/ppermute | solution.py:489
  26.5 1.4 collective-permute-start.2
  28.7 2.0 %constant_dynamic-slice_fusion.2 = (bf16[1,1440,256]{2,1,0:T(8,128)(2,1)S(1)}, bf16[1,1440,256]{2,1,0:T(8,128)(2,1)S(1)}, bf16[1,1440,256]{2,1,0:T(8,128)(2,1)S(1)}, bf16[1,1440,256]{2,1,0:T(8,128)(2,1)S(1)}) fusion(bf16[1,1440,2304]{2,1,0:T(8,128)(2,1)} %param.25, s32[]{:T(128)S(6)} %select_n.58, s32[]{:T(128)S(6)} %select_n.60, s32[]{:T(128)S(6)} %select_n.64, ...), kind=kLoop, calls=%fused_computation.42 | loop fusion | bytes 5898256 | tf_op jit(solution)/shard_map/dynamic_slice | solution.py:600
  30.8 1.8 pad_maximum_fusion
  32.5 1.5 collective-permute-done.refs_1_
  34.1 11.8 %collective-permute-done.1.refs_2_ = bf16[64,2304]{1,0:T(8,128)(2,1)S(1)} collective-permute-done((bf16[64,2304]{1,0:T(8,128)(2,1)}, bf16[64,2304]{1,0:T(8,128)(2,1)S(1)}, u32[]{:S(2)}, u32[]{:S(2)}) %collective-permute-start.1) | collective-permute-done | bytes 294944 | tf_op jit(solution)/shard_map/ppermute | solution.py:489
  45.9 1.2 shard_map.128
  47.8 7.8 %collective-permute-start.3 = (bf16[64,1408]{1,0:T(8,128)(2,1)S(1)}, bf16[64,1408]{1,0:T(8,128)(2,1)S(1)}, u32[]{:S(2)}, u32[]{:S(2)}) collective-permute-start(bf16[64,1408]{1,0:T(8,128)(2,1)S(1)} %get-tuple-element.31), channel_id=1, source_target_pairs={{0,3},{1,0},{2,1},{3,2},{4,7},{5,4},{6,5},{7,6},{8,11},{9,8},{10,9... | collective-permute-start | bytes 540680 | tf_op jit(solution)/shard_map/ppermute | solution.py:492
  56.2 1.0 convolution_convert_fusion.1
  57.2 3.7 %all-to-all-start = ((bf16[8,96,256]{2,1,0:T(8,128)(2,1)}), bf16[8,96,256]{2,1,0:T(8,128)(2,1)S(1)}, u32[]{:S(2)}, u32[]{:S(2)}) async-start(bf16[8,96,256]{2,1,0:T(8,128)(2,1)} %bitcast.10), calls=%async_computation | async-start | bytes 786432 | tf_op jit(solution)/shard_map/all_to_all | solution.py:496
  61.2 10.9 %collective-permute-done.4.refs_2_ = bf16[64,1408]{1,0:T(8,128)(2,1)S(1)} collective-permute-done((bf16[64,1408]{1,0:T(8,128)(2,1)S(1)}, bf16[64,1408]{1,0:T(8,128)(2,1)S(1)}, u32[]{:S(2)}, u32[]{:S(2)}) %collective-permute-start.4) | collective-permute-done | bytes 180256 | tf_op jit(solution)/shard_map/ppermute | solution.py:492
  72.2 0.8 collective-permute-start.6
  73.7 1.4 collective-permute-start.8
  75.1 2.0 %convolution_convert_fusion = bf16[768,1280]{1,0:T(8,128)(2,1)} fusion(pred[768,256]{1,0:T(32,128)(4,1)S(1)} %bitcast_compare_fusion, bf16[256,1280]{1,0:T(8,128)(2,1)S(1)} %pad_maximum_fusion.1), kind=kOutput, calls=%fused_computation.8 | convolution fusion | flops 504299520 | bytes 2818048 | tf_op jit(solution)/shard_map/dot_general | solution.py:500
  77.1 3.8 %all-to-all-start.1 = ((bf16[8,96,1280]{2,1,0:T(8,128)(2,1)}), bf16[8,96,1280]{2,1,0:T(8,128)(2,1)S(1)}, u32[]{:S(2)}, u32[]{:S(2)}) async-start(bf16[8,96,1280]{2,1,0:T(8,128)(2,1)} %bitcast.71), calls=%async_computation.1 | async-start | bytes 3932160 | tf_op jit(solution)/shard_map/all_to_all | solution.py:496
  80.9 3.0 %collective-permute-done.6.__1_.refs_1_ = bf16[768,256]{1,0:T(8,128)(2,1)S(1)} collective-permute-done((bf16[768,256]{1,0:T(8,128)(2,1)S(1)}, bf16[768,256]{1,0:T(8,128)(2,1)S(1)}, u32[]{:S(2)}, u32[]{:S(2)}) %collective-permute-start.6) | collective-permute-done | bytes 393248 | tf_op jit(solution)/shard_map/ppermute | solution.py:492
  83.9 23.1 %collective-permute-done.7.__2_.refs_2_ = bf16[768,256]{1,0:T(8,128)(2,1)S(1)} collective-permute-done((bf16[768,256]{1,0:T(8,128)(2,1)S(1)}, bf16[768,256]{1,0:T(8,128)(2,1)S(1)}, u32[]{:S(2)}, u32[]{:S(2)}) %collective-permute-start.7) | collective-permute-done | bytes 393248 | tf_op jit(solution)/shard_map/ppermute | solution.py:492
  107.0 3.3 %shard_map.130 = bf16[768,2304]{1,0:T(8,128)(2,1)S(1)} custom-call(s32[1]{0:T(128)} %bitcast.places.scalars, bf16[768,1280]{1,0:T(8,128)(2,1)S(1)} %bitcast.62, bf16[768,256]{1,0:T(8,128)(2,1)S(1)} %shard_map.129.refs_0_, bf16[768,256]{1,0:T(8,128)(2,1)S(1)} %collective-permute-done.6.__1_.refs_1_, bf16[768,256]{1,0:T(8,128)(2,1)S(1)} %collective-permute-done.7.__2_.refs_2_, ...), custom_call_target="tpu_custom_call" | custom-call | flops 14155776 | bytes 7077888 | tf_op jit(solution)/shard_map/pallas_call | solution.py:299
  110.4 7.6 %fusion.2 = f32[768,1440]{0,1:T(8,128)S(1)} fusion(bf16[768,2304]{1,0:T(8,128)(2,1)S(1)} %shard_map.130, bf16[1,2304,1440]{1,2,0:T(8,128)(2,1)} %param.23), kind=kOutput, calls=%fused_computation.2 | convolution fusion | flops 5096079360 | bytes 14598144 | tf_op jit(solution)/shard_map/dot_general | solution.py:618
  118.1 5.9 %multiply_convert_fusion = bf16[768,1440]{0,1:T(8,128)(2,1)S(1)} fusion(f32[768,1440]{0,1:T(8,128)S(1)} %fusion.2, bf16[768,2304]{1,0:T(8,128)(2,1)S(1)} %shard_map.130, bf16[1,2304,1440]{1,2,0:T(8,128)(2,1)S(1)} %bitcast.78), kind=kOutput, calls=%fused_computation.4 | convolution fusion | flops 5102714880 | bytes 16809984 | tf_op jit(solution)/shard_map/dot_general | solution.py:619
  124.0 2.7 %fusion.15 = bf16[4,768,256]{2,1,0:T(8,128)(2,1)S(1)} fusion(bf16[4,1440,256]{2,1,0:T(8,128)(2,1)S(1)} %copy-done.24, bf16[768,1440]{0,1:T(8,128)(2,1)S(1)} %multiply_convert_fusion), kind=kOutput, calls=%fused_computation.14 | convolution fusion | flops 2265710592 | bytes 6733824 | tf_op jit(solution)/shard_map/rh,khs->krs/dot_general | solution.py:627
  126.7 1.0 slice_bitcast_fusion
  128.0 1.8 collective-permute-start.13
  129.8 2.9 %collective-permute-start.14 = (bf16[768,256]{1,0:T(8,128)(2,1)}, bf16[768,256]{1,0:T(8,128)(2,1)}, u32[]{:S(2)}, u32[]{:S(2)}) collective-permute-start(bf16[768,256]{1,0:T(8,128)(2,1)} %get-tuple-element.51), channel_id=1, source_target_pairs={{0,3},{1,0},{2,1},{3,2},{4,7},{5,4},{6,5},{7,6},{8,11},{9,8},{10,9... | collective-permute-start | bytes 1179656 | tf_op jit(solution)/shard_map/ppermute | solution.py:489
  132.8 4.5 %fusion.7 = bf16[768,1280]{1,0:T(8,128)(2,1)} fusion(bf16[768,1440]{0,1:T(8,128)(2,1)S(1)} %multiply_convert_fusion, bf16[1,1440,2304]{2,1,0:T(8,128)(2,1)S(1)} %bitcast.76), kind=kOutput, calls=%fused_computation.9 | convolution fusion | flops 2832138240 | bytes 7864320 | tf_op jit(solution)/shard_map/dot_general | solution.py:623
  137.3 3.7 %all-to-all-start.2 = ((bf16[8,96,1280]{2,1,0:T(8,128)(2,1)}), bf16[8,96,1280]{2,1,0:T(8,128)(2,1)S(1)}, u32[]{:S(2)}, u32[]{:S(2)}) async-start(bf16[8,96,1280]{2,1,0:T(8,128)(2,1)} %bitcast.74), calls=%async_computation.2 | async-start | bytes 3932160 | tf_op jit(solution)/shard_map/all_to_all | solution.py:496
  141.0 1.0 collective-permute-done.12.refs_1_
  141.9 0.8 copy-done.16
  142.7 13.2 %collective-permute-done.13.refs_2_ = bf16[768,256]{1,0:T(8,128)(2,1)S(1)} collective-permute-done((bf16[768,256]{1,0:T(8,128)(2,1)}, bf16[768,256]{1,0:T(8,128)(2,1)S(1)}, u32[]{:S(2)}, u32[]{:S(2)}) %collective-permute-start.13) | collective-permute-done | bytes 393248 | tf_op jit(solution)/shard_map/ppermute | solution.py:489
  155.9 0.8 copy-done.18
  156.7 1.0 copy-done.17
  157.7 1.0 copy-done.19
  158.7 2.0 %shard_map.133.__0_ = bf16[768,256]{1,0:T(8,128)(2,1)} custom-call(bf16[768,256]{1,0:T(8,128)(2,1)S(1)} %get-tuple-element.54.refs_0_, bf16[768,256]{1,0:T(8,128)(2,1)S(1)} %copy-done.17, bf16[768,256]{1,0:T(8,128)(2,1)S(1)} %copy-done.19, bf16[768,256]{1,0:T(8,128)(2,1)} %collective-permute-done.14.refs_3_), custom_call_target="tpu_custom_call" | custom-call | flops 137438953472 | bytes 1048576 | tf_op jit(solution)/shard_map/pallas_call | solution.py:398
  160.7 5.5 %all-to-all-done.2 = bf16[8,96,1280]{2,1,0:T(8,128)(2,1)S(1)} async-done(((bf16[8,96,1280]{2,1,0:T(8,128)(2,1)}), bf16[8,96,1280]{2,1,0:T(8,128)(2,1)S(1)}, u32[]{:S(2)}, u32[]{:S(2)}) %all-to-all-start.2) | async-done | bytes 1966112 | tf_op jit(solution)/shard_map/all_to_all | solution.py:496
  166.3 1.0 copy-done.21
  167.2 1.2 shard_map.131
  169.3 3.5 %all-to-all-start.3 = ((bf16[8,96,256]{2,1,0:T(8,128)(2,1)}), bf16[8,96,256]{2,1,0:T(8,128)(2,1)S(1)}, u32[]{:S(2)}, u32[]{:S(2)}) async-start(bf16[8,96,256]{2,1,0:T(8,128)(2,1)} %bitcast.25), calls=%async_computation.3 | async-start | bytes 786432 | tf_op jit(solution)/shard_map/all_to_all | solution.py:496
  172.8 2.6 %collective-permute-start.10 = (bf16[64,1280]{1,0:T(8,128)(2,1)}, bf16[64,1280]{1,0:T(8,128)(2,1)S(1)}, u32[]{:S(2)}, u32[]{:S(2)}) collective-permute-start(bf16[64,1280]{1,0:T(8,128)(2,1)} %copy-done.23), channel_id=1, source_target_pairs={{0,2},{1,3},{2,0},{3,1},{4,6},{5,7},{6,4},{7,5},{8,10},{9,11},{10,... | collective-permute-start | bytes 491528 | tf_op jit(solution)/shard_map/ppermute | solution.py:489
  175.4 3.6 %collective-permute-start.11 = (bf16[64,1280]{1,0:T(8,128)(2,1)}, bf16[64,1280]{1,0:T(8,128)(2,1)S(1)}, u32[]{:S(2)}, u32[]{:S(2)}) collective-permute-start(bf16[64,1280]{1,0:T(8,128)(2,1)} %copy-done.14), channel_id=1, source_target_pairs={{0,3},{1,0},{2,1},{3,2},{4,7},{5,4},{6,5},{7,6},{8,11},{9,8},{10,9... | collective-permute-start | bytes 491528 | tf_op jit(solution)/shard_map/ppermute | solution.py:489
  179.5 1.5 all-to-all-done.3
  181.7 3.8 %collective-permute-start.15 = (bf16[64,256]{1,0:T(8,128)(2,1)S(1)}, bf16[64,256]{1,0:T(8,128)(2,1)S(1)}, u32[]{:S(2)}, u32[]{:S(2)}) collective-permute-start(bf16[64,256]{1,0:T(8,128)(2,1)S(1)} %get-tuple-element.44), channel_id=1, source_target_pairs={{0,1},{1,2},{2,3},{3,0},{4,5},{5,6},{6,7},{7,4},{8,9},{9,10},{10,1... | collective-permute-start | bytes 98312 | tf_op jit(solution)/shard_map/ppermute | solution.py:489
  185.4 3.1 %collective-permute-start.16 = (bf16[64,256]{1,0:T(8,128)(2,1)S(1)}, bf16[64,256]{1,0:T(8,128)(2,1)S(1)}, u32[]{:S(2)}, u32[]{:S(2)}) collective-permute-start(bf16[64,256]{1,0:T(8,128)(2,1)S(1)} %get-tuple-element.45), channel_id=1, source_target_pairs={{0,2},{1,3},{2,0},{3,1},{4,6},{5,7},{6,4},{7,5},{8,10},{9,11},{10,... | collective-permute-start | bytes 98312 | tf_op jit(solution)/shard_map/ppermute | solution.py:489
  188.5 2.6 %collective-permute-start.17 = (bf16[64,256]{1,0:T(8,128)(2,1)S(1)}, bf16[64,256]{1,0:T(8,128)(2,1)S(1)}, u32[]{:S(2)}, u32[]{:S(2)}) collective-permute-start(bf16[64,256]{1,0:T(8,128)(2,1)S(1)} %get-tuple-element.46), channel_id=1, source_target_pairs={{0,3},{1,0},{2,1},{3,2},{4,7},{5,4},{6,5},{7,6},{8,11},{9,8},{10,9... | collective-permute-start | bytes 98312 | tf_op jit(solution)/shard_map/ppermute | solution.py:489
  192.1 1.2 collective-permute-done.16.refs_6_
  193.3 0.8 shard_map.136
  (100 shorter events, 6.4 us)
Async XLA Ops:
  1.5 26.3 %copy-start.26 = (s32[256,2]{0,1:T(2,128)S(1)}, s32[256,2]{0,1:T(2,128)}, u32[]{:S(2)}) copy-start(s32[256,2]{0,1:T(2,128)} %param.22) | copy-start | bytes 6148
  1.5 26.7 %copy-start.25 = (f32[2304]{0:T(1024)S(1)}, f32[2304]{0:T(1024)}, u32[]{:S(2)}) copy-start(f32[2304]{0:T(1024)} %param.20) | copy-start | bytes 27652
  20.8 13.3 %collective-permute-start = (bf16[64,2304]{1,0:T(8,128)(2,1)}, bf16[64,2304]{1,0:T(8,128)(2,1)S(1)}, u32[]{:S(2)}, u32[]{:S(2)}) collective-permute-start(bf16[64,2304]{1,0:T(8,128)(2,1)} %get-tuple-element.27), channel_id=1, source_target_pairs={{0,1},{1,2},{2,3},{3,0},{4,5},{5,6},{6,7},{7,4},{8,9},{9,10},{10,1... | collective-permute-start | bytes 884744 | tf_op jit(solution)/shard_map/ppermute | solution.py:489
  23.9 22.0 %collective-permute-start.1 = (bf16[64,2304]{1,0:T(8,128)(2,1)}, bf16[64,2304]{1,0:T(8,128)(2,1)S(1)}, u32[]{:S(2)}, u32[]{:S(2)}) collective-permute-start(bf16[64,2304]{1,0:T(8,128)(2,1)} %get-tuple-element.28), channel_id=1, source_target_pairs={{0,2},{1,3},{2,0},{3,1},{4,6},{5,7},{6,4},{7,5},{8,10},{9,11},{10,... | collective-permute-start | bytes 884744 | tf_op jit(solution)/shard_map/ppermute | solution.py:489
  26.5 19.4 %collective-permute-start.2 = (bf16[64,2304]{1,0:T(8,128)(2,1)}, bf16[64,2304]{1,0:T(8,128)(2,1)S(1)}, u32[]{:S(2)}, u32[]{:S(2)}) collective-permute-start(bf16[64,2304]{1,0:T(8,128)(2,1)} %get-tuple-element.29), channel_id=1, source_target_pairs={{0,3},{1,0},{2,1},{3,2},{4,7},{5,4},{6,5},{7,6},{8,11},{9,8},{10,9... | collective-permute-start | bytes 884744 | tf_op jit(solution)/shard_map/ppermute | solution.py:489
  28.5 46.6 %copy-start.1 = (s32[256,2]{1,0:T(8,128)}, s32[256,2]{1,0:T(8,128)S(1)}, u32[]{:S(2)}) copy-start(s32[256,2]{1,0:T(8,128)S(1)} %copy.31.routes_ref) | copy-start | bytes 6148
  30.7 15.2 %copy-start = (bf16[256,2304]{1,0:T(8,128)(2,1)S(1)}, bf16[256,2304]{1,0:T(8,128)(2,1)}, u32[]{:S(2)}) copy-start(bf16[256,2304]{1,0:T(8,128)(2,1)} %refs_4_.1) | copy-start | bytes 3538948
  30.7 15.2 %copy-start.11 = (bf16[64,2304]{1,0:T(8,128)(2,1)S(1)}, bf16[64,2304]{1,0:T(8,128)(2,1)}, u32[]{:S(2)}) copy-start(bf16[64,2304]{1,0:T(8,128)(2,1)} %get-tuple-element.26.refs_0_) | copy-start | bytes 884740
  30.8 15.1 %copy-start.15 = (bf16[2304,8]{0,1:T(8,128)(2,1)S(1)}, bf16[2304,8]{0,1:T(8,128)(2,1)}, u32[]{:S(2)}) copy-start(bf16[2304,8]{0,1:T(8,128)(2,1)} %param.21) | copy-start | bytes 110596
  47.8 9.4 %copy-start.20 = (f32[64,1280]{1,0:T(8,128)}, f32[64,1280]{1,0:T(8,128)S(1)}, u32[]{:S(2)}) copy-start(f32[64,1280]{1,0:T(8,128)S(1)} %get-tuple-element.37.base_ref) | copy-start | bytes 983044
  47.8 29.3 %copy-start.3 = (bf16[64,1408]{1,0:T(8,128)(2,1)}, bf16[64,1408]{1,0:T(8,128)(2,1)S(1)}, u32[]{:S(2)}) copy-start(bf16[64,1408]{1,0:T(8,128)(2,1)S(1)} %get-tuple-element.30.refs_0_) | copy-start | bytes 540676
  47.8 13.3 %collective-permute-start.3 = (bf16[64,1408]{1,0:T(8,128)(2,1)S(1)}, bf16[64,1408]{1,0:T(8,128)(2,1)S(1)}, u32[]{:S(2)}, u32[]{:S(2)}) collective-permute-start(bf16[64,1408]{1,0:T(8,128)(2,1)S(1)} %get-tuple-element.31), channel_id=1, source_target_pairs={{0,3},{1,0},{2,1},{3,2},{4,7},{5,4},{6,5},{7,6},{8,11},{9,8},{10,9... | collective-permute-start | bytes 540680 | tf_op jit(solution)/shard_map/ppermute | solution.py:492
  55.6 16.5 %collective-permute-start.4 = (bf16[64,1408]{1,0:T(8,128)(2,1)S(1)}, bf16[64,1408]{1,0:T(8,128)(2,1)S(1)}, u32[]{:S(2)}, u32[]{:S(2)}) collective-permute-start(bf16[64,1408]{1,0:T(8,128)(2,1)S(1)} %get-tuple-element.32), channel_id=1, source_target_pairs={{0,2},{1,3},{2,0},{3,1},{4,6},{5,7},{6,4},{7,5},{8,10},{9,11},{10,... | collective-permute-start | bytes 540680 | tf_op jit(solution)/shard_map/ppermute | solution.py:492
  56.1 16.1 %collective-permute-start.5 = (bf16[64,1408]{1,0:T(8,128)(2,1)S(1)}, bf16[64,1408]{1,0:T(8,128)(2,1)S(1)}, u32[]{:S(2)}, u32[]{:S(2)}) collective-permute-start(bf16[64,1408]{1,0:T(8,128)(2,1)S(1)} %get-tuple-element.33), channel_id=1, source_target_pairs={{0,1},{1,2},{2,3},{3,0},{4,5},{5,6},{6,7},{7,4},{8,9},{9,10},{10,1... | collective-permute-start | bytes 540680 | tf_op jit(solution)/shard_map/ppermute | solution.py:492
  57.2 15.0 %all-to-all-start = ((bf16[8,96,256]{2,1,0:T(8,128)(2,1)}), bf16[8,96,256]{2,1,0:T(8,128)(2,1)S(1)}, u32[]{:S(2)}, u32[]{:S(2)}) async-start(bf16[8,96,256]{2,1,0:T(8,128)(2,1)} %bitcast.10), calls=%async_computation | async-start | bytes 786432 | tf_op jit(solution)/shard_map/all_to_all | solution.py:496
  61.1 16.0 %copy-start.5 = (bf16[64,1408]{1,0:T(8,128)(2,1)}, bf16[64,1408]{1,0:T(8,128)(2,1)S(1)}, u32[]{:S(2)}) copy-start(bf16[64,1408]{1,0:T(8,128)(2,1)S(1)} %collective-permute-done.3.refs_1_) | copy-start | bytes 540676
  72.1 5.0 %copy-start.7 = (bf16[64,1408]{1,0:T(8,128)(2,1)}, bf16[64,1408]{1,0:T(8,128)(2,1)S(1)}, u32[]{:S(2)}) copy-start(bf16[64,1408]{1,0:T(8,128)(2,1)S(1)} %collective-permute-done.4.refs_2_) | copy-start | bytes 540676
  72.1 5.0 %copy-start.9 = (bf16[64,1408]{1,0:T(8,128)(2,1)}, bf16[64,1408]{1,0:T(8,128)(2,1)S(1)}, u32[]{:S(2)}) copy-start(bf16[64,1408]{1,0:T(8,128)(2,1)S(1)} %collective-permute-done.5.refs_3_) | copy-start | bytes 540676
  72.2 11.7 %collective-permute-start.6 = (bf16[768,256]{1,0:T(8,128)(2,1)S(1)}, bf16[768,256]{1,0:T(8,128)(2,1)S(1)}, u32[]{:S(2)}, u32[]{:S(2)}) collective-permute-start(bf16[768,256]{1,0:T(8,128)(2,1)S(1)} %bitcast.64), channel_id=1, source_target_pairs={{0,3},{1,0},{2,1},{3,2},{4,7},{5,4},{6,5},{7,6},{8,11},{9,8},{10,9... | collective-permute-start | bytes 1179656 | tf_op jit(solution)/shard_map/ppermute | solution.py:492
  73.0 34.0 %collective-permute-start.7 = (bf16[768,256]{1,0:T(8,128)(2,1)S(1)}, bf16[768,256]{1,0:T(8,128)(2,1)S(1)}, u32[]{:S(2)}, u32[]{:S(2)}) collective-permute-start(bf16[768,256]{1,0:T(8,128)(2,1)S(1)} %bitcast.65), channel_id=1, source_target_pairs={{0,2},{1,3},{2,0},{3,1},{4,6},{5,7},{6,4},{7,5},{8,10},{9,11},{10,... | collective-permute-start | bytes 1179656 | tf_op jit(solution)/shard_map/ppermute | solution.py:492
  73.7 33.3 %collective-permute-start.8 = (bf16[768,256]{1,0:T(8,128)(2,1)S(1)}, bf16[768,256]{1,0:T(8,128)(2,1)}, u32[]{:S(2)}, u32[]{:S(2)}) collective-permute-start(bf16[768,256]{1,0:T(8,128)(2,1)S(1)} %bitcast.66), channel_id=1, source_target_pairs={{0,1},{1,2},{2,3},{3,0},{4,5},{5,6},{6,7},{7,4},{8,9},{9,10},{10,1... | collective-permute-start | bytes 1179656 | tf_op jit(solution)/shard_map/ppermute | solution.py:492
  77.1 29.9 %all-to-all-start.1 = ((bf16[8,96,1280]{2,1,0:T(8,128)(2,1)}), bf16[8,96,1280]{2,1,0:T(8,128)(2,1)S(1)}, u32[]{:S(2)}, u32[]{:S(2)}) async-start(bf16[8,96,1280]{2,1,0:T(8,128)(2,1)} %bitcast.71), calls=%async_computation.1 | async-start | bytes 3932160 | tf_op jit(solution)/shard_map/all_to_all | solution.py:496
  107.0 11.0 %slice-start.2 = ((s8[6635520]{0:T(1024)(128)(4,1)}), s8[4194304]{0:T(1024)(128)(4,1)S(1)}, s32[]{:S(2)}) async-start(s8[6635520]{0:T(1024)(128)(4,1)} %bitcast.77), calls=%async_computation.6 | async-start | bytes 8388608
  110.3 7.7 %slice-start.3 = ((s8[6635520]{0:T(1024)(128)(4,1)}), s8[2441216]{0:T(1024)(128)(4,1)S(1)}, s32[]{:S(2)}) async-start(s8[6635520]{0:T(1024)(128)(4,1)} %bitcast.77), calls=%async_computation.7 | async-start | bytes 4882432
  110.4 22.4 %slice-start = ((s8[6635520]{0:T(1024)(128)(4,1)}), s8[4194304]{0:T(1024)(128)(4,1)S(1)}, s32[]{:S(2)}) async-start(s8[6635520]{0:T(1024)(128)(4,1)} %bitcast.75), calls=%async_computation.4 | async-start | bytes 8388608
  118.0 5.9 %copy-start.24 = (bf16[4,1440,256]{2,1,0:T(8,128)(2,1)S(1)}, bf16[4,1440,256]{2,1,0:T(8,128)(2,1)}, u32[]{:S(2)}) copy-start(bf16[4,1440,256]{2,1,0:T(8,128)(2,1)} %pad_maximum_fusion) | copy-start | bytes 8847364
  118.1 14.7 %slice-start.1 = ((s8[6635520]{0:T(1024)(128)(4,1)}), s8[2441216]{0:T(1024)(128)(4,1)S(1)}, s32[]{:S(2)}) async-start(s8[6635520]{0:T(1024)(128)(4,1)} %bitcast.75), calls=%async_computation.5 | async-start | bytes 4882432
  127.8 14.2 %collective-permute-start.12 = (bf16[768,256]{1,0:T(8,128)(2,1)}, bf16[768,256]{1,0:T(8,128)(2,1)S(1)}, u32[]{:S(2)}, u32[]{:S(2)}) collective-permute-start(bf16[768,256]{1,0:T(8,128)(2,1)} %get-tuple-element.53), channel_id=1, source_target_pairs={{0,1},{1,2},{2,3},{3,0},{4,5},{5,6},{6,7},{7,4},{8,9},{9,10},{10,1... | collective-permute-start | bytes 1179656 | tf_op jit(solution)/shard_map/ppermute | solution.py:489
  128.0 27.9 %collective-permute-start.13 = (bf16[768,256]{1,0:T(8,128)(2,1)}, bf16[768,256]{1,0:T(8,128)(2,1)S(1)}, u32[]{:S(2)}, u32[]{:S(2)}) collective-permute-start(bf16[768,256]{1,0:T(8,128)(2,1)} %get-tuple-element.52), channel_id=1, source_target_pairs={{0,2},{1,3},{2,0},{3,1},{4,6},{5,7},{6,4},{7,5},{8,10},{9,11},{10,... | collective-permute-start | bytes 1179656 | tf_op jit(solution)/shard_map/ppermute | solution.py:489
  129.8 26.8 %collective-permute-start.14 = (bf16[768,256]{1,0:T(8,128)(2,1)}, bf16[768,256]{1,0:T(8,128)(2,1)}, u32[]{:S(2)}, u32[]{:S(2)}) collective-permute-start(bf16[768,256]{1,0:T(8,128)(2,1)} %get-tuple-element.51), channel_id=1, source_target_pairs={{0,3},{1,0},{2,1},{3,2},{4,7},{5,4},{6,5},{7,6},{8,11},{9,8},{10,9... | collective-permute-start | bytes 1179656 | tf_op jit(solution)/shard_map/ppermute | solution.py:489
  137.3 29.0 %all-to-all-start.2 = ((bf16[8,96,1280]{2,1,0:T(8,128)(2,1)}), bf16[8,96,1280]{2,1,0:T(8,128)(2,1)S(1)}, u32[]{:S(2)}, u32[]{:S(2)}) async-start(bf16[8,96,1280]{2,1,0:T(8,128)(2,1)} %bitcast.74), calls=%async_computation.2 | async-start | bytes 3932160 | tf_op jit(solution)/shard_map/all_to_all | solution.py:496
  156.7 1.0 copy-start.17
  157.7 1.0 copy-start.19
  158.7 7.6 %copy-start.2 = (s32[256,2]{1,0:T(8,128)S(1)}, s32[256,2]{1,0:T(8,128)}, u32[]{:S(2)}) copy-start(s32[256,2]{1,0:T(8,128)} %copy-done.1) | copy-start | bytes 6148
  158.7 7.6 %copy-start.4 = (bf16[64,1408]{1,0:T(8,128)(2,1)S(1)}, bf16[64,1408]{1,0:T(8,128)(2,1)}, u32[]{:S(2)}) copy-start(bf16[64,1408]{1,0:T(8,128)(2,1)} %copy-done.3) | copy-start | bytes 540676
  158.7 7.6 %copy-start.6 = (bf16[64,1408]{1,0:T(8,128)(2,1)S(1)}, bf16[64,1408]{1,0:T(8,128)(2,1)}, u32[]{:S(2)}) copy-start(bf16[64,1408]{1,0:T(8,128)(2,1)} %copy-done.5) | copy-start | bytes 540676
  158.7 7.6 %copy-start.8 = (bf16[64,1408]{1,0:T(8,128)(2,1)S(1)}, bf16[64,1408]{1,0:T(8,128)(2,1)}, u32[]{:S(2)}) copy-start(bf16[64,1408]{1,0:T(8,128)(2,1)} %copy-done.7) | copy-start | bytes 540676
  158.7 7.6 %copy-start.10 = (bf16[64,1408]{1,0:T(8,128)(2,1)S(1)}, bf16[64,1408]{1,0:T(8,128)(2,1)}, u32[]{:S(2)}) copy-start(bf16[64,1408]{1,0:T(8,128)(2,1)} %copy-done.9) | copy-start | bytes 540676
  160.7 20.3 %copy-start.13 = (f32[256,256]{1,0:T(8,128)S(1)}, f32[256,256]{1,0:T(8,128)}, u32[]{:S(2)}) copy-start(f32[256,256]{1,0:T(8,128)} %copy-done.12) | copy-start | bytes 786436
  166.2 1.0 copy-start.21
  168.5 0.8 copy-start.23
  169.3 11.7 %all-to-all-start.3 = ((bf16[8,96,256]{2,1,0:T(8,128)(2,1)}), bf16[8,96,256]{2,1,0:T(8,128)(2,1)S(1)}, u32[]{:S(2)}, u32[]{:S(2)}) async-start(bf16[8,96,256]{2,1,0:T(8,128)(2,1)} %bitcast.25), calls=%async_computation.3 | async-start | bytes 786432 | tf_op jit(solution)/shard_map/all_to_all | solution.py:496
  172.8 15.8 %collective-permute-start.10 = (bf16[64,1280]{1,0:T(8,128)(2,1)}, bf16[64,1280]{1,0:T(8,128)(2,1)S(1)}, u32[]{:S(2)}, u32[]{:S(2)}) collective-permute-start(bf16[64,1280]{1,0:T(8,128)(2,1)} %copy-done.23), channel_id=1, source_target_pairs={{0,2},{1,3},{2,0},{3,1},{4,6},{5,7},{6,4},{7,5},{8,10},{9,11},{10,... | collective-permute-start | bytes 491528 | tf_op jit(solution)/shard_map/ppermute | solution.py:489
  175.4 15.8 %collective-permute-start.11 = (bf16[64,1280]{1,0:T(8,128)(2,1)}, bf16[64,1280]{1,0:T(8,128)(2,1)S(1)}, u32[]{:S(2)}, u32[]{:S(2)}) collective-permute-start(bf16[64,1280]{1,0:T(8,128)(2,1)} %copy-done.14), channel_id=1, source_target_pairs={{0,3},{1,0},{2,1},{3,2},{4,7},{5,4},{6,5},{7,6},{8,11},{9,8},{10,9... | collective-permute-start | bytes 491528 | tf_op jit(solution)/shard_map/ppermute | solution.py:489
  179.0 12.5 %collective-permute-start.9 = (bf16[64,1280]{1,0:T(8,128)(2,1)}, bf16[64,1280]{1,0:T(8,128)(2,1)S(1)}, u32[]{:S(2)}, u32[]{:S(2)}) collective-permute-start(bf16[64,1280]{1,0:T(8,128)(2,1)} %copy-done.22), channel_id=1, source_target_pairs={{0,1},{1,2},{2,3},{3,0},{4,5},{5,6},{6,7},{7,4},{8,9},{9,10},{10,1... | collective-permute-start | bytes 491528 | tf_op jit(solution)/shard_map/ppermute | solution.py:489
  181.7 10.4 %collective-permute-start.15 = (bf16[64,256]{1,0:T(8,128)(2,1)S(1)}, bf16[64,256]{1,0:T(8,128)(2,1)S(1)}, u32[]{:S(2)}, u32[]{:S(2)}) collective-permute-start(bf16[64,256]{1,0:T(8,128)(2,1)S(1)} %get-tuple-element.44), channel_id=1, source_target_pairs={{0,1},{1,2},{2,3},{3,0},{4,5},{5,6},{6,7},{7,4},{8,9},{9,10},{10,1... | collective-permute-start | bytes 98312 | tf_op jit(solution)/shard_map/ppermute | solution.py:489
  185.4 7.9 %collective-permute-start.16 = (bf16[64,256]{1,0:T(8,128)(2,1)S(1)}, bf16[64,256]{1,0:T(8,128)(2,1)S(1)}, u32[]{:S(2)}, u32[]{:S(2)}) collective-permute-start(bf16[64,256]{1,0:T(8,128)(2,1)S(1)} %get-tuple-element.45), channel_id=1, source_target_pairs={{0,2},{1,3},{2,0},{3,1},{4,6},{5,7},{6,4},{7,5},{8,10},{9,11},{10,... | collective-permute-start | bytes 98312 | tf_op jit(solution)/shard_map/ppermute | solution.py:489
  188.5 4.8 %collective-permute-start.17 = (bf16[64,256]{1,0:T(8,128)(2,1)S(1)}, bf16[64,256]{1,0:T(8,128)(2,1)S(1)}, u32[]{:S(2)}, u32[]{:S(2)}) collective-permute-start(bf16[64,256]{1,0:T(8,128)(2,1)S(1)} %get-tuple-element.46), channel_id=1, source_target_pairs={{0,3},{1,0},{2,1},{3,2},{4,7},{5,4},{6,5},{7,6},{8,11},{9,8},{10,9... | collective-permute-start | bytes 98312 | tf_op jit(solution)/shard_map/ppermute | solution.py:489
  (5 other events, 3.6 us)

commit v5 on v4

--- a/solution.py
+++ b/solution.py
@@ -56,18 +56,16 @@
     for g in range(heads):
         now, ahead = ahead, []
         top = row_top(now)
-        totals = mixed = None
+        mixed = None
         for c in range(chunks):
             if g + 1 < heads:
                 ahead.append(score(g + 1, c))
             probs = jnp.exp(now[c] - top)
-            part = lane_halves(probs, jnp.add)
-            totals = part if totals is None else totals + part
             part = lax.dot_general(
                 probs.astype(jnp.bfloat16), value(g, c), NT, preferred_element_type=jnp.float32
             )
             mixed = part if mixed is None else mixed + part
-        outputs.append(mixed / jnp.sum(totals, axis=1, keepdims=True))
+        outputs.append(mixed[:, :HEAD] / mixed[:, HEAD : HEAD + 1])
     return outputs
 
 
@@ -149,8 +147,11 @@
         kc = jnp.concatenate([kc_ref[head_slice(g), chunk_of(c)], bias], axis=0)
         return jnp.dot(queries[g], kc, preferred_element_type=jnp.float32)
 
+    ones = jnp.where(top_row, 1.0, 0.0).astype(jnp.bfloat16)
+
     def value(g, c):
-        return values[g] if c == cached else vc_ref[head_slice(g), chunk_of(c)]
+        rows = values[g] if c == cached else vc_ref[head_slice(g), chunk_of(c)]
+        return jnp.concatenate([rows, ones], axis=0)
 
     outputs = attend_heads(heads, cached + 1, score, value)
     attended[pl.program_id(0)] = jnp.concatenate(outputs, axis=1).astype(jnp.bfloat16)

time: 195 us -> 195 us (level)
  no operation moved by 1% of the time
where the time goes in v5:
time: 195 us; the launch traced here: 194 us
  waiting for transfers between devices  73.7 us (38%)
  starting transfers between devices  54.2 us (28%)
  Pallas kernels  28.3 us (15%)
  matrix products  23.9 us (12%)
  local copies, waits for them, and re-layouts  9.55 us (5%)
  other arithmetic  3.14 us (2%)
    ppermute x6, waiting for transfers between devices, from_block(): return lax.ppermute(array, 'tp', [(i, (i - k) % tp) for i in range(tp)])  37 us
    ppermute x12, waiting for transfers between devices, to_block(): return lax.ppermute(array, 'tp', [(i, (i + k) % tp) for i in range(tp)])  29.7 us
    ppermute x12, starting transfers between devices, to_block(): return lax.ppermute(array, 'tp', [(i, (i + k) % tp) for i in range(tp)])  28.2 us
    pallas_call x1, Pallas kernels, per_device(): pl.pallas_call(functools.partial(attention_kernel, share), grid_spec=pltp...  19 us
    all_to_all x4, starting transfers between devices, exchanged(): lax.all_to_all(blocks, 'req', split_axis=0, concat_axis=0, tiled=True)  14.7 us
    ppermute x6, starting transfers between devices, from_block(): return lax.ppermute(array, 'tp', [(i, (i - k) % tp) for i in range(tp)])  11.3 us
    dot_general x1, matrix products, per_device(): jnp.dot(token_rows, expert_gate[0], preferred_element_type=jnp.float32)  7.66 us
    all_to_all x4, waiting for transfers between devices, exchanged(): lax.all_to_all(blocks, 'req', split_axis=0, concat_axis=0, tiled=True)  7.08 us
  transfers between devices with their start and end apart: 22, of which 12 were waited for; matrix products, arithmetic and copies ran while one was open for 6% of the time, Pallas kernels for 1%

profile of v5, /device:TPU:0, one launch (start us, length us, event | category | flops | bytes accessed | tf_op | source)
XLA Modules:
  0.0 193.9 jit_solution(8891683941142670575)
XLA Ops:
  0.7 0.8 multiply_sine_fusion
  1.5 19.0 %shard_map.127 = (bf16[64,2304]{1,0:T(8,128)(2,1)}, bf16[64,2304]{1,0:T(8,128)(2,1)}, bf16[64,2304]{1,0:T(8,128)(2,1)}, bf16[64,2304]{1,0:T(8,128)(2,1)}) custom-call(s32[1]{0:T(128)} %copy.38.lengths, s32[1]{0:T(128)} %bitcast.places.scalars, bf16[256,2304]{1,0:T(8,128)(2,1)} %refs_4_.1, f32[2304]{0:T(1024)} %gain_ref.1, bf16[3,576,2304]{2,1,0:T(8,128)(2,1)} %bitcast.70, ...), custom_call_target="tpu_custom_call" | custom-call | flops 4076863488 | bytes 15335424 | tf_op jit(solution)/shard_map/pallas_call | solution.py:548
  20.6 3.1 %collective-permute-start = (bf16[64,2304]{1,0:T(8,128)(2,1)}, bf16[64,2304]{1,0:T(8,128)(2,1)S(1)}, u32[]{:S(2)}, u32[]{:S(2)}) collective-permute-start(bf16[64,2304]{1,0:T(8,128)(2,1)} %get-tuple-element.27), channel_id=1, source_target_pairs={{0,1},{1,2},{2,3},{3,0},{4,5},{5,6},{6,7},{7,4},{8,9},{9,10},{10,1... | collective-permute-start | bytes 884744 | tf_op jit(solution)/shard_map/ppermute | solution.py:490
  23.6 2.6 %collective-permute-start.1 = (bf16[64,2304]{1,0:T(8,128)(2,1)}, bf16[64,2304]{1,0:T(8,128)(2,1)S(1)}, u32[]{:S(2)}, u32[]{:S(2)}) collective-permute-start(bf16[64,2304]{1,0:T(8,128)(2,1)} %get-tuple-element.28), channel_id=1, source_target_pairs={{0,2},{1,3},{2,0},{3,1},{4,6},{5,7},{6,4},{7,5},{8,10},{9,11},{10,... | collective-permute-start | bytes 884744 | tf_op jit(solution)/shard_map/ppermute | solution.py:490
  26.2 1.4 collective-permute-start.2
  28.5 2.0 %constant_dynamic-slice_fusion.2 = (bf16[1,1440,256]{2,1,0:T(8,128)(2,1)S(1)}, bf16[1,1440,256]{2,1,0:T(8,128)(2,1)S(1)}, bf16[1,1440,256]{2,1,0:T(8,128)(2,1)S(1)}, bf16[1,1440,256]{2,1,0:T(8,128)(2,1)S(1)}) fusion(bf16[1,1440,2304]{2,1,0:T(8,128)(2,1)} %param.25, s32[]{:T(128)S(6)} %select_n.58, s32[]{:T(128)S(6)} %select_n.60, s32[]{:T(128)S(6)} %select_n.64, ...), kind=kLoop, calls=%fused_computation.42 | loop fusion | bytes 5898256 | tf_op jit(solution)/shard_map/dynamic_slice | solution.py:601
  30.5 1.8 pad_maximum_fusion
  32.3 1.6 collective-permute-done.refs_1_
  33.9 11.8 %collective-permute-done.1.refs_2_ = bf16[64,2304]{1,0:T(8,128)(2,1)S(1)} collective-permute-done((bf16[64,2304]{1,0:T(8,128)(2,1)}, bf16[64,2304]{1,0:T(8,128)(2,1)S(1)}, u32[]{:S(2)}, u32[]{:S(2)}) %collective-permute-start.1) | collective-permute-done | bytes 294944 | tf_op jit(solution)/shard_map/ppermute | solution.py:490
  45.7 1.2 shard_map.128
  47.6 7.8 %collective-permute-start.3 = (bf16[64,1408]{1,0:T(8,128)(2,1)S(1)}, bf16[64,1408]{1,0:T(8,128)(2,1)S(1)}, u32[]{:S(2)}, u32[]{:S(2)}) collective-permute-start(bf16[64,1408]{1,0:T(8,128)(2,1)S(1)} %get-tuple-element.31), channel_id=1, source_target_pairs={{0,3},{1,0},{2,1},{3,2},{4,7},{5,4},{6,5},{7,6},{8,11},{9,8},{10,9... | collective-permute-start | bytes 540680 | tf_op jit(solution)/shard_map/ppermute | solution.py:493
  56.0 1.0 convolution_convert_fusion.1
  57.0 3.7 %all-to-all-start = ((bf16[8,96,256]{2,1,0:T(8,128)(2,1)}), bf16[8,96,256]{2,1,0:T(8,128)(2,1)S(1)}, u32[]{:S(2)}, u32[]{:S(2)}) async-start(bf16[8,96,256]{2,1,0:T(8,128)(2,1)} %bitcast.10), calls=%async_computation | async-start | bytes 786432 | tf_op jit(solution)/shard_map/all_to_all | solution.py:497
  60.9 10.9 %collective-permute-done.4.refs_2_ = bf16[64,1408]{1,0:T(8,128)(2,1)S(1)} collective-permute-done((bf16[64,1408]{1,0:T(8,128)(2,1)S(1)}, bf16[64,1408]{1,0:T(8,128)(2,1)S(1)}, u32[]{:S(2)}, u32[]{:S(2)}) %collective-permute-start.4) | collective-permute-done | bytes 180256 | tf_op jit(solution)/shard_map/ppermute | solution.py:493
  72.0 0.8 collective-permute-start.6
  73.4 1.4 collective-permute-start.8
  74.9 2.0 %convolution_convert_fusion = bf16[768,1280]{1,0:T(8,128)(2,1)} fusion(pred[768,256]{1,0:T(32,128)(4,1)S(1)} %bitcast_compare_fusion, bf16[256,1280]{1,0:T(8,128)(2,1)S(1)} %pad_maximum_fusion.1), kind=kOutput, calls=%fused_computation.8 | convolution fusion | flops 504299520 | bytes 2818048 | tf_op jit(solution)/shard_map/dot_general | solution.py:501
  76.9 3.8 %all-to-all-start.1 = ((bf16[8,96,1280]{2,1,0:T(8,128)(2,1)}), bf16[8,96,1280]{2,1,0:T(8,128)(2,1)S(1)}, u32[]{:S(2)}, u32[]{:S(2)}) async-start(bf16[8,96,1280]{2,1,0:T(8,128)(2,1)} %bitcast.71), calls=%async_computation.1 | async-start | bytes 3932160 | tf_op jit(solution)/shard_map/all_to_all | solution.py:497
  80.7 3.0 %collective-permute-done.6.__1_.refs_1_ = bf16[768,256]{1,0:T(8,128)(2,1)S(1)} collective-permute-done((bf16[768,256]{1,0:T(8,128)(2,1)S(1)}, bf16[768,256]{1,0:T(8,128)(2,1)S(1)}, u32[]{:S(2)}, u32[]{:S(2)}) %collective-permute-start.6) | collective-permute-done | bytes 393248 | tf_op jit(solution)/shard_map/ppermute | solution.py:493
  83.7 23.1 %collective-permute-done.7.__2_.refs_2_ = bf16[768,256]{1,0:T(8,128)(2,1)S(1)} collective-permute-done((bf16[768,256]{1,0:T(8,128)(2,1)S(1)}, bf16[768,256]{1,0:T(8,128)(2,1)S(1)}, u32[]{:S(2)}, u32[]{:S(2)}) %collective-permute-start.7) | collective-permute-done | bytes 393248 | tf_op jit(solution)/shard_map/ppermute | solution.py:493
  106.8 3.3 %shard_map.130 = bf16[768,2304]{1,0:T(8,128)(2,1)S(1)} custom-call(s32[1]{0:T(128)} %bitcast.places.scalars, bf16[768,1280]{1,0:T(8,128)(2,1)S(1)} %bitcast.62, bf16[768,256]{1,0:T(8,128)(2,1)S(1)} %shard_map.129.refs_0_, bf16[768,256]{1,0:T(8,128)(2,1)S(1)} %collective-permute-done.6.__1_.refs_1_, bf16[768,256]{1,0:T(8,128)(2,1)S(1)} %collective-permute-done.7.__2_.refs_2_, ...), custom_call_target="tpu_custom_call" | custom-call | flops 14155776 | bytes 7077888 | tf_op jit(solution)/shard_map/pallas_call | solution.py:300
  110.1 7.7 %fusion.2 = f32[768,1440]{0,1:T(8,128)S(1)} fusion(bf16[768,2304]{1,0:T(8,128)(2,1)S(1)} %shard_map.130, bf16[1,2304,1440]{1,2,0:T(8,128)(2,1)} %param.23), kind=kOutput, calls=%fused_computation.2 | convolution fusion | flops 5096079360 | bytes 14598144 | tf_op jit(solution)/shard_map/dot_general | solution.py:619
  117.8 5.9 %multiply_convert_fusion = bf16[768,1440]{0,1:T(8,128)(2,1)S(1)} fusion(f32[768,1440]{0,1:T(8,128)S(1)} %fusion.2, bf16[768,2304]{1,0:T(8,128)(2,1)S(1)} %shard_map.130, bf16[1,2304,1440]{1,2,0:T(8,128)(2,1)S(1)} %bitcast.78), kind=kOutput, calls=%fused_computation.4 | convolution fusion | flops 5102714880 | bytes 16809984 | tf_op jit(solution)/shard_map/dot_general | solution.py:620
  123.8 2.7 %fusion.15 = bf16[4,768,256]{2,1,0:T(8,128)(2,1)S(1)} fusion(bf16[4,1440,256]{2,1,0:T(8,128)(2,1)S(1)} %copy-done.24, bf16[768,1440]{0,1:T(8,128)(2,1)S(1)} %multiply_convert_fusion), kind=kOutput, calls=%fused_computation.14 | convolution fusion | flops 2265710592 | bytes 6733824 | tf_op jit(solution)/shard_map/rh,khs->krs/dot_general | solution.py:628
  126.5 1.0 slice_bitcast_fusion
  127.8 1.8 collective-permute-start.13
  129.6 2.9 %collective-permute-start.14 = (bf16[768,256]{1,0:T(8,128)(2,1)}, bf16[768,256]{1,0:T(8,128)(2,1)}, u32[]{:S(2)}, u32[]{:S(2)}) collective-permute-start(bf16[768,256]{1,0:T(8,128)(2,1)} %get-tuple-element.51), channel_id=1, source_target_pairs={{0,3},{1,0},{2,1},{3,2},{4,7},{5,4},{6,5},{7,6},{8,11},{9,8},{10,9... | collective-permute-start | bytes 1179656 | tf_op jit(solution)/shard_map/ppermute | solution.py:490
  132.5 4.5 %fusion.7 = bf16[768,1280]{1,0:T(8,128)(2,1)} fusion(bf16[768,1440]{0,1:T(8,128)(2,1)S(1)} %multiply_convert_fusion, bf16[1,1440,2304]{2,1,0:T(8,128)(2,1)S(1)} %bitcast.76), kind=kOutput, calls=%fused_computation.9 | convolution fusion | flops 2832138240 | bytes 7864320 | tf_op jit(solution)/shard_map/dot_general | solution.py:624
  137.0 3.7 %all-to-all-start.2 = ((bf16[8,96,1280]{2,1,0:T(8,128)(2,1)}), bf16[8,96,1280]{2,1,0:T(8,128)(2,1)S(1)}, u32[]{:S(2)}, u32[]{:S(2)}) async-start(bf16[8,96,1280]{2,1,0:T(8,128)(2,1)} %bitcast.74), calls=%async_computation.2 | async-start | bytes 3932160 | tf_op jit(solution)/shard_map/all_to_all | solution.py:497
  140.8 0.9 collective-permute-done.12.refs_1_
  141.7 0.8 copy-done.16
  142.4 13.2 %collective-permute-done.13.refs_2_ = bf16[768,256]{1,0:T(8,128)(2,1)S(1)} collective-permute-done((bf16[768,256]{1,0:T(8,128)(2,1)}, bf16[768,256]{1,0:T(8,128)(2,1)S(1)}, u32[]{:S(2)}, u32[]{:S(2)}) %collective-permute-start.13) | collective-permute-done | bytes 393248 | tf_op jit(solution)/shard_map/ppermute | solution.py:490
  155.6 0.8 copy-done.18
  156.4 1.0 copy-done.17
  157.4 1.0 copy-done.19
  158.4 2.0 %shard_map.133.__0_ = bf16[768,256]{1,0:T(8,128)(2,1)} custom-call(bf16[768,256]{1,0:T(8,128)(2,1)S(1)} %get-tuple-element.54.refs_0_, bf16[768,256]{1,0:T(8,128)(2,1)S(1)} %copy-done.17, bf16[768,256]{1,0:T(8,128)(2,1)S(1)} %copy-done.19, bf16[768,256]{1,0:T(8,128)(2,1)} %collective-permute-done.14.refs_3_), custom_call_target="tpu_custom_call" | custom-call | flops 137438953472 | bytes 1048576 | tf_op jit(solution)/shard_map/pallas_call | solution.py:399
  160.4 5.5 %all-to-all-done.2 = bf16[8,96,1280]{2,1,0:T(8,128)(2,1)S(1)} async-done(((bf16[8,96,1280]{2,1,0:T(8,128)(2,1)}), bf16[8,96,1280]{2,1,0:T(8,128)(2,1)S(1)}, u32[]{:S(2)}, u32[]{:S(2)}) %all-to-all-start.2) | async-done | bytes 1966112 | tf_op jit(solution)/shard_map/all_to_all | solution.py:497
  166.0 1.0 copy-done.21
  167.0 1.2 shard_map.131
  169.1 3.5 %all-to-all-start.3 = ((bf16[8,96,256]{2,1,0:T(8,128)(2,1)}), bf16[8,96,256]{2,1,0:T(8,128)(2,1)S(1)}, u32[]{:S(2)}, u32[]{:S(2)}) async-start(bf16[8,96,256]{2,1,0:T(8,128)(2,1)} %bitcast.25), calls=%async_computation.3 | async-start | bytes 786432 | tf_op jit(solution)/shard_map/all_to_all | solution.py:497
  172.5 2.6 %collective-permute-start.10 = (bf16[64,1280]{1,0:T(8,128)(2,1)}, bf16[64,1280]{1,0:T(8,128)(2,1)S(1)}, u32[]{:S(2)}, u32[]{:S(2)}) collective-permute-start(bf16[64,1280]{1,0:T(8,128)(2,1)} %copy-done.23), channel_id=1, source_target_pairs={{0,2},{1,3},{2,0},{3,1},{4,6},{5,7},{6,4},{7,5},{8,10},{9,11},{10,... | collective-permute-start | bytes 491528 | tf_op jit(solution)/shard_map/ppermute | solution.py:490
  175.2 3.6 %collective-permute-start.11 = (bf16[64,1280]{1,0:T(8,128)(2,1)}, bf16[64,1280]{1,0:T(8,128)(2,1)S(1)}, u32[]{:S(2)}, u32[]{:S(2)}) collective-permute-start(bf16[64,1280]{1,0:T(8,128)(2,1)} %copy-done.14), channel_id=1, source_target_pairs={{0,3},{1,0},{2,1},{3,2},{4,7},{5,4},{6,5},{7,6},{8,11},{9,8},{10,9... | collective-permute-start | bytes 491528 | tf_op jit(solution)/shard_map/ppermute | solution.py:490
  179.3 1.5 all-to-all-done.3
  181.4 3.8 %collective-permute-start.15 = (bf16[64,256]{1,0:T(8,128)(2,1)S(1)}, bf16[64,256]{1,0:T(8,128)(2,1)S(1)}, u32[]{:S(2)}, u32[]{:S(2)}) collective-permute-start(bf16[64,256]{1,0:T(8,128)(2,1)S(1)} %get-tuple-element.44), channel_id=1, source_target_pairs={{0,1},{1,2},{2,3},{3,0},{4,5},{5,6},{6,7},{7,4},{8,9},{9,10},{10,1... | collective-permute-start | bytes 98312 | tf_op jit(solution)/shard_map/ppermute | solution.py:490
  185.2 3.1 %collective-permute-start.16 = (bf16[64,256]{1,0:T(8,128)(2,1)S(1)}, bf16[64,256]{1,0:T(8,128)(2,1)S(1)}, u32[]{:S(2)}, u32[]{:S(2)}) collective-permute-start(bf16[64,256]{1,0:T(8,128)(2,1)S(1)} %get-tuple-element.45), channel_id=1, source_target_pairs={{0,2},{1,3},{2,0},{3,1},{4,6},{5,7},{6,4},{7,5},{8,10},{9,11},{10,... | collective-permute-start | bytes 98312 | tf_op jit(solution)/shard_map/ppermute | solution.py:490
  188.3 2.6 %collective-permute-start.17 = (bf16[64,256]{1,0:T(8,128)(2,1)S(1)}, bf16[64,256]{1,0:T(8,128)(2,1)S(1)}, u32[]{:S(2)}, u32[]{:S(2)}) collective-permute-start(bf16[64,256]{1,0:T(8,128)(2,1)S(1)} %get-tuple-element.46), channel_id=1, source_target_pairs={{0,3},{1,0},{2,1},{3,2},{4,7},{5,4},{6,5},{7,6},{8,11},{9,8},{10,9... | collective-permute-start | bytes 98312 | tf_op jit(solution)/shard_map/ppermute | solution.py:490
  191.9 1.2 collective-permute-done.16.refs_6_
  193.1 0.8 shard_map.136
  (100 shorter events, 6.4 us)
Async XLA Ops:
  1.5 26.1 %copy-start.26 = (s32[256,2]{0,1:T(2,128)S(1)}, s32[256,2]{0,1:T(2,128)}, u32[]{:S(2)}) copy-start(s32[256,2]{0,1:T(2,128)} %param.22) | copy-start | bytes 6148
  1.5 26.5 %copy-start.25 = (f32[2304]{0:T(1024)S(1)}, f32[2304]{0:T(1024)}, u32[]{:S(2)}) copy-start(f32[2304]{0:T(1024)} %param.20) | copy-start | bytes 27652
  20.6 13.3 %collective-permute-start = (bf16[64,2304]{1,0:T(8,128)(2,1)}, bf16[64,2304]{1,0:T(8,128)(2,1)S(1)}, u32[]{:S(2)}, u32[]{:S(2)}) collective-permute-start(bf16[64,2304]{1,0:T(8,128)(2,1)} %get-tuple-element.27), channel_id=1, source_target_pairs={{0,1},{1,2},{2,3},{3,0},{4,5},{5,6},{6,7},{7,4},{8,9},{9,10},{10,1... | collective-permute-start | bytes 884744 | tf_op jit(solution)/shard_map/ppermute | solution.py:490
  23.6 22.0 %collective-permute-start.1 = (bf16[64,2304]{1,0:T(8,128)(2,1)}, bf16[64,2304]{1,0:T(8,128)(2,1)S(1)}, u32[]{:S(2)}, u32[]{:S(2)}) collective-permute-start(bf16[64,2304]{1,0:T(8,128)(2,1)} %get-tuple-element.28), channel_id=1, source_target_pairs={{0,2},{1,3},{2,0},{3,1},{4,6},{5,7},{6,4},{7,5},{8,10},{9,11},{10,... | collective-permute-start | bytes 884744 | tf_op jit(solution)/shard_map/ppermute | solution.py:490
  26.2 19.4 %collective-permute-start.2 = (bf16[64,2304]{1,0:T(8,128)(2,1)}, bf16[64,2304]{1,0:T(8,128)(2,1)S(1)}, u32[]{:S(2)}, u32[]{:S(2)}) collective-permute-start(bf16[64,2304]{1,0:T(8,128)(2,1)} %get-tuple-element.29), channel_id=1, source_target_pairs={{0,3},{1,0},{2,1},{3,2},{4,7},{5,4},{6,5},{7,6},{8,11},{9,8},{10,9... | collective-permute-start | bytes 884744 | tf_op jit(solution)/shard_map/ppermute | solution.py:490
  28.3 46.6 %copy-start.1 = (s32[256,2]{1,0:T(8,128)}, s32[256,2]{1,0:T(8,128)S(1)}, u32[]{:S(2)}) copy-start(s32[256,2]{1,0:T(8,128)S(1)} %copy.31.routes_ref) | copy-start | bytes 6148
  30.5 15.2 %copy-start = (bf16[256,2304]{1,0:T(8,128)(2,1)S(1)}, bf16[256,2304]{1,0:T(8,128)(2,1)}, u32[]{:S(2)}) copy-start(bf16[256,2304]{1,0:T(8,128)(2,1)} %refs_4_.1) | copy-start | bytes 3538948
  30.5 15.1 %copy-start.11 = (bf16[64,2304]{1,0:T(8,128)(2,1)S(1)}, bf16[64,2304]{1,0:T(8,128)(2,1)}, u32[]{:S(2)}) copy-start(bf16[64,2304]{1,0:T(8,128)(2,1)} %get-tuple-element.26.refs_0_) | copy-start | bytes 884740
  30.5 15.1 %copy-start.15 = (bf16[2304,8]{0,1:T(8,128)(2,1)S(1)}, bf16[2304,8]{0,1:T(8,128)(2,1)}, u32[]{:S(2)}) copy-start(bf16[2304,8]{0,1:T(8,128)(2,1)} %param.21) | copy-start | bytes 110596
  47.6 9.4 %copy-start.20 = (f32[64,1280]{1,0:T(8,128)}, f32[64,1280]{1,0:T(8,128)S(1)}, u32[]{:S(2)}) copy-start(f32[64,1280]{1,0:T(8,128)S(1)} %get-tuple-element.37.base_ref) | copy-start | bytes 983044
  47.6 29.3 %copy-start.3 = (bf16[64,1408]{1,0:T(8,128)(2,1)}, bf16[64,1408]{1,0:T(8,128)(2,1)S(1)}, u32[]{:S(2)}) copy-start(bf16[64,1408]{1,0:T(8,128)(2,1)S(1)} %get-tuple-element.30.refs_0_) | copy-start | bytes 540676
  47.6 13.3 %collective-permute-start.3 = (bf16[64,1408]{1,0:T(8,128)(2,1)S(1)}, bf16[64,1408]{1,0:T(8,128)(2,1)S(1)}, u32[]{:S(2)}, u32[]{:S(2)}) collective-permute-start(bf16[64,1408]{1,0:T(8,128)(2,1)S(1)} %get-tuple-element.31), channel_id=1, source_target_pairs={{0,3},{1,0},{2,1},{3,2},{4,7},{5,4},{6,5},{7,6},{8,11},{9,8},{10,9... | collective-permute-start | bytes 540680 | tf_op jit(solution)/shard_map/ppermute | solution.py:493
  55.4 16.5 %collective-permute-start.4 = (bf16[64,1408]{1,0:T(8,128)(2,1)S(1)}, bf16[64,1408]{1,0:T(8,128)(2,1)S(1)}, u32[]{:S(2)}, u32[]{:S(2)}) collective-permute-start(bf16[64,1408]{1,0:T(8,128)(2,1)S(1)} %get-tuple-element.32), channel_id=1, source_target_pairs={{0,2},{1,3},{2,0},{3,1},{4,6},{5,7},{6,4},{7,5},{8,10},{9,11},{10,... | collective-permute-start | bytes 540680 | tf_op jit(solution)/shard_map/ppermute | solution.py:493
  55.8 16.1 %collective-permute-start.5 = (bf16[64,1408]{1,0:T(8,128)(2,1)S(1)}, bf16[64,1408]{1,0:T(8,128)(2,1)S(1)}, u32[]{:S(2)}, u32[]{:S(2)}) collective-permute-start(bf16[64,1408]{1,0:T(8,128)(2,1)S(1)} %get-tuple-element.33), channel_id=1, source_target_pairs={{0,1},{1,2},{2,3},{3,0},{4,5},{5,6},{6,7},{7,4},{8,9},{9,10},{10,1... | collective-permute-start | bytes 540680 | tf_op jit(solution)/shard_map/ppermute | solution.py:493
  57.0 15.0 %all-to-all-start = ((bf16[8,96,256]{2,1,0:T(8,128)(2,1)}), bf16[8,96,256]{2,1,0:T(8,128)(2,1)S(1)}, u32[]{:S(2)}, u32[]{:S(2)}) async-start(bf16[8,96,256]{2,1,0:T(8,128)(2,1)} %bitcast.10), calls=%async_computation | async-start | bytes 786432 | tf_op jit(solution)/shard_map/all_to_all | solution.py:497
  60.9 16.0 %copy-start.5 = (bf16[64,1408]{1,0:T(8,128)(2,1)}, bf16[64,1408]{1,0:T(8,128)(2,1)S(1)}, u32[]{:S(2)}) copy-start(bf16[64,1408]{1,0:T(8,128)(2,1)S(1)} %collective-permute-done.3.refs_1_) | copy-start | bytes 540676
  71.9 5.0 %copy-start.7 = (bf16[64,1408]{1,0:T(8,128)(2,1)}, bf16[64,1408]{1,0:T(8,128)(2,1)S(1)}, u32[]{:S(2)}) copy-start(bf16[64,1408]{1,0:T(8,128)(2,1)S(1)} %collective-permute-done.4.refs_2_) | copy-start | bytes 540676
  71.9 5.0 %copy-start.9 = (bf16[64,1408]{1,0:T(8,128)(2,1)}, bf16[64,1408]{1,0:T(8,128)(2,1)S(1)}, u32[]{:S(2)}) copy-start(bf16[64,1408]{1,0:T(8,128)(2,1)S(1)} %collective-permute-done.5.refs_3_) | copy-start | bytes 540676
  72.0 11.7 %collective-permute-start.6 = (bf16[768,256]{1,0:T(8,128)(2,1)S(1)}, bf16[768,256]{1,0:T(8,128)(2,1)S(1)}, u32[]{:S(2)}, u32[]{:S(2)}) collective-permute-start(bf16[768,256]{1,0:T(8,128)(2,1)S(1)} %bitcast.64), channel_id=1, source_target_pairs={{0,3},{1,0},{2,1},{3,2},{4,7},{5,4},{6,5},{7,6},{8,11},{9,8},{10,9... | collective-permute-start | bytes 1179656 | tf_op jit(solution)/shard_map/ppermute | solution.py:493
  72.8 34.0 %collective-permute-start.7 = (bf16[768,256]{1,0:T(8,128)(2,1)S(1)}, bf16[768,256]{1,0:T(8,128)(2,1)S(1)}, u32[]{:S(2)}, u32[]{:S(2)}) collective-permute-start(bf16[768,256]{1,0:T(8,128)(2,1)S(1)} %bitcast.65), channel_id=1, source_target_pairs={{0,2},{1,3},{2,0},{3,1},{4,6},{5,7},{6,4},{7,5},{8,10},{9,11},{10,... | collective-permute-start | bytes 1179656 | tf_op jit(solution)/shard_map/ppermute | solution.py:493
  73.4 33.3 %collective-permute-start.8 = (bf16[768,256]{1,0:T(8,128)(2,1)S(1)}, bf16[768,256]{1,0:T(8,128)(2,1)}, u32[]{:S(2)}, u32[]{:S(2)}) collective-permute-start(bf16[768,256]{1,0:T(8,128)(2,1)S(1)} %bitcast.66), channel_id=1, source_target_pairs={{0,1},{1,2},{2,3},{3,0},{4,5},{5,6},{6,7},{7,4},{8,9},{9,10},{10,1... | collective-permute-start | bytes 1179656 | tf_op jit(solution)/shard_map/ppermute | solution.py:493
  76.9 29.8 %all-to-all-start.1 = ((bf16[8,96,1280]{2,1,0:T(8,128)(2,1)}), bf16[8,96,1280]{2,1,0:T(8,128)(2,1)S(1)}, u32[]{:S(2)}, u32[]{:S(2)}) async-start(bf16[8,96,1280]{2,1,0:T(8,128)(2,1)} %bitcast.71), calls=%async_computation.1 | async-start | bytes 3932160 | tf_op jit(solution)/shard_map/all_to_all | solution.py:497
  106.7 11.0 %slice-start.2 = ((s8[6635520]{0:T(1024)(128)(4,1)}), s8[4194304]{0:T(1024)(128)(4,1)S(1)}, s32[]{:S(2)}) async-start(s8[6635520]{0:T(1024)(128)(4,1)} %bitcast.77), calls=%async_computation.6 | async-start | bytes 8388608
  110.1 7.7 %slice-start.3 = ((s8[6635520]{0:T(1024)(128)(4,1)}), s8[2441216]{0:T(1024)(128)(4,1)S(1)}, s32[]{:S(2)}) async-start(s8[6635520]{0:T(1024)(128)(4,1)} %bitcast.77), calls=%async_computation.7 | async-start | bytes 4882432
  110.1 22.4 %slice-start = ((s8[6635520]{0:T(1024)(128)(4,1)}), s8[4194304]{0:T(1024)(128)(4,1)S(1)}, s32[]{:S(2)}) async-start(s8[6635520]{0:T(1024)(128)(4,1)} %bitcast.75), calls=%async_computation.4 | async-start | bytes 8388608
  117.8 5.9 %copy-start.24 = (bf16[4,1440,256]{2,1,0:T(8,128)(2,1)S(1)}, bf16[4,1440,256]{2,1,0:T(8,128)(2,1)}, u32[]{:S(2)}) copy-start(bf16[4,1440,256]{2,1,0:T(8,128)(2,1)} %pad_maximum_fusion) | copy-start | bytes 8847364
  117.8 14.7 %slice-start.1 = ((s8[6635520]{0:T(1024)(128)(4,1)}), s8[2441216]{0:T(1024)(128)(4,1)S(1)}, s32[]{:S(2)}) async-start(s8[6635520]{0:T(1024)(128)(4,1)} %bitcast.75), calls=%async_computation.5 | async-start | bytes 4882432
  127.5 14.2 %collective-permute-start.12 = (bf16[768,256]{1,0:T(8,128)(2,1)}, bf16[768,256]{1,0:T(8,128)(2,1)S(1)}, u32[]{:S(2)}, u32[]{:S(2)}) collective-permute-start(bf16[768,256]{1,0:T(8,128)(2,1)} %get-tuple-element.53), channel_id=1, source_target_pairs={{0,1},{1,2},{2,3},{3,0},{4,5},{5,6},{6,7},{7,4},{8,9},{9,10},{10,1... | collective-permute-start | bytes 1179656 | tf_op jit(solution)/shard_map/ppermute | solution.py:490
  127.8 27.8 %collective-permute-start.13 = (bf16[768,256]{1,0:T(8,128)(2,1)}, bf16[768,256]{1,0:T(8,128)(2,1)S(1)}, u32[]{:S(2)}, u32[]{:S(2)}) collective-permute-start(bf16[768,256]{1,0:T(8,128)(2,1)} %get-tuple-element.52), channel_id=1, source_target_pairs={{0,2},{1,3},{2,0},{3,1},{4,6},{5,7},{6,4},{7,5},{8,10},{9,11},{10,... | collective-permute-start | bytes 1179656 | tf_op jit(solution)/shard_map/ppermute | solution.py:490
  129.6 26.8 %collective-permute-start.14 = (bf16[768,256]{1,0:T(8,128)(2,1)}, bf16[768,256]{1,0:T(8,128)(2,1)}, u32[]{:S(2)}, u32[]{:S(2)}) collective-permute-start(bf16[768,256]{1,0:T(8,128)(2,1)} %get-tuple-element.51), channel_id=1, source_target_pairs={{0,3},{1,0},{2,1},{3,2},{4,7},{5,4},{6,5},{7,6},{8,11},{9,8},{10,9... | collective-permute-start | bytes 1179656 | tf_op jit(solution)/shard_map/ppermute | solution.py:490
  137.0 29.0 %all-to-all-start.2 = ((bf16[8,96,1280]{2,1,0:T(8,128)(2,1)}), bf16[8,96,1280]{2,1,0:T(8,128)(2,1)S(1)}, u32[]{:S(2)}, u32[]{:S(2)}) async-start(bf16[8,96,1280]{2,1,0:T(8,128)(2,1)} %bitcast.74), calls=%async_computation.2 | async-start | bytes 3932160 | tf_op jit(solution)/shard_map/all_to_all | solution.py:497
  156.4 1.0 copy-start.17
  157.4 1.0 copy-start.19
  158.4 7.6 %copy-start.2 = (s32[256,2]{1,0:T(8,128)S(1)}, s32[256,2]{1,0:T(8,128)}, u32[]{:S(2)}) copy-start(s32[256,2]{1,0:T(8,128)} %copy-done.1) | copy-start | bytes 6148
  158.4 7.6 %copy-start.4 = (bf16[64,1408]{1,0:T(8,128)(2,1)S(1)}, bf16[64,1408]{1,0:T(8,128)(2,1)}, u32[]{:S(2)}) copy-start(bf16[64,1408]{1,0:T(8,128)(2,1)} %copy-done.3) | copy-start | bytes 540676
  158.4 7.6 %copy-start.6 = (bf16[64,1408]{1,0:T(8,128)(2,1)S(1)}, bf16[64,1408]{1,0:T(8,128)(2,1)}, u32[]{:S(2)}) copy-start(bf16[64,1408]{1,0:T(8,128)(2,1)} %copy-done.5) | copy-start | bytes 540676
  158.4 7.6 %copy-start.8 = (bf16[64,1408]{1,0:T(8,128)(2,1)S(1)}, bf16[64,1408]{1,0:T(8,128)(2,1)}, u32[]{:S(2)}) copy-start(bf16[64,1408]{1,0:T(8,128)(2,1)} %copy-done.7) | copy-start | bytes 540676
  158.4 7.6 %copy-start.10 = (bf16[64,1408]{1,0:T(8,128)(2,1)S(1)}, bf16[64,1408]{1,0:T(8,128)(2,1)}, u32[]{:S(2)}) copy-start(bf16[64,1408]{1,0:T(8,128)(2,1)} %copy-done.9) | copy-start | bytes 540676
  160.4 20.4 %copy-start.13 = (f32[256,256]{1,0:T(8,128)S(1)}, f32[256,256]{1,0:T(8,128)}, u32[]{:S(2)}) copy-start(f32[256,256]{1,0:T(8,128)} %copy-done.12) | copy-start | bytes 786436
  166.0 1.0 copy-start.21
  168.3 0.8 copy-start.23
  169.1 11.7 %all-to-all-start.3 = ((bf16[8,96,256]{2,1,0:T(8,128)(2,1)}), bf16[8,96,256]{2,1,0:T(8,128)(2,1)S(1)}, u32[]{:S(2)}, u32[]{:S(2)}) async-start(bf16[8,96,256]{2,1,0:T(8,128)(2,1)} %bitcast.25), calls=%async_computation.3 | async-start | bytes 786432 | tf_op jit(solution)/shard_map/all_to_all | solution.py:497
  172.5 15.8 %collective-permute-start.10 = (bf16[64,1280]{1,0:T(8,128)(2,1)}, bf16[64,1280]{1,0:T(8,128)(2,1)S(1)}, u32[]{:S(2)}, u32[]{:S(2)}) collective-permute-start(bf16[64,1280]{1,0:T(8,128)(2,1)} %copy-done.23), channel_id=1, source_target_pairs={{0,2},{1,3},{2,0},{3,1},{4,6},{5,7},{6,4},{7,5},{8,10},{9,11},{10,... | collective-permute-start | bytes 491528 | tf_op jit(solution)/shard_map/ppermute | solution.py:490
  175.2 15.8 %collective-permute-start.11 = (bf16[64,1280]{1,0:T(8,128)(2,1)}, bf16[64,1280]{1,0:T(8,128)(2,1)S(1)}, u32[]{:S(2)}, u32[]{:S(2)}) collective-permute-start(bf16[64,1280]{1,0:T(8,128)(2,1)} %copy-done.14), channel_id=1, source_target_pairs={{0,3},{1,0},{2,1},{3,2},{4,7},{5,4},{6,5},{7,6},{8,11},{9,8},{10,9... | collective-permute-start | bytes 491528 | tf_op jit(solution)/shard_map/ppermute | solution.py:490
  178.8 12.5 %collective-permute-start.9 = (bf16[64,1280]{1,0:T(8,128)(2,1)}, bf16[64,1280]{1,0:T(8,128)(2,1)S(1)}, u32[]{:S(2)}, u32[]{:S(2)}) collective-permute-start(bf16[64,1280]{1,0:T(8,128)(2,1)} %copy-done.22), channel_id=1, source_target_pairs={{0,1},{1,2},{2,3},{3,0},{4,5},{5,6},{6,7},{7,4},{8,9},{9,10},{10,1... | collective-permute-start | bytes 491528 | tf_op jit(solution)/shard_map/ppermute | solution.py:490
  181.4 10.4 %collective-permute-start.15 = (bf16[64,256]{1,0:T(8,128)(2,1)S(1)}, bf16[64,256]{1,0:T(8,128)(2,1)S(1)}, u32[]{:S(2)}, u32[]{:S(2)}) collective-permute-start(bf16[64,256]{1,0:T(8,128)(2,1)S(1)} %get-tuple-element.44), channel_id=1, source_target_pairs={{0,1},{1,2},{2,3},{3,0},{4,5},{5,6},{6,7},{7,4},{8,9},{9,10},{10,1... | collective-permute-start | bytes 98312 | tf_op jit(solution)/shard_map/ppermute | solution.py:490
  185.2 7.9 %collective-permute-start.16 = (bf16[64,256]{1,0:T(8,128)(2,1)S(1)}, bf16[64,256]{1,0:T(8,128)(2,1)S(1)}, u32[]{:S(2)}, u32[]{:S(2)}) collective-permute-start(bf16[64,256]{1,0:T(8,128)(2,1)S(1)} %get-tuple-element.45), channel_id=1, source_target_pairs={{0,2},{1,3},{2,0},{3,1},{4,6},{5,7},{6,4},{7,5},{8,10},{9,11},{10,... | collective-permute-start | bytes 98312 | tf_op jit(solution)/shard_map/ppermute | solution.py:490
  188.3 4.8 %collective-permute-start.17 = (bf16[64,256]{1,0:T(8,128)(2,1)S(1)}, bf16[64,256]{1,0:T(8,128)(2,1)S(1)}, u32[]{:S(2)}, u32[]{:S(2)}) collective-permute-start(bf16[64,256]{1,0:T(8,128)(2,1)S(1)} %get-tuple-element.46), channel_id=1, source_target_pairs={{0,3},{1,0},{2,1},{3,2},{4,7},{5,4},{6,5},{7,6},{8,11},{9,8},{10,9... | collective-permute-start | bytes 98312 | tf_op jit(solution)/shard_map/ppermute | solution.py:490
  (5 other events, 3.6 us)
